TPU v7x, 32 devices: a whole 2x2x4 slice. The times are simulated.
32 devices in a mesh: dp: 8 (over y, x, core), tensor: 4 (over z).
Axes of the slice: x: 2, y: 2, z: 4, core: 2. Of those that a mesh axis runs over, the one named last changes fastest.
Arguments:
- tokens: bfloat16 [2, 2048, 1024], P(None, 'dp', 'tensor'), may hold values from -6 to 6
- lengths: int32 [2, 8], P(None, 'dp'), may hold values from 16 to 256, as said below
- norm_gain: float32 [1024], replicated, may hold values from 0.5 to 1.5
- in_weight: bfloat16 [1024, 2, 2048], P('dp', None, 'tensor'), may hold values from -0.1875 to 0.1875
- x_weight: bfloat16 [2048, 96], P('tensor'), may hold values from -0.125 to 0.125
- dt_weight: bfloat16 [64, 2048], P(None, 'tensor'), may hold values from -0.75 to 0.75
- dt_bias: float32 [2048], P('tensor'), may hold values from -6 to -2
- conv_weight: float32 [4, 2048], P(None, 'tensor'), may hold values from -3 to 3
- conv_bias: float32 [2048], P('tensor'), may hold values from -3 to 3
- a_log: float32 [16, 2048], P(None, 'tensor'), may hold values from 0 to 2.77
- skip: float32 [2048], P('tensor'), may hold values from 0.5 to 1.5
- out_weight: bfloat16 [2048, 1024], P('tensor', 'dp'), may hold values from -0.125 to 0.125
- cotangent: bfloat16 [2, 2048, 1024], P(None, 'dp', 'tensor'), may hold values from -6 to 6
Outputs:
- mixed: bfloat16 [2, 2048, 1024], P(None, 'dp', 'tensor')
- input_grad: float32 [2, 2048, 1024], P(None, 'dp', 'tensor')
- grad_norm_gain: float32 [1024], replicated
- grad_in_weight: float32 [1024, 2, 2048], P('dp', None, 'tensor')
- grad_x_weight: float32 [2048, 96], P('tensor')
- grad_dt_weight: float32 [64, 2048], P(None, 'tensor')
- grad_dt_bias: float32 [2048], P('tensor')
- grad_conv_weight: float32 [4, 2048], P(None, 'tensor')
- grad_conv_bias: float32 [2048], P('tensor')
- grad_a_log: float32 [16, 2048], P(None, 'tensor')
- grad_skip: float32 [2048], P('tensor')
- grad_out_weight: float32 [2048, 1024], P('tensor', 'dp')
Inputs may be any that keep to these rules, and one draw needn't show every extreme that they name: lengths[m, c] is the number of valid tokens at the head of context c of micro-batch m; the rest is padding. Some context is full and some has exactly 16 valid tokens.
All inputs are finite; a program needn't handle non-finite values.
Results may differ from a plain program's by a relative error of at most 0.011.
Values may be sent and summed in bfloat16 or wider, within the bound.
No kernel may reach another device: no remote copies, remote signals or barrier semaphores. Data moves between devices by JAX's collectives and lax.ppermute only.
A program may use at most 192 MiB of HBM per device.

v0:
```python
import math
from functools import partial

import jax
import jax.numpy as jnp
from jax import lax
from jax.experimental import pallas as pl
from jax.experimental.pallas import tpu as pltpu
from jax.sharding import PartitionSpec as P

EPS = 1e-05
LOG2E = math.log2(math.e)
F32 = jnp.float32
BF16 = jnp.bfloat16
GROUP = 8
LANES = 128


def contract(left, right, left_dim, right_dim):
    return lax.dot_general(
        left, right, (((left_dim,), (right_dim,)), ((), ())), preferred_element_type=F32
    )


def sigmoid(v):
    return 1.0 / (1.0 + jnp.exp(-v))


def softplus(v):
    return jnp.maximum(v, 0.0) + jnp.log1p(jnp.exp(-jnp.abs(v)))


def swap(value, axis, mask):
    count = lax.axis_size(axis)
    return lax.ppermute(value, axis, [(i, i ^ mask) for i in range(count)])


def pre_kernel(parts, blocks, ids, *refs):
    xs, refs = refs[:parts], refs[parts:]
    ws, refs = refs[:blocks], refs[blocks:]
    gain, conv_w, conv_b, xw_t = refs[:4]
    normed, w_full, inner, summed, u_act, gate, inv, proj, proj_low, padded = refs[4:]
    quarter = xs[0].shape[2]
    chans = inner.shape[2]

    @pl.when(pl.program_id(0) == 0)
    def _():
        gather_rows(ids, ws, w_full)
        padded[:GROUP, :] = jnp.zeros((GROUP, chans), F32)

    square = 0.0
    for x in xs:
        rows = x[0].astype(F32)
        square = square + jnp.sum(rows * rows, axis=1, keepdims=True)
    scale = lax.rsqrt(square / (parts * quarter) + EPS)
    inv[0] = jnp.broadcast_to(scale, inv.shape[1:])
    for k, x in enumerate(xs):
        cols = pl.ds(pl.multiple_of((ids[0] ^ k) * quarter, LANES), quarter)
        normed[0, :, cols] = (x[0].astype(F32) * scale * gain[:, cols]).astype(BF16)
    both = jnp.dot(normed[0], w_full[...], preferred_element_type=F32)
    gate[0] = both[:, chans:]
    inner_in = both[:, :chans]
    inner[0] = inner_in
    tokens = inner_in.shape[0]
    padded[GROUP:, :] = inner_in
    taps = conv_w.shape[0]
    total = jnp.broadcast_to(conv_b[...], inner_in.shape)
    for j in range(taps):
        total = total + conv_w[j : j + 1, :] * padded[pl.ds(GROUP - taps + 1 + j, tokens), :]
    summed[0] = total
    act = total * sigmoid(total)
    u_act[0] = act
    partial_sum = contract(xw_t[...], act.astype(BF16), 1, 1)
    proj[0] = partial_sum
    proj_low[0] = partial_sum.astype(BF16)


def gather_rows(ids, blocks, full):
    if len(blocks) == 1:
        full[...] = blocks[0][...]
        return
    chips = len(blocks) // 2
    for side in range(2):
        for j in range(chips):
            block = blocks[side * chips + j]
            index = (ids[1] ^ (2 * j)) ^ side
            rows = block.shape[0]
            full[pl.ds(pl.multiple_of(index * rows, 16), rows), :] = block[...]


def gather_cols(ids, blocks, full):
    if len(blocks) == 1:
        full[...] = blocks[0][...]
        return
    chips = len(blocks) // 2
    for side in range(2):
        for j in range(chips):
            block = blocks[side * chips + j]
            index = (ids[1] ^ (2 * j)) ^ side
            cols = block.shape[1]
            full[:, pl.ds(pl.multiple_of(index * cols, LANES), cols)] = block[...]


def fold(pend, out, start):
    for g in range(pend.shape[0]):
        total = pend[g, pl.ds(0, GROUP, stride=GROUP), :]
        for s in range(1, GROUP):
            total = total + pend[g, pl.ds(s, GROUP, stride=GROUP), :]
        out[pl.ds(start, GROUP), g * LANES : (g + 1) * LANES] = total


def fwd_kernel(parts, blocks, ids, lens, *refs):
    projs, refs = refs[:parts], refs[parts:]
    ws, refs = refs[:blocks], refs[blocks:]
    u_act, gate, dt_w, dt_b, a_log, skip = refs[:6]
    refs = refs[6:]
    dt_lin, y_rows, gated, states, w_full, own = refs[:6]
    sends, refs = refs[6 : 5 + parts], refs[5 + parts :]
    dt, dtu, y, pend, carry = refs
    span, chans = dt.shape
    nstate = a_log.shape[0]
    rank = dt_w.shape[0]
    block = pl.program_id(1)
    groups = chans // LANES

    @pl.when((pl.program_id(0) == 0) & (block == 0))
    def _():
        gather_cols(ids, ws, w_full)

    @pl.when(block == 0)
    def _():
        carry[...] = jnp.zeros(carry.shape, F32)

    proj = projs[0][0]
    for other in projs[1:]:
        proj = proj + other[0].astype(F32)
    lin = contract(proj[:rank].astype(BF16), dt_w[...], 0, 0) + dt_b[...]
    dt_lin[0] = lin
    step = softplus(lin)
    dt[...] = step
    dtu[...] = step * u_act[0]
    b_in = proj[rank : rank + nstate]
    c_in = proj[rank + nstate :]
    rate = -LOG2E * jnp.exp(a_log[...])
    lane = [slice(g * LANES, (g + 1) * LANES) for g in range(groups)]

    def steps(i, state):
        state = list(state)
        start = pl.multiple_of(i * GROUP, GROUP)
        shift = lax.rem(span - start, span)
        b_roll = pltpu.roll(b_in, shift, 1)
        c_roll = pltpu.roll(c_in, shift, 1)
        dt_rows = dt[pl.ds(start, GROUP), :]
        dtu_rows = dtu[pl.ds(start, GROUP), :]
        for k in range(GROUP):
            b_t = jnp.broadcast_to(b_roll[:, k : k + 1], (nstate, LANES))
            c_t = jnp.broadcast_to(c_roll[:, k : k + 1], (nstate, LANES))
            for g in range(groups):
                dt_t = dt_rows[k : k + 1, lane[g]]
                dtu_t = dtu_rows[k : k + 1, lane[g]]
                new = jnp.exp2(dt_t * rate[:, lane[g]]) * state[g] + dtu_t * b_t
                state[g] = new
                states[0, pl.ds(pl.multiple_of((start + k) * nstate, nstate), nstate), lane[g]] = new
                term = c_t * new
                pend[g, k * GROUP : (k + 1) * GROUP, :] = sum(
                    term[s : s + GROUP] for s in range(0, nstate, GROUP)
                )
        fold(pend, y, start)
        return tuple(state)

    last = lax.fori_loop(0, span // GROUP, steps, tuple(carry[:, l] for l in lane))
    for g in range(groups):
        carry[:, lane[g]] = last[g]
    rows = y[...] + skip[...] * u_act[0]
    y_rows[0] = rows
    gate_in = gate[0]
    position = block * span + lax.broadcasted_iota(jnp.int32, (span, 1), 0)
    live = (position < lens[pl.program_id(0)]).astype(F32)
    low = (rows * (gate_in * sigmoid(gate_in)) * live).astype(BF16)
    gated[0] = low
    quarter = own.shape[2]
    for k in range(parts):
        cols = pl.ds(pl.multiple_of((ids[0] ^ k) * quarter, LANES), quarter)
        term = jnp.dot(low, w_full[:, cols], preferred_element_type=F32)
        if k == 0:
            own[0] = term
        else:
            sends[k - 1][0] = term.astype(BF16)


def bwd_kernel(parts, ids, lens, *refs):
    projs, refs = refs[:parts], refs[parts:]
    cots, refs = refs[:parts], refs[parts:]
    w_full, u_act, gate, dt_lin, y_rows, states, dt_w, a_log, skip = refs[:9]
    refs = refs[9:]
    cot_full, d_proj, d_proj_low, d_scan, d_gate, small = refs[:6]
    dt, dtu, d_y, d_dtu, d_dta, pend_q, pend_r, carry, g_rate = refs[6:]
    span, chans = dt.shape
    nstate = a_log.shape[0]
    rank = dt_w.shape[0]
    first = (pl.program_id(0) == 0) & (pl.program_id(1) == 0)
    last = (pl.program_id(0) == pl.num_programs(0) - 1) & (pl.program_id(1) == pl.num_programs(1) - 1)
    block = pl.num_programs(1) - 1 - pl.program_id(1)
    groups = chans // LANES
    quarter = cots[0].shape[2]
    lane = [slice(g * LANES, (g + 1) * LANES) for g in range(groups)]

    @pl.when(first)
    def _():
        small[...] = jnp.zeros(small.shape, F32)
        g_rate[...] = jnp.zeros(g_rate.shape, F32)

    @pl.when(pl.program_id(1) == 0)
    def _():
        carry[...] = jnp.zeros(carry.shape, F32)

    for k, cot in enumerate(cots):
        cols = pl.ds(pl.multiple_of((ids[0] ^ k) * quarter, LANES), quarter)
        cot_full[0, :, cols] = cot[0]
    d_gated = contract(cot_full[0], w_full[...], 1, 1)

    proj = projs[0][0]
    for other in projs[1:]:
        proj = proj + other[0].astype(F32)
    dt_low = proj[:rank].astype(BF16)
    b_in = proj[rank : rank + nstate]
    c_in = proj[rank + nstate :]
    lin = dt_lin[0]
    u = u_act[0]
    step = softplus(lin)
    dt[...] = step
    dtu[...] = step * u
    gate_in = gate[0]
    gate_sig = sigmoid(gate_in)
    position = block * span + lax.broadcasted_iota(jnp.int32, (span, 1), 0)
    live = (position < lens[pl.program_id(0)]).astype(F32)
    d_live = d_gated * live
    d_rows = d_live * (gate_in * gate_sig)
    d_y[...] = d_rows
    d_gate[0] = (d_live * y_rows[0] * (gate_sig * (1.0 + gate_in * (1.0 - gate_sig)))).astype(BF16)
    rate = -jnp.exp(a_log[...])
    rate2 = LOG2E * rate
    lanes = lax.broadcasted_iota(jnp.int32, (nstate, span), 1)
    count = span // GROUP

    def steps(i, loop):
        run, acc, d_b, d_c = list(loop[0]), list(loop[1]), loop[2], loop[3]
        start = pl.multiple_of((count - 1 - i) * GROUP, GROUP)
        shift = lax.rem(span - start, span)
        b_roll = pltpu.roll(b_in, shift, 1)
        c_roll = pltpu.roll(c_in, shift, 1)
        dt_rows = dt[pl.ds(start, GROUP), :]
        dtu_rows = dtu[pl.ds(start, GROUP), :]
        dy_rows = d_y[pl.ds(start, GROUP), :]
        for k in reversed(range(GROUP)):
            b_t = jnp.broadcast_to(b_roll[:, k : k + 1], (nstate, LANES))
            c_t = jnp.broadcast_to(c_roll[:, k : k + 1], (nstate, LANES))
            sum_b = 0.0
            sum_c = 0.0
            for g in range(groups):
                dt_t = dt_rows[k : k + 1, lane[g]]
                dtu_t = dtu_rows[k : k + 1, lane[g]]
                dy_t = dy_rows[k : k + 1, lane[g]]
                state = states[0, pl.ds(pl.multiple_of((start + k) * nstate, nstate), nstate), lane[g]]
                d_state = run[g] + c_t * dy_t
                kept = state - dtu_t * b_t
                d_exp = d_state * kept
                acc[g] = acc[g] + d_exp * dt_t
                run[g] = jnp.exp2(dt_t * rate2[:, lane[g]]) * d_state
                term_q = d_exp * rate[:, lane[g]]
                term_r = d_state * b_t
                rows = slice(k * GROUP, (k + 1) * GROUP)
                pend_q[g, rows, :] = sum(term_q[s : s + GROUP] for s in range(0, nstate, GROUP))
                pend_r[g, rows, :] = sum(term_r[s : s + GROUP] for s in range(0, nstate, GROUP))
                sum_b = sum_b + d_state * dtu_t
                sum_c = sum_c + state * dy_t
            here = lanes == start + k
            d_b = jnp.where(here, jnp.sum(sum_b, axis=1, keepdims=True), d_b)
            d_c = jnp.where(here, jnp.sum(sum_c, axis=1, keepdims=True), d_c)
        fold(pend_q, d_dta, start)
        fold(pend_r, d_dtu, start)
        return tuple(run), tuple(acc), d_b, d_c

    empty = jnp.zeros((nstate, span), F32)
    run, acc, d_b, d_c = lax.fori_loop(
        0,
        count,
        steps,
        (tuple(carry[:, l] for l in lane), tuple(g_rate[:, l] for l in lane), empty, empty),
    )
    for g in range(groups):
        carry[:, lane[g]] = run[g]
        g_rate[:, lane[g]] = acc[g]
    d_lin = (d_dtu[...] * u + d_dta[...]) * sigmoid(lin)
    d_scan[0] = d_dtu[...] * step + d_rows * skip[...]
    d_low = d_lin.astype(BF16)
    full = jnp.concatenate([contract(dt_w[...], d_low, 1, 1), d_b, d_c], axis=0)
    d_proj[0] = full
    d_proj_low[0] = full.astype(BF16)
    small[:rank, :] += jnp.dot(dt_low, d_low, preferred_element_type=F32)
    row = rank + nstate
    small[row : row + 1, :] += jnp.sum(d_lin, axis=0, keepdims=True)
    small[row + 1 : row + 2, :] += jnp.sum(d_rows * u, axis=0, keepdims=True)

    @pl.when(last)
    def _():
        small[rank : rank + nstate, :] = g_rate[...] * rate


def post_kernel(parts, ids, *refs):
    projs, refs = refs[:parts], refs[parts:]
    xs, refs = refs[:parts], refs[parts:]
    d_scan, d_gate, u_act, summed, inner, inv, w_full, gain, xw_t, conv_w = refs[:10]
    refs = refs[10:]
    d_both, small, tiny, own = refs[:4]
    sends, refs = refs[4 : 3 + parts], refs[3 + parts :]
    padded, front = refs
    tokens, chans = d_scan.shape[1:]
    quarter = own.shape[2]
    taps = conv_w.shape[0]
    m = pl.program_id(0)

    @pl.when(m == 0)
    def _():
        padded[tokens:, :] = jnp.zeros((GROUP, chans), F32)
        front[:GROUP, :] = jnp.zeros((GROUP, chans), F32)
        small[...] = jnp.zeros(small.shape, F32)
        tiny[...] = jnp.zeros(tiny.shape, F32)

    proj = projs[0][0]
    for other in projs[1:]:
        proj = proj + other[0].astype(F32)
    d_proj = proj.astype(BF16)
    count = d_proj.shape[0]
    d_u = d_scan[0] + contract(d_proj, xw_t[...], 0, 0)
    small[:count, :] += jnp.dot(d_proj, u_act[0].astype(BF16), preferred_element_type=F32)
    conv = summed[0]
    sig = sigmoid(conv)
    d_conv = d_u * (sig * (1.0 + conv * (1.0 - sig)))
    padded[:tokens, :] = d_conv
    front[GROUP:, :] = inner[0]
    d_inner = 0.0
    for j in range(taps):
        d_inner = d_inner + conv_w[j : j + 1, :] * padded[pl.ds(taps - 1 - j, tokens), :]
        small[count + j : count + j + 1, :] += jnp.sum(
            d_conv * front[pl.ds(GROUP - taps + 1 + j, tokens), :], axis=0, keepdims=True
        )
    small[count + taps : count + taps + 1, :] += jnp.sum(d_conv, axis=0, keepdims=True)
    d_both[0, :, :chans] = d_inner.astype(BF16)
    d_both[0, :, chans:] = d_gate[0]
    scale = inv[0][:, :1]
    ones = jnp.ones((GROUP, quarter), F32)
    dots = 0.0
    for k in range(parts):
        cols = pl.ds(pl.multiple_of((ids[0] ^ k) * quarter, LANES), quarter)
        d_norm = contract(d_both[0], w_full[cols, :], 1, 1)
        if k == 0:
            own[0] = d_norm
        else:
            sends[k - 1][0] = d_norm.astype(BF16)
        along = d_norm * xs[k][0].astype(F32)
        tiny[0:1, cols] += jnp.sum(along * scale, axis=0, keepdims=True)
        dots = dots + lax.dot_general(
            ones,
            along * gain[:, cols],
            (((1,), (1,)), ((), ())),
            precision=lax.Precision.HIGHEST,
            preferred_element_type=F32,
        )
    tiny[1:2, pl.ds(pl.multiple_of(m * tokens, LANES), tokens)] = dots[:1]


def grad_in_kernel(chips, ids, normed, d_both, mine, theirs):
    if chips == 0:
        mine[...] = contract(normed[...], d_both[...], 0, 0)
        return
    rows = mine.shape[1]
    for side, out in enumerate((theirs, mine)):
        for j in range(chips):
            index = (ids[1] ^ (2 * j)) ^ (1 - side)
            cols = pl.ds(pl.multiple_of(index * rows, LANES), rows)
            out[j] = contract(normed[:, cols], d_both[...], 0, 0).astype(out.dtype)


def grad_out_kernel(chips, ids, gated, cot, mine, theirs):
    if chips == 0:
        mine[...] = contract(gated[...], cot[...], 0, 0)
        return
    width = mine.shape[2]
    for side, out in enumerate((theirs, mine)):
        for j in range(chips):
            index = (ids[1] ^ (2 * j)) ^ (1 - side)
            cols = pl.ds(pl.multiple_of(index * width, LANES), width)
            out[j] = contract(gated[...], cot[:, cols], 0, 0).astype(out.dtype)


def whole(shape):
    return pl.BlockSpec(shape, lambda *_: (0,) * len(shape))


SMEM = pl.BlockSpec(memory_space=pltpu.SMEM)


def params(grid, mib=56):
    return pltpu.CompilerParams(
        dimension_semantics=("arbitrary",) * grid, vmem_limit_bytes=mib * 1024 * 1024
    )


def struct(shape, dtype):
    return jax.ShapeDtypeStruct(shape, dtype)


def run_pre(ids, xs, ws, gain, conv_w, conv_b, xw_t):
    micro, tokens, quarter = xs[0].shape
    width = gain.shape[1]
    chans = conv_w.shape[1]
    count = xw_t.shape[0]
    per = lambda *tail: pl.BlockSpec((1,) + tail, lambda m: (m,) + (0,) * len(tail))
    return pl.pallas_call(
        partial(pre_kernel, len(xs), len(ws)),
        grid=(micro,),
        in_specs=[SMEM]
        + [per(tokens, quarter)] * len(xs)
        + [whole(w.shape) for w in ws]
        + [whole(gain.shape), whole(conv_w.shape), whole(conv_b.shape), whole(xw_t.shape)],
        out_specs=[
            per(tokens, width),
            whole((width, 2 * chans)),
            per(tokens, chans),
            per(tokens, chans),
            per(tokens, chans),
            per(tokens, chans),
            per(tokens, LANES),
            per(count, tokens),
            per(count, tokens),
        ],
        out_shape=[
            struct((micro, tokens, width), BF16),
            struct((width, 2 * chans), BF16),
            struct((micro, tokens, chans), F32),
            struct((micro, tokens, chans), F32),
            struct((micro, tokens, chans), F32),
            struct((micro, tokens, chans), F32),
            struct((micro, tokens, LANES), F32),
            struct((micro, count, tokens), F32),
            struct((micro, count, tokens), BF16),
        ],
        scratch_shapes=[pltpu.VMEM((tokens + GROUP, chans), F32)],
        compiler_params=params(1),
        name="pre",
    )(ids, *xs, *ws, gain, conv_w, conv_b, xw_t)


def run_fwd(ids, lens, projs, ws, u_act, gate, dt_w, dt_b, a_log, skip, width):
    micro, tokens, chans = u_act.shape
    parts = len(projs)
    quarter = width // parts
    count = projs[0].shape[1]
    nstate = a_log.shape[0]
    span = min(LANES, tokens)
    rows = lambda *tail: pl.BlockSpec((1, span) + tail, lambda m, b: (m, b) + (0,) * len(tail))
    return pl.pallas_call(
        partial(fwd_kernel, parts, len(ws)),
        grid=(micro, tokens // span),
        in_specs=[SMEM, SMEM]
        + [pl.BlockSpec((1, count, span), lambda m, b: (m, 0, b))] * parts
        + [whole(w.shape) for w in ws]
        + [rows(chans), rows(chans)]
        + [whole(v.shape) for v in (dt_w, dt_b, a_log, skip)],
        out_specs=[
            rows(chans),
            rows(chans),
            rows(chans),
            pl.BlockSpec((1, span * nstate, chans), lambda m, b: (m, b, 0)),
            whole((chans, width)),
        ]
        + [rows(quarter)] * parts,
        out_shape=[
            struct((micro, tokens, chans), F32),
            struct((micro, tokens, chans), F32),
            struct((micro, tokens, chans), BF16),
            struct((micro, tokens * nstate, chans), F32),
            struct((chans, width), BF16),
            struct((micro, tokens, quarter), F32),
        ]
        + [struct((micro, tokens, quarter), BF16)] * (parts - 1),
        scratch_shapes=[pltpu.VMEM((span, chans), F32)] * 3
        + [pltpu.VMEM((chans // LANES, GROUP * GROUP, LANES), F32), pltpu.VMEM((nstate, chans), F32)],
        compiler_params=params(2),
        name="scan_forward",
    )(ids, lens, *projs, *ws, u_act, gate, dt_w, dt_b, a_log, skip)


def run_bwd(ids, lens, projs, cots, w_full, u_act, gate, dt_lin, y_rows, states, dt_w, a_log, skip):
    micro, tokens, chans = u_act.shape
    parts = len(projs)
    width = w_full.shape[1]
    quarter = cots[0].shape[2]
    count = projs[0].shape[1]
    nstate = a_log.shape[0]
    rank = dt_w.shape[0]
    span = min(LANES, tokens)
    blocks = tokens // span
    small = rank + nstate + GROUP
    rows = lambda *tail: pl.BlockSpec(
        (1, span) + tail, lambda m, b: (m, blocks - 1 - b) + (0,) * len(tail)
    )
    proj = pl.BlockSpec((1, count, span), lambda m, b: (m, 0, blocks - 1 - b))
    return pl.pallas_call(
        partial(bwd_kernel, parts),
        grid=(micro, blocks),
        in_specs=[SMEM, SMEM]
        + [proj] * parts
        + [rows(quarter)] * parts
        + [whole(w_full.shape), rows(chans), rows(chans), rows(chans), rows(chans)]
        + [pl.BlockSpec((1, span * nstate, chans), lambda m, b: (m, blocks - 1 - b, 0))]
        + [whole(v.shape) for v in (dt_w, a_log, skip)],
        out_specs=[rows(width), proj, proj, rows(chans), rows(chans), whole((small, chans))],
        out_shape=[
            struct((micro, tokens, width), BF16),
            struct((micro, count, tokens), F32),
            struct((micro, count, tokens), BF16),
            struct((micro, tokens, chans), F32),
            struct((micro, tokens, chans), BF16),
            struct((small, chans), F32),
        ],
        scratch_shapes=[pltpu.VMEM((span, chans), F32)] * 5
        + [pltpu.VMEM((chans // LANES, GROUP * GROUP, LANES), F32)] * 2
        + [pltpu.VMEM((nstate, chans), F32)] * 2,
        compiler_params=params(2),
        name="scan_backward",
    )(ids, lens, *projs, *cots, w_full, u_act, gate, dt_lin, y_rows, states, dt_w, a_log, skip)


def run_post(ids, projs, xs, d_scan, d_gate, u_act, summed, inner, inv, w_full, gain, xw_t, conv_w):
    micro, tokens, chans = u_act.shape
    parts = len(projs)
    width = w_full.shape[0]
    quarter = width // parts
    count = projs[0].shape[1]
    taps = conv_w.shape[0]
    small = count + GROUP * -(-(taps + 1) // GROUP)
    lanes = max(width, LANES * -(-micro * tokens // LANES))
    per = lambda *tail: pl.BlockSpec((1,) + tail, lambda m: (m,) + (0,) * len(tail))
    return pl.pallas_call(
        partial(post_kernel, parts),
        grid=(micro,),
        in_specs=[SMEM]
        + [per(count, tokens)] * parts
        + [per(tokens, quarter)] * parts
        + [per(tokens, chans)] * 5
        + [per(tokens, LANES)]
        + [whole(v.shape) for v in (w_full, gain, xw_t, conv_w)],
        out_specs=[per(tokens, 2 * chans), whole((small, chans)), whole((GROUP, lanes))]
        + [per(tokens, quarter)] * parts,
        out_shape=[
            struct((micro, tokens, 2 * chans), BF16),
            struct((small, chans), F32),
            struct((GROUP, lanes), F32),
            struct((micro, tokens, quarter), F32),
        ]
        + [struct((micro, tokens, quarter), BF16)] * (parts - 1),
        scratch_shapes=[pltpu.VMEM((tokens + GROUP, chans), F32)] * 2,
        compiler_params=params(1),
        name="post",
    )(ids, *projs, *xs, d_scan, d_gate, u_act, summed, inner, inv, w_full, gain, xw_t, conv_w)


def run_grad(kernel, name, ids, left, right, shape, chips):
    if chips == 0:
        outs = [struct(shape, F32), struct((GROUP, LANES), BF16)]
    else:
        outs = [struct((chips,) + shape, F32), struct((chips,) + shape, BF16)]
    return pl.pallas_call(
        partial(kernel, chips),
        in_specs=[SMEM, pl.BlockSpec(memory_space=pltpu.VMEM), pl.BlockSpec(memory_space=pltpu.VMEM)],
        out_specs=[pl.BlockSpec(memory_space=pltpu.VMEM)] * 2,
        out_shape=outs,
        compiler_params=pltpu.CompilerParams(vmem_limit_bytes=56 * 1024 * 1024),
        name=name,
    )(ids, left, right)


def others(value, axis, step=1):
    count = lax.axis_size(axis)
    return [swap(value, axis, mask) for mask in range(step, count, step)]


def gather_blocks(shard):
    mine = [shard] + others(shard, "dp", 2)
    return mine + [swap(block, "dp", 1) for block in mine]


def sum_scattered(mine, theirs):
    got = swap(theirs, "dp", 1)
    total = mine + got.astype(F32)
    result = total[0]
    for j in range(1, mine.shape[0]):
        result = result + swap(total[j].astype(BF16), "dp", 2 * j).astype(F32)
    return result


def sum_all(value):
    core = lax.rem(lax.axis_index("dp"), 2)
    half = value.shape[0] // 2
    halves = value.reshape((2, half) + value.shape[1:])
    mine = lax.dynamic_index_in_dim(halves, core, 0, keepdims=False)
    theirs = lax.dynamic_index_in_dim(halves, 1 - core, 0, keepdims=False)
    total = mine + swap(theirs, "dp", 1)
    for got in others(total, "dp", 2):
        total = total + got
    other = swap(total, "dp", 1)
    first = jnp.where(core == 0, total, other)
    second = jnp.where(core == 0, other, total)
    return jnp.concatenate([first, second], axis=0)


def body(
    tokens,
    lengths,
    norm_gain,
    in_weight,
    x_weight,
    dt_weight,
    dt_bias,
    conv_weight,
    conv_bias,
    a_log,
    skip,
    out_weight,
    cotangent,
):
    micro, seq, quarter = tokens.shape
    chans = in_weight.shape[2]
    width = norm_gain.shape[0]
    dps = lax.axis_size("dp")
    rank = dt_weight.shape[0]
    nstate = a_log.shape[0]
    taps = conv_weight.shape[0]
    count = x_weight.shape[1]
    ids = jnp.stack([lax.axis_index("tensor"), lax.axis_index("dp")]).astype(jnp.int32)
    lens = lengths[:, 0]
    gain = norm_gain[None]
    xw_t = x_weight.T
    in_rows = in_weight.reshape(in_weight.shape[0], 2 * chans)
    by_block = in_rows.shape[0] % LANES == 0 and out_weight.shape[1] % LANES == 0
    chips = dps // 2 if by_block else 0

    xs = [tokens] + others(tokens, "tensor")
    if by_block:
        in_blocks = gather_blocks(in_rows)
        out_blocks = gather_blocks(out_weight)
    else:
        in_blocks = [lax.all_gather(in_rows, "dp", axis=0, tiled=True)]
        out_blocks = [lax.all_gather(out_weight, "dp", axis=1, tiled=True)]
    cots = [cotangent] + others(cotangent, "tensor")

    normed, in_full, inner, summed, u_act, gate, inv, proj, proj_low = run_pre(
        ids, xs, in_blocks, gain, conv_weight, conv_bias[None], xw_t
    )
    projs = [proj] + others(proj_low, "tensor")
    dt_lin, y_rows, gated, states, out_full, own_out, *out_terms = run_fwd(
        ids, lens, projs, out_blocks, u_act, gate, dt_weight, dt_bias[None], a_log, skip[None], width
    )
    branch = own_out
    for k, term in enumerate(out_terms):
        branch = branch + swap(term, "tensor", k + 1).astype(F32)
    mixed = (tokens.astype(F32) + branch).astype(BF16)
    cot_full, d_proj, d_proj_low, d_scan, d_gate, small = run_bwd(
        ids, lens, projs, cots, out_full, u_act, gate, dt_lin, y_rows, states, dt_weight, a_log, skip[None]
    )
    d_projs = [d_proj] + others(d_proj_low, "tensor")
    out_mine, out_theirs = run_grad(
        grad_out_kernel,
        "grad_out",
        ids,
        gated.reshape(micro * seq, chans),
        cot_full.reshape(micro * seq, width),
        (chans, out_weight.shape[1]) if chips else (chans, width),
        chips,
    )
    d_both, small_in, tiny, own_norm, *norm_terms = run_post(
        ids, d_projs, xs, d_scan, d_gate, u_act, summed, inner, inv, in_full, gain, xw_t, conv_weight
    )
    in_mine, in_theirs = run_grad(
        grad_in_kernel,
        "grad_in",
        ids,
        normed.reshape(micro * seq, width),
        d_both.reshape(micro * seq, 2 * chans),
        (in_rows.shape[0], 2 * chans) if chips else (width, 2 * chans),
        chips,
    )
    for got in others(tiny, "tensor"):
        tiny = tiny + got
    d_norm = own_norm
    for k, term in enumerate(norm_terms):
        d_norm = d_norm + swap(term, "tensor", k + 1).astype(F32)
    if chips:
        grad_out = sum_scattered(out_mine, out_theirs)
        grad_in = sum_scattered(in_mine, in_theirs)
    else:
        grad_out = lax.psum_scatter(out_mine, "dp", scatter_dimension=1, tiled=True)
        grad_in = lax.psum_scatter(in_mine, "dp", scatter_dimension=0, tiled=True)
    small = sum_all(small)
    gain_rows = tiny[0, :width].reshape(-1, chans)
    small_in = lax.dynamic_update_slice_in_dim(small_in, gain_rows, count + taps + 1, 0)
    small_in = sum_all(small_in)
    scale = inv[:, :, :1]
    dots = tiny[1, : micro * seq].reshape(micro, seq, 1)
    own_gain = lax.dynamic_slice_in_dim(norm_gain, ids[0] * quarter, quarter, 0)
    d_x = scale * (d_norm * own_gain) - tokens.astype(F32) * (scale * scale * scale * dots / width)
    input_grad = cotangent.astype(F32) + d_x
    row = count + taps + 1
    return (
        mixed,
        input_grad,
        small_in[row : row + width // chans].reshape(width),
        grad_in.reshape(in_weight.shape),
        small_in[:count].T,
        small[:rank],
        small[rank + nstate],
        small_in[count : count + taps],
        small_in[count + taps],
        small[rank : rank + nstate],
        small[rank + nstate + 1],
        grad_out,
    )


def solution(mesh):
    rows = P(None, "dp", "tensor")
    chans = P(None, "tensor")
    return jax.shard_map(
        body,
        mesh=mesh,
        in_specs=(
            rows,
            P(None, "dp"),
            P(),
            P("dp", None, "tensor"),
            P("tensor", None),
            chans,
            P("tensor"),
            chans,
            P("tensor"),
            chans,
            P("tensor"),
            P("tensor", "dp"),
            rows,
        ),
        out_specs=(
            rows,
            rows,
            P(),
            P("dp", None, "tensor"),
            P("tensor", None),
            chans,
            P("tensor"),
            chans,
            P("tensor"),
            chans,
            P("tensor"),
            P("tensor", "dp"),
        ),
        check_vma=False,
    )
```

profile of v0, /device:TPU:0, one launch (start us, length us, event | category | flops | bytes accessed | tf_op | source)
XLA Modules:
  0.0 241.6 jit_solution(3274638860135188943)
XLA Ops:
  0.6 3.0 %collective-permute-start.13 = (bf16[512,128]{1,0:T(8,128)(2,1)}, bf16[512,128]{1,0:T(8,128)(2,1)S(1)}, u32[]{:S(2)}, u32[]{:S(2)}) collective-permute-start(bf16[512,128]{1,0:T(8,128)(2,1)} %refs_4_.3), channel_id=1, source_target_pairs={{0,8},{4,12},{8,0},{12,4},{16,24},{20,28},{24,16},{28,20},{1,9},{5... | collective-permute-start | bytes 393224 | tf_op jit(solution)/shard_map/ppermute | solution.py:35
  10.1 2.9 %collective-permute-start.5 = (bf16[128,1024]{1,0:T(8,128)(2,1)S(1)}, bf16[128,1024]{1,0:T(8,128)(2,1)S(1)}, u32[]{:S(2)}, u32[]{:S(2)}) collective-permute-start(bf16[128,1024]{1,0:T(8,128)(2,1)S(1)} %bitcast.62), channel_id=1, source_target_pairs={{0,24},{4,28},{8,16},{12,20},{16,8},{20,12},{24,0},{28,4},{1,25},{... | collective-permute-start | bytes 786440 | tf_op jit(solution)/shard_map/ppermute | solution.py:35
  13.0 4.8 %collective-permute-done.15.refs_7_ = bf16[512,128]{1,0:T(8,128)(2,1)S(1)} collective-permute-done((bf16[512,128]{1,0:T(8,128)(2,1)}, bf16[512,128]{1,0:T(8,128)(2,1)S(1)}, u32[]{:S(2)}, u32[]{:S(2)}) %collective-permute-start.15) | collective-permute-done | bytes 131104 | tf_op jit(solution)/shard_map/ppermute | solution.py:35
  19.5 2.6 %collective-permute-start.1 = (bf16[2,256,256]{2,1,0:T(8,128)(2,1)}, bf16[2,256,256]{2,1,0:T(8,128)(2,1)S(1)}, u32[]{:S(2)}, u32[]{:S(2)}) collective-permute-start(bf16[2,256,256]{2,1,0:T(8,128)(2,1)} %refs_4_.5), channel_id=1, source_target_pairs={{0,2},{1,3},{2,0},{3,1},{4,6},{5,7},{6,4},{7,5},{8,10},{9,11},{10,... | collective-permute-start | bytes 786440 | tf_op jit(solution)/shard_map/ppermute | solution.py:35
  22.1 3.3 %collective-permute-done.4.refs_6_ = bf16[128,1024]{1,0:T(8,128)(2,1)S(1)} collective-permute-done((bf16[128,1024]{1,0:T(8,128)(2,1)S(1)}, bf16[128,1024]{1,0:T(8,128)(2,1)S(1)}, u32[]{:S(2)}, u32[]{:S(2)}) %collective-permute-start.4) | collective-permute-done | bytes 262176 | tf_op jit(solution)/shard_map/ppermute | solution.py:35
  25.4 3.6 %collective-permute-start.2 = (bf16[2,256,256]{2,1,0:T(8,128)(2,1)}, bf16[2,256,256]{2,1,0:T(8,128)(2,1)S(1)}, u32[]{:S(2)}, u32[]{:S(2)}) collective-permute-start(bf16[2,256,256]{2,1,0:T(8,128)(2,1)} %refs_4_.5), channel_id=1, source_target_pairs={{0,3},{1,2},{2,1},{3,0},{4,7},{5,6},{6,5},{7,4},{8,11},{9,10},{10,... | collective-permute-start | bytes 786440 | tf_op jit(solution)/shard_map/ppermute | solution.py:35
  29.5 2.6 %collective-permute-done.refs_1_.refs_5_ = bf16[2,256,256]{2,1,0:T(8,128)(2,1)S(1)} collective-permute-done((bf16[2,256,256]{2,1,0:T(8,128)(2,1)}, bf16[2,256,256]{2,1,0:T(8,128)(2,1)S(1)}, u32[]{:S(2)}, u32[]{:S(2)}) %collective-permute-start) | collective-permute-done | bytes 262176 | tf_op jit(solution)/shard_map/ppermute | solution.py:35
  32.1 8.6 %collective-permute-done.1.refs_2_.refs_6_ = bf16[2,256,256]{2,1,0:T(8,128)(2,1)S(1)} collective-permute-done((bf16[2,256,256]{2,1,0:T(8,128)(2,1)}, bf16[2,256,256]{2,1,0:T(8,128)(2,1)S(1)}, u32[]{:S(2)}, u32[]{:S(2)}) %collective-permute-start.1) | collective-permute-done | bytes 262176 | tf_op jit(solution)/shard_map/ppermute | solution.py:35
  42.1 4.5 %collective-permute-start.23 = (bf16[2,256,256]{2,1,0:T(8,128)(2,1)}, bf16[2,256,256]{2,1,0:T(8,128)(2,1)S(1)}, u32[]{:S(2)}, u32[]{:S(2)}) collective-permute-start(bf16[2,256,256]{2,1,0:T(8,128)(2,1)} %refs_4_.4), channel_id=1, source_target_pairs={{0,1},{1,0},{2,3},{3,2},{4,5},{5,4},{6,7},{7,6},{8,9},{9,8},{10,11... | collective-permute-start | bytes 786440 | tf_op jit(solution)/shard_map/ppermute | solution.py:35
  50.2 6.7 %pre.1 = (bf16[2,256,1024]{2,1,0:T(8,128)(2,1)}, bf16[1024,1024]{1,0:T(8,128)(2,1)}, f32[2,256,512]{2,1,0:T(8,128)}, f32[2,256,512]{2,1,0:T(8,128)}, f32[2,256,5...) custom-call(s32[2]{0:T(128)} %pad_add_fusion.ids, ...), custom_call_target="tpu_custom_call" | custom-call | tf_op jit(solution)/shard_map/pre/pallas_call | solution.py:420
  57.6 2.5 %collective-permute-start.11 = (bf16[2,96,256]{2,1,0:T(8,128)(2,1)}, bf16[2,96,256]{2,1,0:T(8,128)(2,1)S(1)}, u32[]{:S(2)}, u32[]{:S(2)}) collective-permute-start(bf16[2,96,256]{2,1,0:T(8,128)(2,1)} %get-tuple-element.48), channel_id=1, source_target_pairs={{0,2},{1,3},{2,0},{3,1},{4,6},{5,7},{6,4},{7,5},{8,10},{9,11},{10,... | collective-permute-start | bytes 294920 | tf_op jit(solution)/shard_map/ppermute | solution.py:35
  60.0 8.5 %collective-permute-done.10.refs_1_ = bf16[2,96,256]{2,1,0:T(8,128)(2,1)S(1)} collective-permute-done((bf16[2,96,256]{2,1,0:T(8,128)(2,1)}, bf16[2,96,256]{2,1,0:T(8,128)(2,1)S(1)}, u32[]{:S(2)}, u32[]{:S(2)}) %collective-permute-start.10) | collective-permute-done | bytes 98336 | tf_op jit(solution)/shard_map/ppermute | solution.py:35
  68.5 3.2 %collective-permute-start.12 = (bf16[2,96,256]{2,1,0:T(8,128)(2,1)}, bf16[2,96,256]{2,1,0:T(8,128)(2,1)S(1)}, u32[]{:S(2)}, u32[]{:S(2)}) collective-permute-start(bf16[2,96,256]{2,1,0:T(8,128)(2,1)} %get-tuple-element.48), channel_id=1, source_target_pairs={{0,3},{1,2},{2,1},{3,0},{4,7},{5,6},{6,5},{7,4},{8,11},{9,10},{10,... | collective-permute-start | bytes 294920 | tf_op jit(solution)/shard_map/ppermute | solution.py:35
  71.7 8.4 %collective-permute-done.11.refs_2_ = bf16[2,96,256]{2,1,0:T(8,128)(2,1)S(1)} collective-permute-done((bf16[2,96,256]{2,1,0:T(8,128)(2,1)}, bf16[2,96,256]{2,1,0:T(8,128)(2,1)S(1)}, u32[]{:S(2)}, u32[]{:S(2)}) %collective-permute-start.11) | collective-permute-done | bytes 98336 | tf_op jit(solution)/shard_map/ppermute | solution.py:35
  80.9 21.4 %scan_forward.1 = (f32[2,256,512]{2,1,0:T(8,128)}, f32[2,256,512]{2,1,0:T(8,128)}, bf16[2,256,512]{2,1,0:T(8,128)(2,1)}, f32[2,4096,512]{2,1,0:T(8,128)}, bf16[5...) custom-call(s32[2]{0:T(128)} %pad_add_fusion.ids, ...), custom_call_target="tpu_custom_call" | custom-call | tf_op jit(solution)/shard_map/scan_forward/pallas_call | solution.py:463
  103.2 41.4 %scan_backward.1 = (bf16[2,256,1024]{2,1,0:T(8,128)(2,1)}, f32[2,96,256]{2,1,0:T(8,128)}, bf16[2,96,256]{2,1,0:T(8,128)(2,1)}, f32[2,256,512]{2,1,0:T(8,128)}, b...) custom-call(s32[2]{0:T(128)} %pad_add_fusion.ids, s32[2]{0:T(128)} %bitcast.76, f32[2,96,256]{2,1,0:T(8,128)} %get-tuple-element.47.refs_0_, ...), custom_call_target="tpu_custom_call" | custom-call | tf_op jit(solution)/shard_map/scan_backward/pallas_call | solution.py:510
  151.9 3.7 %grad_out.1 = (f32[4,512,128]{2,1,0:T(8,128)}, bf16[4,512,128]{2,1,0:T(8,128)(2,1)}) custom-call(s32[2]{0:T(128)} %pad_add_fusion.ids, bf16[512,512]{1,0:T(8,128)(2,1)} %bitcast.66, bf16[512,1024]{1,0:T(8,128)(2,1)} %bitcast.65), custom_call_target="tpu_custom_call" | custom-call | tf_op jit(solution)/shard_map/grad_out/pallas_call | solution.py:575
  158.3 9.5 %post.1 = (bf16[2,256,1024]{2,1,0:T(8,128)(2,1)}, f32[104,512]{1,0:T(8,128)}, f32[8,1024]{1,0:T(8,128)}, f32[2,256,256]{2,1,0:T(8,128)}, bf16[2,256,256]{2,1,0:T...) custom-call(s32[2]{0:T(128)} %pad_add_fusion.ids, f32[2,96,256]{2,1,0:T(8,128)} %get-tuple-element.60.refs_0_, ...), custom_call_target="tpu_custom_call" | custom-call | tf_op jit(solution)/shard_map/post/pallas_call | solution.py:546
  169.8 2.4 %collective-permute-start.34 = (f32[8,1024]{1,0:T(8,128)}, f32[8,1024]{1,0:T(8,128)S(1)}, u32[]{:S(2)}, u32[]{:S(2)}) collective-permute-start(f32[8,1024]{1,0:T(8,128)} %get-tuple-element.71), channel_id=1, source_target_pairs={{0,3},{1,2},{2,1},{3,0},{4,7},{5,6},{6,5},{7,4},{8,11},{9,10},{10,... | collective-permute-start | bytes 98312 | tf_op jit(solution)/shard_map/ppermute | solution.py:35
  172.3 4.2 %grad_in.1 = (f32[4,128,1024]{2,1,0:T(8,128)}, bf16[4,128,1024]{2,1,0:T(8,128)(2,1)}) custom-call(s32[2]{0:T(128)} %pad_add_fusion.ids, bf16[512,1024]{1,0:T(8,128)(2,1)} %bitcast.58, bf16[512,1024]{1,0:T(8,128)(2,1)} %bitcast.59), custom_call_target="tpu_custom_call" | custom-call | tf_op jit(solution)/shard_map/grad_in/pallas_call | solution.py:575
  196.5 3.6 %collective-permute-done.22 = bf16[2,256,256]{2,1,0:T(8,128)(2,1)S(1)} collective-permute-done((bf16[2,256,256]{2,1,0:T(8,128)(2,1)}, bf16[2,256,256]{2,1,0:T(8,128)(2,1)S(1)}, u32[]{:S(2)}, u32[]{:S(2)}) %collective-permute-start.22) | collective-permute-done | bytes 262176 | tf_op jit(solution)/shard_map/ppermute | solution.py:35
  200.0 6.3 %collective-permute-done.29 = bf16[2,256,256]{2,1,0:T(8,128)(2,1)S(1)} collective-permute-done((bf16[2,256,256]{2,1,0:T(8,128)(2,1)}, bf16[2,256,256]{2,1,0:T(8,128)(2,1)S(1)}, u32[]{:S(2)}, u32[]{:S(2)}) %collective-permute-start.29) | collective-permute-done | bytes 262176 | tf_op jit(solution)/shard_map/ppermute | solution.py:35
  206.3 13.9 %collective-permute-done.30 = bf16[2,256,256]{2,1,0:T(8,128)(2,1)S(1)} collective-permute-done((bf16[2,256,256]{2,1,0:T(8,128)(2,1)}, bf16[2,256,256]{2,1,0:T(8,128)(2,1)S(1)}, u32[]{:S(2)}, u32[]{:S(2)}) %collective-permute-start.30) | collective-permute-done | bytes 262176 | tf_op jit(solution)/shard_map/ppermute | solution.py:35
  232.9 3.7 %collective-permute-done.41 = bf16[128,1024]{1,0:T(8,128)(2,1)S(1)} collective-permute-done((bf16[128,1024]{1,0:T(8,128)(2,1)S(1)}, bf16[128,1024]{1,0:T(8,128)(2,1)S(1)}, u32[]{:S(2)}, u32[]{:S(2)}) %collective-permute-start.41) | collective-permute-done | bytes 262176 | tf_op jit(solution)/shard_map/ppermute | solution.py:35
  (194 shorter events, 65.1 us)
Async XLA Ops:
  4.6 14.9 %collective-permute-start.3 = (bf16[128,1024]{1,0:T(8,128)(2,1)S(1)}, bf16[128,1024]{1,0:T(8,128)(2,1)S(1)}, u32[]{:S(2)}, u32[]{:S(2)}) collective-permute-start(bf16[128,1024]{1,0:T(8,128)(2,1)S(1)} %bitcast.60), channel_id=1, source_target_pairs={{0,8},{4,12},{8,0},{12,4},{16,24},{20,28},{24,16},{28,20},{1,9},{5... | collective-permute-start | bytes 786440 | tf_op jit(solution)/shard_map/ppermute | solution.py:35
  8.2 17.1 %collective-permute-start.4 = (bf16[128,1024]{1,0:T(8,128)(2,1)S(1)}, bf16[128,1024]{1,0:T(8,128)(2,1)S(1)}, u32[]{:S(2)}, u32[]{:S(2)}) collective-permute-start(bf16[128,1024]{1,0:T(8,128)(2,1)S(1)} %bitcast.61), channel_id=1, source_target_pairs={{0,16},{4,20},{8,24},{12,28},{16,0},{20,4},{24,8},{28,12},{1,17},{... | collective-permute-start | bytes 786440 | tf_op jit(solution)/shard_map/ppermute | solution.py:35
  10.1 18.9 %collective-permute-start.5 = (bf16[128,1024]{1,0:T(8,128)(2,1)S(1)}, bf16[128,1024]{1,0:T(8,128)(2,1)S(1)}, u32[]{:S(2)}, u32[]{:S(2)}) collective-permute-start(bf16[128,1024]{1,0:T(8,128)(2,1)S(1)} %bitcast.62), channel_id=1, source_target_pairs={{0,24},{4,28},{8,16},{12,20},{16,8},{20,12},{24,0},{28,4},{1,25},{... | collective-permute-start | bytes 786440 | tf_op jit(solution)/shard_map/ppermute | solution.py:35
  17.9 14.3 %collective-permute-start = (bf16[2,256,256]{2,1,0:T(8,128)(2,1)}, bf16[2,256,256]{2,1,0:T(8,128)(2,1)S(1)}, u32[]{:S(2)}, u32[]{:S(2)}) collective-permute-start(bf16[2,256,256]{2,1,0:T(8,128)(2,1)} %refs_4_.5), channel_id=1, source_target_pairs={{0,1},{1,0},{2,3},{3,2},{4,5},{5,4},{6,7},{7,6},{8,9},{9,8},{10,11... | collective-permute-start | bytes 786440 | tf_op jit(solution)/shard_map/ppermute | solution.py:35
  19.5 21.2 %collective-permute-start.1 = (bf16[2,256,256]{2,1,0:T(8,128)(2,1)}, bf16[2,256,256]{2,1,0:T(8,128)(2,1)S(1)}, u32[]{:S(2)}, u32[]{:S(2)}) collective-permute-start(bf16[2,256,256]{2,1,0:T(8,128)(2,1)} %refs_4_.5), channel_id=1, source_target_pairs={{0,2},{1,3},{2,0},{3,1},{4,6},{5,7},{6,4},{7,5},{8,10},{9,11},{10,... | collective-permute-start | bytes 786440 | tf_op jit(solution)/shard_map/ppermute | solution.py:35
  25.4 15.4 %collective-permute-start.2 = (bf16[2,256,256]{2,1,0:T(8,128)(2,1)}, bf16[2,256,256]{2,1,0:T(8,128)(2,1)S(1)}, u32[]{:S(2)}, u32[]{:S(2)}) collective-permute-start(bf16[2,256,256]{2,1,0:T(8,128)(2,1)} %refs_4_.5), channel_id=1, source_target_pairs={{0,3},{1,2},{2,1},{3,0},{4,7},{5,6},{6,5},{7,4},{8,11},{9,10},{10,... | collective-permute-start | bytes 786440 | tf_op jit(solution)/shard_map/ppermute | solution.py:35
  29.0 17.6 %collective-permute-start.7 = (bf16[128,1024]{1,0:T(8,128)(2,1)S(1)}, bf16[128,1024]{1,0:T(8,128)(2,1)S(1)}, u32[]{:S(2)}, u32[]{:S(2)}) collective-permute-start(bf16[128,1024]{1,0:T(8,128)(2,1)S(1)} %collective-permute-done.3.refs_5_), channel_id=1, source_target_pairs={{0,4},{4,0},{8,12},{12,8},{16,20},{20,16},{24,28},{28,24},{1,5},{5... | collective-permute-start | bytes 786440 | tf_op jit(solution)/shard_map/ppermute | solution.py:35
  29.0 19.2 %collective-permute-start.8 = (bf16[128,1024]{1,0:T(8,128)(2,1)S(1)}, bf16[128,1024]{1,0:T(8,128)(2,1)S(1)}, u32[]{:S(2)}, u32[]{:S(2)}) collective-permute-start(bf16[128,1024]{1,0:T(8,128)(2,1)S(1)} %collective-permute-done.4.refs_6_), channel_id=1, source_target_pairs={{0,4},{4,0},{8,12},{12,8},{16,20},{20,16},{24,28},{28,24},{1,5},{5... | collective-permute-start | bytes 786440 | tf_op jit(solution)/shard_map/ppermute | solution.py:35
  32.1 17.4 %collective-permute-start.9 = (bf16[128,1024]{1,0:T(8,128)(2,1)S(1)}, bf16[128,1024]{1,0:T(8,128)(2,1)}, u32[]{:S(2)}, u32[]{:S(2)}) collective-permute-start(bf16[128,1024]{1,0:T(8,128)(2,1)S(1)} %collective-permute-done.5.refs_7_), channel_id=1, source_target_pairs={{0,4},{4,0},{8,12},{12,8},{16,20},{20,16},{24,28},{28,24},{1,5},{5... | collective-permute-start | bytes 786440 | tf_op jit(solution)/shard_map/ppermute | solution.py:35
  40.8 16.2 %collective-permute-start.18 = (bf16[512,128]{1,0:T(8,128)(2,1)}, bf16[512,128]{1,0:T(8,128)(2,1)}, u32[]{:S(2)}, u32[]{:S(2)}) collective-permute-start(bf16[512,128]{1,0:T(8,128)(2,1)} %collective-permute-done.14.refs_6_), channel_id=1, source_target_pairs={{0,4},{4,0},{8,12},{12,8},{16,20},{20,16},{24,28},{28,24},{1,5},{5... | collective-permute-start | bytes 393224 | tf_op jit(solution)/shard_map/ppermute | solution.py:35
  42.1 60.2 %collective-permute-start.23 = (bf16[2,256,256]{2,1,0:T(8,128)(2,1)}, bf16[2,256,256]{2,1,0:T(8,128)(2,1)S(1)}, u32[]{:S(2)}, u32[]{:S(2)}) collective-permute-start(bf16[2,256,256]{2,1,0:T(8,128)(2,1)} %refs_4_.4), channel_id=1, source_target_pairs={{0,1},{1,0},{2,3},{3,2},{4,5},{5,4},{6,7},{7,6},{8,9},{9,8},{10,11... | collective-permute-start | bytes 786440 | tf_op jit(solution)/shard_map/ppermute | solution.py:35
  46.6 55.7 %collective-permute-start.24 = (bf16[2,256,256]{2,1,0:T(8,128)(2,1)}, bf16[2,256,256]{2,1,0:T(8,128)(2,1)S(1)}, u32[]{:S(2)}, u32[]{:S(2)}) collective-permute-start(bf16[2,256,256]{2,1,0:T(8,128)(2,1)} %refs_4_.4), channel_id=1, source_target_pairs={{0,2},{1,3},{2,0},{3,1},{4,6},{5,7},{6,4},{7,5},{8,10},{9,11},{10,... | collective-permute-start | bytes 786440 | tf_op jit(solution)/shard_map/ppermute | solution.py:35
  48.2 54.1 %collective-permute-start.25 = (bf16[2,256,256]{2,1,0:T(8,128)(2,1)}, bf16[2,256,256]{2,1,0:T(8,128)(2,1)S(1)}, u32[]{:S(2)}, u32[]{:S(2)}) collective-permute-start(bf16[2,256,256]{2,1,0:T(8,128)(2,1)} %refs_4_.4), channel_id=1, source_target_pairs={{0,3},{1,2},{2,1},{3,0},{4,7},{5,6},{6,5},{7,4},{8,11},{9,10},{10,... | collective-permute-start | bytes 786440 | tf_op jit(solution)/shard_map/ppermute | solution.py:35
  57.6 22.6 %collective-permute-start.11 = (bf16[2,96,256]{2,1,0:T(8,128)(2,1)}, bf16[2,96,256]{2,1,0:T(8,128)(2,1)S(1)}, u32[]{:S(2)}, u32[]{:S(2)}) collective-permute-start(bf16[2,96,256]{2,1,0:T(8,128)(2,1)} %get-tuple-element.48), channel_id=1, source_target_pairs={{0,2},{1,3},{2,0},{3,1},{4,6},{5,7},{6,4},{7,5},{8,10},{9,11},{10,... | collective-permute-start | bytes 294920 | tf_op jit(solution)/shard_map/ppermute | solution.py:35
  150.0 19.8 %collective-permute-start.44 = (f32[44,512]{1,0:T(8,128)S(1)}, f32[44,512]{1,0:T(8,128)S(1)}, u32[]{:S(2)}, u32[]{:S(2)}) collective-permute-start(f32[44,512]{1,0:T(8,128)S(1)} %dynamic-slice_bitcast_fusion.1), channel_id=1, source_target_pairs={{0,4},{4,0},{8,12},{12,8},{16,20},{20,16},{24,28},{28,24},{1,5},{5... | collective-permute-start | bytes 270344 | tf_op jit(solution)/shard_map/ppermute | solution.py:35
  150.8 38.0 %collective-permute-start.20 = (bf16[2,256,256]{2,1,0:T(8,128)(2,1)}, bf16[2,256,256]{2,1,0:T(8,128)(2,1)S(1)}, u32[]{:S(2)}, u32[]{:S(2)}) collective-permute-start(bf16[2,256,256]{2,1,0:T(8,128)(2,1)} %get-tuple-element.52), channel_id=1, source_target_pairs={{0,1},{1,0},{2,3},{3,2},{4,5},{5,4},{6,7},{7,6},{8,9},{9,8},{10,11... | collective-permute-start | bytes 786440 | tf_op jit(solution)/shard_map/ppermute | solution.py:35
  155.6 40.8 %collective-permute-start.21 = (bf16[2,256,256]{2,1,0:T(8,128)(2,1)}, bf16[2,256,256]{2,1,0:T(8,128)(2,1)S(1)}, u32[]{:S(2)}, u32[]{:S(2)}) collective-permute-start(bf16[2,256,256]{2,1,0:T(8,128)(2,1)} %get-tuple-element.53), channel_id=1, source_target_pairs={{0,2},{1,3},{2,0},{3,1},{4,6},{5,7},{6,4},{7,5},{8,10},{9,11},{10,... | collective-permute-start | bytes 786440 | tf_op jit(solution)/shard_map/ppermute | solution.py:35
  190.6 15.7 %collective-permute-start.29 = (bf16[2,256,256]{2,1,0:T(8,128)(2,1)}, bf16[2,256,256]{2,1,0:T(8,128)(2,1)S(1)}, u32[]{:S(2)}, u32[]{:S(2)}) collective-permute-start(bf16[2,256,256]{2,1,0:T(8,128)(2,1)} %get-tuple-element.68), channel_id=1, source_target_pairs={{0,1},{1,0},{2,3},{3,2},{4,5},{5,4},{6,7},{7,6},{8,9},{9,8},{10,11... | collective-permute-start | bytes 786440 | tf_op jit(solution)/shard_map/ppermute | solution.py:35
  190.8 29.5 %collective-permute-start.30 = (bf16[2,256,256]{2,1,0:T(8,128)(2,1)}, bf16[2,256,256]{2,1,0:T(8,128)(2,1)S(1)}, u32[]{:S(2)}, u32[]{:S(2)}) collective-permute-start(bf16[2,256,256]{2,1,0:T(8,128)(2,1)} %get-tuple-element.69), channel_id=1, source_target_pairs={{0,2},{1,3},{2,0},{3,1},{4,6},{5,7},{6,4},{7,5},{8,10},{9,11},{10,... | collective-permute-start | bytes 786440 | tf_op jit(solution)/shard_map/ppermute | solution.py:35
  193.7 26.6 %collective-permute-start.31 = (bf16[2,256,256]{2,1,0:T(8,128)(2,1)}, bf16[2,256,256]{2,1,0:T(8,128)(2,1)S(1)}, u32[]{:S(2)}, u32[]{:S(2)}) collective-permute-start(bf16[2,256,256]{2,1,0:T(8,128)(2,1)} %get-tuple-element.70), channel_id=1, source_target_pairs={{0,3},{1,2},{2,1},{3,0},{4,7},{5,6},{6,5},{7,4},{8,11},{9,10},{10,... | collective-permute-start | bytes 786440 | tf_op jit(solution)/shard_map/ppermute | solution.py:35
  196.4 25.2 %collective-permute-start.49 = (bf16[4,512,128]{2,1,0:T(8,128)(2,1)S(1)}, bf16[4,512,128]{2,1,0:T(8,128)(2,1)S(1)}, u32[]{:S(2)}, u32[]{:S(2)}) collective-permute-start(bf16[4,512,128]{2,1,0:T(8,128)(2,1)S(1)} %copy-done.34), channel_id=1, source_target_pairs={{0,4},{4,0},{8,12},{12,8},{16,20},{20,16},{24,28},{28,24},{1,5},{5... | collective-permute-start | bytes 1572872 | tf_op jit(solution)/shard_map/ppermute | solution.py:35
  200.0 25.3 %collective-permute-start.40 = (bf16[4,128,1024]{2,1,0:T(8,128)(2,1)S(1)}, bf16[4,128,1024]{2,1,0:T(8,128)(2,1)S(1)}, u32[]{:S(2)}, u32[]{:S(2)}) collective-permute-start(bf16[4,128,1024]{2,1,0:T(8,128)(2,1)S(1)} %copy-done.33), channel_id=1, source_target_pairs={{0,4},{4,0},{8,12},{12,8},{16,20},{20,16},{24,28},{28,24},{1,5},{5... | collective-permute-start | bytes 3145736 | tf_op jit(solution)/shard_map/ppermute | solution.py:35
  206.3 15.2 %collective-permute-start.39 = (f32[52,512]{1,0:T(8,128)S(1)}, f32[52,512]{1,0:T(8,128)S(1)}, u32[]{:S(2)}, u32[]{:S(2)}) collective-permute-start(f32[52,512]{1,0:T(8,128)S(1)} %add_add_fusion), channel_id=1, source_target_pairs={{0,4},{4,0},{8,12},{12,8},{16,20},{20,16},{24,28},{28,24},{1,5},{5... | collective-permute-start | bytes 319496 | tf_op jit(solution)/shard_map/ppermute | solution.py:35
  226.7 12.0 %collective-permute-start.42 = (bf16[128,1024]{1,0:T(8,128)(2,1)S(1)}, bf16[128,1024]{1,0:T(8,128)(2,1)S(1)}, u32[]{:S(2)}, u32[]{:S(2)}) collective-permute-start(bf16[128,1024]{1,0:T(8,128)(2,1)S(1)} %get-tuple-element.90), channel_id=1, source_target_pairs={{0,16},{4,20},{8,24},{12,28},{16,0},{20,4},{24,8},{28,12},{1,17},{... | collective-permute-start | bytes 786440 | tf_op jit(solution)/shard_map/ppermute | solution.py:35
  (64 other events, 826.3 us)
where the time goes:
time: 245 us; the launch traced here: 242 us
  Pallas kernels  86.8 us (35%)
  waiting for transfers between devices  73.6 us (30%)
  starting transfers between devices  64.9 us (26%)
  local copies, waits for them, and re-layouts  9.93 us (4%)
  other arithmetic  5.15 us (2%)
    ppermute x53, waiting for transfers between devices, swap(): return lax.ppermute(value, axis, [(i, i ^ mask) for i in range(count)])  73.6 us
    ppermute x53, starting transfers between devices, swap(): return lax.ppermute(value, axis, [(i, i ^ mask) for i in range(count)])  64.9 us
    pallas_call x1, Pallas kernels, run_bwd(): pl.pallas_call(partial(bwd_kernel, parts), grid=(micro, blocks), in_specs...  41.4 us
    pallas_call x1, Pallas kernels, run_fwd(): pl.pallas_call(partial(fwd_kernel, parts, len(ws)), grid=(micro, tokens /...  21.4 us
    pallas_call x1, Pallas kernels, run_post(): pl.pallas_call(partial(post_kernel, parts), grid=(micro,), in_specs=[SMEM...  9.49 us
    pallas_call x2, Pallas kernels, run_grad(): pl.pallas_call(partial(kernel, chips), in_specs=[SMEM, pl.BlockSpec(memor...  7.88 us
    pallas_call x1, Pallas kernels, run_pre(): pl.pallas_call(partial(pre_kernel, len(xs), len(ws)), grid=(micro,), in_s...  6.69 us
  transfers between devices with their start and end apart: 53, of which 21 were waited for; matrix products, arithmetic and copies ran while one was open for 5% of the time, Pallas kernels for 19%

commit v1 on v0

v1 whole, which is shorter than its diff:
```python
from functools import partial

import jax
import jax.numpy as jnp
from jax import lax
from jax.experimental import pallas as pl
from jax.experimental.pallas import tpu as pltpu
from jax.sharding import PartitionSpec as P

EPS = 1e-05
F32 = jnp.float32
BF16 = jnp.bfloat16
GROUP = 8
LANES = 128
STEP = 48


def contract(left, right, left_dim, right_dim):
    return lax.dot_general(
        left, right, (((left_dim,), (right_dim,)), ((), ())), preferred_element_type=F32
    )


def sigmoid(v):
    return 1.0 / (1.0 + jnp.exp(-v))


def softplus(v):
    return jnp.maximum(v, 0.0) + jnp.log1p(jnp.exp(-jnp.abs(v)))


def swap(value, axis, mask):
    count = lax.axis_size(axis)
    return lax.ppermute(value, axis, [(i, i ^ mask) for i in range(count)])


def pre_kernel(parts, blocks, ids, *refs):
    xs, refs = refs[:parts], refs[parts:]
    ws, refs = refs[:blocks], refs[blocks:]
    gain, conv_w, conv_b, xw_t = refs[:4]
    normed, w_full, inner, summed, u_act, gate, inv, proj, proj_low, padded = refs[4:]
    quarter = xs[0].shape[2]
    chans = inner.shape[2]

    @pl.when(pl.program_id(0) == 0)
    def _():
        gather_rows(ids, ws, w_full)
        padded[:GROUP, :] = jnp.zeros((GROUP, chans), F32)

    square = 0.0
    for x in xs:
        rows = x[0].astype(F32)
        square = square + jnp.sum(rows * rows, axis=1, keepdims=True)
    scale = lax.rsqrt(square / (parts * quarter) + EPS)
    inv[0] = jnp.broadcast_to(scale, inv.shape[1:])
    for k, x in enumerate(xs):
        cols = pl.ds(pl.multiple_of((ids[0] ^ k) * quarter, LANES), quarter)
        normed[0, :, cols] = (x[0].astype(F32) * scale * gain[:, cols]).astype(BF16)
    both = jnp.dot(normed[0], w_full[:, : 2 * chans], preferred_element_type=F32)
    gate[0] = both[:, chans:]
    inner_in = both[:, :chans]
    inner[0] = inner_in
    tokens = inner_in.shape[0]
    padded[GROUP:, :] = inner_in
    taps = conv_w.shape[0]
    total = jnp.broadcast_to(conv_b[...], inner_in.shape)
    for j in range(taps):
        total = total + conv_w[j : j + 1, :] * padded[pl.ds(GROUP - taps + 1 + j, tokens), :]
    summed[0] = total
    act = total * sigmoid(total)
    u_act[0] = act
    partial_sum = contract(xw_t[...], act.astype(BF16), 1, 1)
    proj[0] = partial_sum
    proj_low[0] = partial_sum.astype(BF16)


def core_half(ids, chans, flip=0):
    half = chans // 2
    return pl.ds(pl.multiple_of(((ids[1] & 1) ^ flip) * half, LANES), half)


def gather_rows(ids, blocks, full):
    if len(blocks) == 1:
        full[...] = blocks[0][...]
        return
    chips = len(blocks) // 2
    for side in range(2):
        for j in range(chips):
            block = blocks[side * chips + j]
            index = (ids[1] ^ (2 * j)) ^ side
            rows = block.shape[0]
            full[pl.ds(pl.multiple_of(index * rows, 16), rows), :] = block[...]


def split(v):
    high = v.astype(BF16)
    return high, (v - high.astype(F32)).astype(BF16)


def spread(left, right, out):
    count, span = left.shape
    lanes = lax.broadcasted_iota(jnp.int32, left.shape, 1)
    shape = (2 * span, 2 * LANES)
    from_left = lax.broadcasted_iota(jnp.int32, shape, 0) < span
    to_left = lax.broadcasted_iota(jnp.int32, shape, 1) < LANES
    ones = jnp.where(from_left == to_left, 1.0, 0.0).astype(BF16)
    rows = []
    for t in range(span):
        pair = [jnp.where(lanes == t, part, 0.0).astype(BF16) for part in (left, right)]
        rows.append(jnp.concatenate(pair, axis=1))
    out[...] = jnp.dot(jnp.concatenate(rows, axis=0), ones, preferred_element_type=F32)


def gather(left, right, count):
    span = right.shape[0]
    lanes = lax.broadcasted_iota(jnp.int32, (count, span), 1)
    wide = contract(left[...], right, 1, 1)
    totals = [jnp.zeros((count, span), F32)] * 4
    for t in range(span):
        totals[t % 4] = jnp.where(lanes == t, wide[t * count : (t + 1) * count, :], totals[t % 4])
    return (totals[0] + totals[1]) + (totals[2] + totals[3])


def sigmoid_of_softplus(step):
    series = step * (1.0 - step * (0.5 - step * (1.0 / 6.0 - step * (1.0 / 24.0))))
    return jnp.where(step < 0.05, series, 1.0 - jnp.exp(-step))


def fold(pend, out, start, half):
    for g in range(pend.shape[0]):
        total = pend[g, pl.ds(half * GROUP * GROUP, GROUP, stride=GROUP), :]
        for s in range(1, GROUP):
            total = total + pend[g, pl.ds(half * GROUP * GROUP + s, GROUP, stride=GROUP), :]
        out[pl.ds(start, GROUP), g * LANES : (g + 1) * LANES] = total


def fwd_kernel(parts, ids, lens, *refs):
    projs, refs = refs[:parts], refs[parts:]
    w_out, u_act, gate, dt_w, dt_b, a_log, skip = refs[:7]
    refs = refs[7:]
    dt, y_rows, gated, edge, low_state, vectors, own = refs[:7]
    sends, refs = refs[7 : 6 + parts], refs[6 + parts :]
    dtu, y, pend, carry = refs
    span, chans = dtu.shape
    nstate = a_log.shape[0]
    rank = dt_w.shape[0]
    block = pl.program_id(1)
    groups = chans // LANES

    @pl.when(block == 0)
    def _():
        carry[...] = jnp.zeros(carry.shape, F32)

    proj = projs[0][0]
    for other in projs[1:]:
        proj = proj + other[0].astype(F32)
    lin = contract(proj[:rank].astype(BF16), dt_w[...], 0, 0) + dt_b[...]
    step = softplus(lin)
    dt[0] = step
    dtu[...] = step * u_act[0]
    spread(proj[rank : rank + nstate], proj[rank + nstate :], vectors.at[0])
    rate = -jnp.exp(a_log[...])
    lane = [slice(g * LANES, (g + 1) * LANES) for g in range(groups)]

    edge[0, 0] = carry[...]

    def steps(i, state):
        state = list(state)
        for half in range(2):
            start = pl.multiple_of((2 * i + half) * GROUP, GROUP)
            dt_rows = dt[0, pl.ds(start, GROUP), :]
            dtu_rows = dtu[pl.ds(start, GROUP), :]
            for k in range(GROUP):
                at = pl.ds(pl.multiple_of((start + k) * nstate, nstate), nstate)
                b_t = vectors[0, at, :LANES]
                c_t = vectors[0, at, LANES:]
                rows = pl.ds((half * GROUP + k) * GROUP, GROUP)
                for g in range(groups):
                    dt_t = dt_rows[k : k + 1, lane[g]]
                    dtu_t = dtu_rows[k : k + 1, lane[g]]
                    new = jnp.exp(dt_t * rate[:, lane[g]]) * state[g] + dtu_t * b_t
                    state[g] = new
                    low_state[0, at, lane[g]] = new.astype(BF16)
                    term = c_t * new
                    pend[g, rows, :] = sum(term[s : s + GROUP] for s in range(0, nstate, GROUP))
            fold(pend, y, start, half)
        return tuple(state)

    last = lax.fori_loop(0, span // (2 * GROUP), steps, tuple(carry[:, l] for l in lane))
    for g in range(groups):
        carry[:, lane[g]] = last[g]
    rows = y[...] + skip[...] * u_act[0]
    y_rows[0] = rows
    gate_in = gate[0]
    position = block * span + lax.broadcasted_iota(jnp.int32, (span, 1), 0)
    live = (position < lens[pl.program_id(0)]).astype(F32)
    low = (rows * (gate_in * sigmoid(gate_in)) * live).astype(BF16)
    gated[0] = low
    quarter = own.shape[2]
    for k in range(parts):
        rows = pl.ds(pl.multiple_of((ids[0] ^ k) * quarter, LANES), quarter)
        term = contract(low, w_out[rows, :], 1, 1)
        if k == 0:
            own[0] = term
        else:
            sends[k - 1][0] = term.astype(BF16)


def bwd_kernel(parts, ids, lens, *refs):
    projs, refs = refs[:parts], refs[parts:]
    cots, refs = refs[:parts], refs[parts:]
    w_full, u_act, gate, dt, y_rows, edge, low_state, vectors, dt_w, a_log, skip = refs[:11]
    refs = refs[11:]
    cot_full, d_proj, d_proj_low, d_scan, d_gate, small = refs[:6]
    dtu, d_y, d_dtu, d_dta, pend_q, pend_r, carry, g_rate, low_grad = refs[6:]
    span, chans = dtu.shape
    nstate = a_log.shape[0]
    rank = dt_w.shape[0]
    first = (pl.program_id(0) == 0) & (pl.program_id(1) == 0)
    last = (pl.program_id(0) == pl.num_programs(0) - 1) & (pl.program_id(1) == pl.num_programs(1) - 1)
    block = pl.num_programs(1) - 1 - pl.program_id(1)
    groups = chans // LANES
    quarter = cots[0].shape[2]
    lane = [slice(g * LANES, (g + 1) * LANES) for g in range(groups)]

    @pl.when(first)
    def _():
        small[...] = jnp.zeros(small.shape, F32)
        g_rate[...] = jnp.zeros(g_rate.shape, F32)

    @pl.when(pl.program_id(1) == 0)
    def _():
        carry[...] = jnp.zeros(carry.shape, F32)

    for k, cot in enumerate(cots):
        cols = pl.ds(pl.multiple_of((ids[0] ^ k) * quarter, LANES), quarter)
        cot_full[0, :, cols] = cot[0]
    d_gated = jnp.dot(cot_full[0], w_full[...], preferred_element_type=F32)

    proj = projs[0][0]
    for other in projs[1:]:
        proj = proj + other[0].astype(F32)
    dt_low = proj[:rank].astype(BF16)
    u = u_act[0]
    step = dt[0]
    dtu[...] = step * u
    gate_in = gate[0]
    gate_sig = sigmoid(gate_in)
    position = block * span + lax.broadcasted_iota(jnp.int32, (span, 1), 0)
    live = (position < lens[pl.program_id(0)]).astype(F32)
    d_live = d_gated * live
    d_rows = d_live * (gate_in * gate_sig)
    d_y[...] = d_rows
    d_gate[0] = (d_live * y_rows[0] * (gate_sig * (1.0 + gate_in * (1.0 - gate_sig)))).astype(BF16)
    rate = -jnp.exp(a_log[...])
    count = span // (2 * GROUP)

    def steps(i, loop):
        run, acc = list(loop[0]), list(loop[1])
        for half in reversed(range(2)):
            start = pl.multiple_of((2 * (count - 1 - i) + half) * GROUP, GROUP)
            dt_rows = dt[0, pl.ds(start, GROUP), :]
            dy_rows = d_y[pl.ds(start, GROUP), :]
            for k in reversed(range(GROUP)):
                at = pl.ds(pl.multiple_of((start + k) * nstate, nstate), nstate)
                b_t = vectors[0, at, :LANES]
                c_t = vectors[0, at, LANES:]
                rows = pl.ds((half * GROUP + k) * GROUP, GROUP)
                before = start + k - 1
                if half == 0 and k == 0:
                    before = jnp.maximum(before, 0)
                before = pl.ds(pl.multiple_of(before * nstate, nstate), nstate)
                for g in range(groups):
                    old = low_state[0, before, lane[g]].astype(F32)
                    if half == 0 and k == 0:
                        old = jnp.where(start == 0, edge[0, 0, :, lane[g]], old)
                    dt_t = dt_rows[k : k + 1, lane[g]]
                    dy_t = dy_rows[k : k + 1, lane[g]]
                    d_state = run[g] + c_t * dy_t
                    low_grad[at, lane[g]] = d_state.astype(BF16)
                    decayed = jnp.exp(dt_t * rate[:, lane[g]]) * d_state
                    run[g] = decayed
                    d_exp = decayed * old
                    acc[g] = acc[g] + d_exp * dt_t
                    term_q = d_exp * rate[:, lane[g]]
                    term_r = d_state * b_t
                    pend_q[g, rows, :] = sum(term_q[s : s + GROUP] for s in range(0, nstate, GROUP))
                    pend_r[g, rows, :] = sum(term_r[s : s + GROUP] for s in range(0, nstate, GROUP))
            fold(pend_q, d_dta, start, half)
            fold(pend_r, d_dtu, start, half)
        return tuple(run), tuple(acc)

    run, acc = lax.fori_loop(
        0,
        count,
        steps,
        (tuple(carry[:, l] for l in lane), tuple(g_rate[:, l] for l in lane)),
    )
    d_b = gather(low_grad, dtu[...].astype(BF16), nstate)
    d_c = gather(low_state.at[0], d_rows.astype(BF16), nstate)
    for g in range(groups):
        carry[:, lane[g]] = run[g]
        g_rate[:, lane[g]] = acc[g]
    d_lin = (d_dtu[...] * u + d_dta[...]) * sigmoid_of_softplus(step)
    d_scan[0] = d_dtu[...] * step + d_rows * skip[...]
    d_low = d_lin.astype(BF16)
    full = jnp.concatenate([contract(dt_w[...], d_low, 1, 1), d_b, d_c], axis=0)
    d_proj[0] = full
    d_proj_low[0] = full.astype(BF16)
    small[:rank, :] += jnp.dot(dt_low, d_low, preferred_element_type=F32)
    row = rank + nstate
    small[row : row + 1, :] += jnp.sum(d_lin, axis=0, keepdims=True)
    small[row + 1 : row + 2, :] += jnp.sum(d_rows * u, axis=0, keepdims=True)

    @pl.when(last)
    def _():
        small[rank : rank + nstate, :] = g_rate[...] * rate


def post_kernel(parts, ids, *refs):
    projs, refs = refs[:parts], refs[parts:]
    xs, refs = refs[:parts], refs[parts:]
    d_scan, d_gate, u_act, summed, inner, inv, w_full, gain, xw_t, conv_w, scan_small = refs[:11]
    refs = refs[11:]
    d_both, small, small_theirs, tiny, own = refs[:5]
    sends, refs = refs[5 : 4 + parts], refs[4 + parts :]
    padded, front = refs
    tokens, chans = d_scan.shape[1:]
    quarter = own.shape[2]
    taps = conv_w.shape[0]
    m = pl.program_id(0)
    base = scan_small.shape[0]

    @pl.when(m == 0)
    def _():
        padded[tokens:, :] = jnp.zeros((GROUP, chans), F32)
        front[:GROUP, :] = jnp.zeros((GROUP, chans), F32)
        small[...] = jnp.zeros(small.shape, F32)
        small[:base, :] = scan_small[...]
        tiny[...] = jnp.zeros(tiny.shape, F32)

    proj = projs[0][0]
    for other in projs[1:]:
        proj = proj + other[0].astype(F32)
    d_proj = proj.astype(BF16)
    count = d_proj.shape[0]
    d_u = d_scan[0] + contract(d_proj, xw_t[...], 0, 0)
    small[base : base + count, :] += jnp.dot(d_proj, u_act[0].astype(BF16), preferred_element_type=F32)
    conv = summed[0]
    sig = sigmoid(conv)
    d_conv = d_u * (sig * (1.0 + conv * (1.0 - sig)))
    padded[:tokens, :] = d_conv
    front[GROUP:, :] = inner[0]
    d_inner = 0.0
    for j in range(taps):
        d_inner = d_inner + conv_w[j : j + 1, :] * padded[pl.ds(taps - 1 - j, tokens), :]
        small[base + count + j : base + count + j + 1, :] += jnp.sum(
            d_conv * front[pl.ds(GROUP - taps + 1 + j, tokens), :], axis=0, keepdims=True
        )
    small[base + count + taps : base + count + taps + 1, :] += jnp.sum(d_conv, axis=0, keepdims=True)

    @pl.when(m == pl.num_programs(0) - 1)
    def _():
        small_theirs[...] = small[:, core_half(ids, chans, 1)]

    d_both[0, :, :chans] = d_inner.astype(BF16)
    d_both[0, :, chans:] = d_gate[0]
    scale = inv[0][:, :1]
    dots = 0.0
    for k in range(parts):
        cols = pl.ds(pl.multiple_of((ids[0] ^ k) * quarter, LANES), quarter)
        d_norm = contract(d_both[0], w_full[cols, :], 1, 1)
        if k == 0:
            own[0] = d_norm
        else:
            sends[k - 1][0] = d_norm.astype(BF16)
        along = d_norm * xs[k][0].astype(F32)
        tiny[0:1, cols] += jnp.sum(along * scale, axis=0, keepdims=True)
        weighted = along * gain[:, cols]
        for c in range(0, quarter, LANES):
            dots = dots + weighted[:, c : c + LANES]
    dots = jnp.sum(jnp.transpose(dots), axis=0, keepdims=True)
    tiny[1:2, pl.ds(pl.multiple_of(m * tokens, LANES), tokens)] = dots


def grad_kernel(chips, ids, rows_of, columns_of, mine, theirs):
    if chips == 0:
        mine[...] = contract(rows_of[...], columns_of[...], 0, 0)
        return
    rows = mine.shape[1]
    for side, out in enumerate((theirs, mine)):
        for j in range(chips):
            index = (ids[1] ^ (2 * j)) ^ (1 - side)
            cols = pl.ds(pl.multiple_of(index * rows, LANES), rows)
            out[j] = contract(rows_of[:, cols], columns_of[...], 0, 0).astype(out.dtype)


def merge_kernel(
    row, ids, mine_in, got_in, mine_out, got_out, small, small_got, tiny, tiny_got, own, part, *sends
):
    rows, wide = mine_in.shape[1:]
    chans = small.shape[1]
    half = chans // 2
    width = tiny.shape[1]
    part[...] = small[:, core_half(ids, chans)] + small_got[...]
    for i in range(width // chans):
        cols = pl.ds(pl.multiple_of((ids[1] & 1) * half, LANES) + i * chans, half)
        part[row + i : row + i + 1, :] = tiny[0:1, cols] + tiny_got[0:1, cols]
    own[:, :wide] = mine_in[0] + got_in[0].astype(F32)
    own[:, wide:] = mine_out[0] + got_out[0].astype(F32)
    pieces = part.shape[0] // STEP
    for j, send in enumerate(sends):
        send[:rows, :wide] = (mine_in[j + 1] + got_in[j + 1].astype(F32)).astype(BF16)
        send[:rows, wide:] = (mine_out[j + 1] + got_out[j + 1].astype(F32)).astype(BF16)
        for c in range(pieces):
            send[rows:, c * half : (c + 1) * half] = part[c * STEP : (c + 1) * STEP, :].astype(BF16)
        send[rows:, pieces * half :] = jnp.zeros((STEP, send.shape[1] - pieces * half), BF16)


def final_kernel(own, part, *refs):
    gots, (grad_in, grad_out, half) = refs[:-3], refs[-3:]
    rows, kinds, chans = grad_in.shape
    wide = kinds * chans
    total = own[...]
    for got in gots:
        total = total + got[:rows, :].astype(F32)
    for k in range(kinds):
        grad_in[:, k, :] = total[:, k * chans : (k + 1) * chans]
    grad_out[...] = jnp.transpose(total[:, wide:])
    lanes = part.shape[1]
    for c in range(part.shape[0] // STEP):
        total = part[c * STEP : (c + 1) * STEP, :]
        for got in gots:
            total = total + got[rows:, c * lanes : (c + 1) * lanes].astype(F32)
        half[c * STEP : (c + 1) * STEP, :] = total


def outputs_kernel(base, ids, half, half_got, gain, x_w, dt_w, dt_b, conv_w, conv_b, a_log, skip, full):
    chans = full.shape[1]
    full[:, core_half(ids, chans)] = half[...]
    full[:, core_half(ids, chans, 1)] = half_got[...]
    rank = dt_w.shape[0]
    nstate = a_log.shape[0]
    count = x_w.shape[0]
    taps = conv_w.shape[0]
    dt_w[...] = full[:rank, :]
    a_log[...] = full[rank : rank + nstate, :]
    dt_b[...] = full[rank + nstate : rank + nstate + 1, :]
    skip[...] = full[rank + nstate + 1 : rank + nstate + 2, :]
    x_w[...] = full[base : base + count, :]
    conv_w[...] = full[base + count : base + count + taps, :]
    conv_b[...] = full[base + count + taps : base + count + taps + 1, :]
    for i in range(gain.shape[1] // chans):
        row = base + count + taps + 1 + i
        gain[:, i * chans : (i + 1) * chans] = full[row : row + 1, :]


def whole(shape):
    return pl.BlockSpec(shape, lambda *_: (0,) * len(shape))


SMEM = pl.BlockSpec(memory_space=pltpu.SMEM)


def params(grid, mib=56):
    return pltpu.CompilerParams(
        dimension_semantics=("arbitrary",) * grid, vmem_limit_bytes=mib * 1024 * 1024
    )


def struct(shape, dtype):
    return jax.ShapeDtypeStruct(shape, dtype)


def run_pre(ids, xs, ws, gain, conv_w, conv_b, xw_t):
    micro, tokens, quarter = xs[0].shape
    width = gain.shape[1]
    chans = conv_w.shape[1]
    count = xw_t.shape[0]
    per = lambda *tail: pl.BlockSpec((1,) + tail, lambda m: (m,) + (0,) * len(tail))
    return pl.pallas_call(
        partial(pre_kernel, len(xs), len(ws)),
        grid=(micro,),
        in_specs=[SMEM]
        + [per(tokens, quarter)] * len(xs)
        + [whole(w.shape) for w in ws]
        + [whole(gain.shape), whole(conv_w.shape), whole(conv_b.shape), whole(xw_t.shape)],
        out_specs=[
            per(tokens, width),
            whole((width, ws[0].shape[1])),
            per(tokens, chans),
            per(tokens, chans),
            per(tokens, chans),
            per(tokens, chans),
            per(tokens, LANES),
            per(count, tokens),
            per(count, tokens),
        ],
        out_shape=[
            struct((micro, tokens, width), BF16),
            struct((width, ws[0].shape[1]), BF16),
            struct((micro, tokens, chans), F32),
            struct((micro, tokens, chans), F32),
            struct((micro, tokens, chans), F32),
            struct((micro, tokens, chans), F32),
            struct((micro, tokens, LANES), F32),
            struct((micro, count, tokens), F32),
            struct((micro, count, tokens), BF16),
        ],
        scratch_shapes=[pltpu.VMEM((tokens + GROUP, chans), F32)],
        compiler_params=params(1),
        name="pre",
    )(ids, *xs, *ws, gain, conv_w, conv_b, xw_t)


def run_fwd(ids, lens, projs, w_full, u_act, gate, dt_w, dt_b, a_log, skip):
    micro, tokens, chans = u_act.shape
    parts = len(projs)
    width = w_full.shape[0]
    quarter = width // parts
    count = projs[0].shape[1]
    nstate = a_log.shape[0]
    span = min(LANES, tokens)
    rows = lambda *tail: pl.BlockSpec((1, span) + tail, lambda m, b: (m, b) + (0,) * len(tail))
    return pl.pallas_call(
        partial(fwd_kernel, parts),
        grid=(micro, tokens // span),
        in_specs=[SMEM, SMEM]
        + [pl.BlockSpec((1, count, span), lambda m, b: (m, 0, b))] * parts
        + [pl.BlockSpec((width, chans), lambda m, b: (0, 2)), rows(chans), rows(chans)]
        + [whole(v.shape) for v in (dt_w, dt_b, a_log, skip)],
        out_specs=[
            rows(chans),
            rows(chans),
            rows(chans),
            pl.BlockSpec((1, 1, nstate, chans), lambda m, b: (m, b, 0, 0)),
            pl.BlockSpec((1, span * nstate, chans), lambda m, b: (m, b, 0)),
            pl.BlockSpec((1, span * nstate, 2 * LANES), lambda m, b: (m, b, 0)),
        ]
        + [rows(quarter)] * parts,
        out_shape=[
            struct((micro, tokens, chans), F32),
            struct((micro, tokens, chans), F32),
            struct((micro, tokens, chans), BF16),
            struct((micro, tokens // span, nstate, chans), F32),
            struct((micro, tokens * nstate, chans), BF16),
            struct((micro, tokens * nstate, 2 * LANES), F32),
            struct((micro, tokens, quarter), F32),
        ]
        + [struct((micro, tokens, quarter), BF16)] * (parts - 1),
        scratch_shapes=[pltpu.VMEM((span, chans), F32)] * 2
        + [pltpu.VMEM((chans // LANES, 2 * GROUP * GROUP, LANES), F32), pltpu.VMEM((nstate, chans), F32)],
        compiler_params=params(2),
        name="scan_forward",
    )(ids, lens, *projs, w_full, u_act, gate, dt_w, dt_b, a_log, skip)


def run_bwd(ids, lens, projs, cots, w_full, u_act, gate, dt, y_rows, edge, low_state, vectors, dt_w, a_log, skip):
    micro, tokens, chans = u_act.shape
    parts = len(projs)
    width = w_full.shape[0]
    quarter = cots[0].shape[2]
    count = projs[0].shape[1]
    nstate = a_log.shape[0]
    rank = dt_w.shape[0]
    span = min(LANES, tokens)
    blocks = tokens // span
    small = STEP * -(-(rank + nstate + 2) // STEP)
    rows = lambda *tail: pl.BlockSpec(
        (1, span) + tail, lambda m, b: (m, blocks - 1 - b) + (0,) * len(tail)
    )
    proj = pl.BlockSpec((1, count, span), lambda m, b: (m, 0, blocks - 1 - b))
    return pl.pallas_call(
        partial(bwd_kernel, parts),
        grid=(micro, blocks),
        in_specs=[SMEM, SMEM]
        + [proj] * parts
        + [rows(quarter)] * parts
        + [pl.BlockSpec((width, chans), lambda m, b: (0, 2)), rows(chans), rows(chans), rows(chans), rows(chans)]
        + [pl.BlockSpec((1, 1, nstate, chans), lambda m, b: (m, blocks - 1 - b, 0, 0))]
        + [pl.BlockSpec((1, span * nstate, chans), lambda m, b: (m, blocks - 1 - b, 0))]
        + [pl.BlockSpec((1, span * nstate, 2 * LANES), lambda m, b: (m, blocks - 1 - b, 0))]
        + [whole(v.shape) for v in (dt_w, a_log, skip)],
        out_specs=[rows(width), proj, proj, rows(chans), rows(chans), whole((small, chans))],
        out_shape=[
            struct((micro, tokens, width), BF16),
            struct((micro, count, tokens), F32),
            struct((micro, count, tokens), BF16),
            struct((micro, tokens, chans), F32),
            struct((micro, tokens, chans), BF16),
            struct((small, chans), F32),
        ],
        scratch_shapes=[pltpu.VMEM((span, chans), F32)] * 4
        + [pltpu.VMEM((chans // LANES, 2 * GROUP * GROUP, LANES), F32)] * 2
        + [pltpu.VMEM((nstate, chans), F32)] * 2
        + [pltpu.VMEM((span * nstate, chans), BF16)],
        compiler_params=params(2),
        name="scan_backward",
    )(ids, lens, *projs, *cots, w_full, u_act, gate, dt, y_rows, edge, low_state, vectors, dt_w, a_log, skip)


def run_post(ids, projs, xs, d_scan, d_gate, u_act, summed, inner, inv, w_full, gain, xw_t, conv_w, scan_small):
    micro, tokens, chans = u_act.shape
    parts = len(projs)
    width = w_full.shape[0]
    quarter = width // parts
    count = projs[0].shape[1]
    taps = conv_w.shape[0]
    small = scan_small.shape[0] + STEP * -(-(count + taps + 1 + width // chans) // STEP)
    lanes = max(width, LANES * -(-micro * tokens // LANES))
    per = lambda *tail: pl.BlockSpec((1,) + tail, lambda m: (m,) + (0,) * len(tail))
    return pl.pallas_call(
        partial(post_kernel, parts),
        grid=(micro,),
        in_specs=[SMEM]
        + [per(count, tokens)] * parts
        + [per(tokens, quarter)] * parts
        + [per(tokens, chans)] * 5
        + [per(tokens, LANES)]
        + [whole((width, 2 * chans))]
        + [whole(v.shape) for v in (gain, xw_t, conv_w, scan_small)],
        out_specs=[
            per(tokens, 2 * chans),
            whole((small, chans)),
            whole((small, chans // 2)),
            whole((GROUP, lanes)),
        ]
        + [per(tokens, quarter)] * parts,
        out_shape=[
            struct((micro, tokens, 2 * chans), BF16),
            struct((small, chans), F32),
            struct((small, chans // 2), F32),
            struct((GROUP, lanes), F32),
            struct((micro, tokens, quarter), F32),
        ]
        + [struct((micro, tokens, quarter), BF16)] * (parts - 1),
        scratch_shapes=[pltpu.VMEM((tokens + GROUP, chans), F32)] * 2,
        compiler_params=params(1),
        name="post",
    )(ids, *projs, *xs, d_scan, d_gate, u_act, summed, inner, inv, w_full, gain, xw_t, conv_w, scan_small)


def run_grad(name, ids, left, right, shape, chips):
    if chips == 0:
        outs = [struct(shape, F32), struct((GROUP, LANES), BF16)]
    else:
        outs = [struct((chips,) + shape, F32), struct((chips,) + shape, BF16)]
    return pl.pallas_call(
        partial(grad_kernel, chips),
        in_specs=[SMEM, pl.BlockSpec(memory_space=pltpu.VMEM), pl.BlockSpec(memory_space=pltpu.VMEM)],
        out_specs=[pl.BlockSpec(memory_space=pltpu.VMEM)] * 2,
        out_shape=outs,
        compiler_params=pltpu.CompilerParams(vmem_limit_bytes=56 * 1024 * 1024),
        name=name,
    )(ids, left, right)


VMEM = pl.BlockSpec(memory_space=pltpu.VMEM)


def run_local(kernel, name, outs, ids, *operands, scratch=()):
    return pl.pallas_call(
        kernel,
        in_specs=([SMEM] if ids is not None else []) + [VMEM] * len(operands),
        out_specs=[VMEM] * len(outs),
        out_shape=outs,
        scratch_shapes=list(scratch),
        compiler_params=pltpu.CompilerParams(vmem_limit_bytes=56 * 1024 * 1024),
        name=name,
    )(*(() if ids is None else (ids,)), *operands)


def after(value, *earlier):
    return lax.optimization_barrier((value, earlier))[0]


def others(value, axis, step=1):
    count = lax.axis_size(axis)
    return [swap(value, axis, mask) for mask in range(step, count, step)]


def with_sibling(blocks):
    return blocks + [swap(block, "dp", 1) for block in blocks]


def sum_all(value):
    core = lax.rem(lax.axis_index("dp"), 2)
    half = value.shape[0] // 2
    halves = value.reshape((2, half) + value.shape[1:])
    mine = lax.dynamic_index_in_dim(halves, core, 0, keepdims=False)
    theirs = lax.dynamic_index_in_dim(halves, 1 - core, 0, keepdims=False)
    total = mine + swap(theirs, "dp", 1)
    for got in others(total, "dp", 2):
        total = total + got
    other = swap(total, "dp", 1)
    first = jnp.where(core == 0, total, other)
    second = jnp.where(core == 0, other, total)
    return jnp.concatenate([first, second], axis=0)


def body(
    tokens,
    lengths,
    norm_gain,
    in_weight,
    x_weight,
    dt_weight,
    dt_bias,
    conv_weight,
    conv_bias,
    a_log,
    skip,
    out_weight,
    cotangent,
):
    micro, seq, quarter = tokens.shape
    chans = in_weight.shape[2]
    width = norm_gain.shape[0]
    dps = lax.axis_size("dp")
    rank = dt_weight.shape[0]
    nstate = a_log.shape[0]
    taps = conv_weight.shape[0]
    count = x_weight.shape[1]
    ids = jnp.stack([lax.axis_index("tensor"), lax.axis_index("dp")]).astype(jnp.int32)
    lens = lengths[:, 0]
    gain = norm_gain[None]
    xw_t = x_weight.T
    in_rows = in_weight.reshape(in_weight.shape[0], 2 * chans)
    by_block = in_rows.shape[0] % LANES == 0
    chips = dps // 2 if by_block else 0
    parts = lax.axis_size("tensor")
    weight = jnp.concatenate([in_rows, out_weight.T], axis=1)

    xs = [tokens] + others(tokens, "tensor")
    if by_block:
        mine = [weight] + [
            swap(after(weight, xs[1]) if mask > 4 else weight, "dp", mask) for mask in range(2, dps, 2)
        ]
        blocks = with_sibling(after(mine, *xs))
    else:
        blocks = [lax.all_gather(weight, "dp", axis=0, tiled=True)]
    normed, w_full, inner, summed, u_act, gate, inv, proj, proj_low = run_pre(
        ids, xs, blocks, gain, conv_weight, conv_bias[None], xw_t
    )
    early = swap(after(cotangent, *xs), "tensor", 2)
    projs = [proj] + others(proj_low, "tensor")
    late = after(cotangent, *projs)
    cots = [cotangent] + [early if mask == 2 else swap(late, "tensor", mask) for mask in range(1, parts)]
    dt, y_rows, gated, edge, low_state, vectors, own_out, *out_terms = run_fwd(
        ids, lens, projs, w_full, u_act, gate, dt_weight, dt_bias[None], a_log, skip[None]
    )
    out_got = [swap(term, "tensor", k + 1) for k, term in enumerate(out_terms)]
    cot_full, d_proj, d_proj_low, d_scan, d_gate, small = run_bwd(
        ids, lens, projs, cots, w_full, u_act, gate, dt, y_rows, edge, low_state, vectors, dt_weight, a_log, skip[None]
    )
    d_projs = [d_proj] + others(after(d_proj_low, *out_got), "tensor")
    branch = own_out
    for term in out_got:
        branch = branch + term.astype(F32)
    mixed = (tokens.astype(F32) + branch).astype(BF16)
    out_mine, out_theirs = run_grad(
        "grad_out",
        ids,
        after(cot_full, d_projs[1]).reshape(micro * seq, width),
        gated.reshape(micro * seq, chans),
        (weight.shape[0] if chips else width, chans),
        chips,
    )
    d_both, small, small_theirs, tiny, own_norm, *norm_terms = run_post(
        ids,
        d_projs,
        xs,
        after(d_scan, out_mine),
        d_gate,
        u_act,
        summed,
        inner,
        inv,
        w_full,
        gain,
        xw_t,
        conv_weight,
        small,
    )
    tiny_got = others(tiny, "tensor")
    norm_got = [swap(term, "tensor", k + 1) for k, term in enumerate(norm_terms[:1] + list(after(norm_terms[1:], *tiny_got)))]
    in_mine, in_theirs = run_grad(
        "grad_in",
        ids,
        after(normed, tiny_got[0]).reshape(micro * seq, width),
        d_both.reshape(micro * seq, 2 * chans),
        (weight.shape[0] if chips else width, 2 * chans),
        chips,
    )
    for got in tiny_got:
        tiny = tiny + got
    base = STEP * -(-(rank + nstate + 2) // STEP)
    row = base + count + taps + 1
    if chips:
        part_shape = struct((small.shape[0], chans // 2), F32)
        own_grad, part, *sends = run_local(
            partial(merge_kernel, row),
            "merge",
            [struct(weight.shape, F32), part_shape]
            + [struct((weight.shape[0] + STEP, weight.shape[1]), BF16)] * (chips - 1),
            ids,
            after(in_mine, norm_got[0]),
            swap(in_theirs, "dp", 1),
            out_mine,
            swap(out_theirs, "dp", 1),
            small,
            swap(small_theirs, "dp", 1),
            tiny,
            swap(tiny, "dp", 1),
        )
        gots = [swap(send, "dp", 2 * (j + 1)) for j, send in enumerate(sends)]
        own_grad = after(own_grad, *norm_got)
        grad_in, grad_out, half = run_local(
            final_kernel,
            "final",
            [struct(in_weight.shape, F32), struct(out_weight.shape, F32), part_shape],
            None,
            own_grad,
            part,
            *gots,
        )
        g_gain, g_x, g_dt, g_dtb, g_conv, g_convb, g_alog, g_skip = run_local(
            partial(outputs_kernel, base),
            "outputs",
            [
                struct((1, width), F32),
                struct((count, chans), F32),
                struct((rank, chans), F32),
                struct((1, chans), F32),
                struct((taps, chans), F32),
                struct((1, chans), F32),
                struct((nstate, chans), F32),
                struct((1, chans), F32),
            ],
            ids,
            half,
            swap(half, "dp", 1),
            scratch=[pltpu.VMEM((small.shape[0], chans), F32)],
        )
        smalls = (g_gain[0], g_x.T, g_dt, g_dtb[0], g_conv, g_convb[0], g_alog, g_skip[0])
    else:
        grad_in = lax.psum_scatter(in_mine, "dp", scatter_dimension=0, tiled=True)
        grad_out = lax.psum_scatter(out_mine, "dp", scatter_dimension=0, tiled=True).T
        small = sum_all(lax.dynamic_update_slice_in_dim(small, tiny[0, :width].reshape(-1, chans), row, 0))
        smalls = (
            small[row : row + width // chans].reshape(width),
            small[base : base + count].T,
            small[:rank],
            small[rank + nstate],
            small[base + count : base + count + taps],
            small[base + count + taps],
            small[rank : rank + nstate],
            small[rank + nstate + 1],
        )
    d_norm = own_norm
    for term in norm_got:
        d_norm = d_norm + term.astype(F32)
    scale = inv[:, :, :1]
    dots = tiny[1, : micro * seq].reshape(micro, seq, 1)
    own_gain = lax.dynamic_slice_in_dim(norm_gain, ids[0] * quarter, quarter, 0)
    d_x = scale * (d_norm * own_gain) - tokens.astype(F32) * (scale * scale * scale * dots / width)
    input_grad = cotangent.astype(F32) + d_x
    return (mixed, input_grad, smalls[0], grad_in.reshape(in_weight.shape)) + smalls[1:] + (grad_out,)


def solution(mesh):
    rows = P(None, "dp", "tensor")
    chans = P(None, "tensor")
    return jax.shard_map(
        body,
        mesh=mesh,
        in_specs=(
            rows,
            P(None, "dp"),
            P(),
            P("dp", None, "tensor"),
            P("tensor", None),
            chans,
            P("tensor"),
            chans,
            P("tensor"),
            chans,
            P("tensor"),
            P("tensor", "dp"),
            rows,
        ),
        out_specs=(
            rows,
            rows,
            P(),
            P("dp", None, "tensor"),
            P("tensor", None),
            chans,
            P("tensor"),
            chans,
            P("tensor"),
            chans,
            P("tensor"),
            P("tensor", "dp"),
        ),
        check_vma=False,
    )
```

time: 245 us -> 189 us (0.77); the launches traced: 242 us -> 188 us
  waiting for transfers between devices: 73.6 us -> 53.4 us
  Pallas kernels: 86.8 us -> 69.6 us
  starting transfers between devices: 64.9 us -> 50.7 us
    ppermute x53 -> x36, waiting for transfers between devices: 73.6 us -> 53.4 us  [swap(): return lax.ppermute(value, axis, [(i, i ^ mask) for i in range(count)])]
    pallas_call x1, Pallas kernels: 41.4 us -> 21.4 us  [run_bwd(): pl.pallas_call(partial(bwd_kernel, parts), grid=(micro, blocks), in_specs...]
    ppermute x53 -> x36, starting transfers between devices: 64.9 us -> 50.7 us  [swap(): return lax.ppermute(value, axis, [(i, i ^ mask) for i in range(count)])]
    pallas_call x3 -> x6, Pallas kernels: 29.3 us -> 32.6 us  [the longest x1 16.2 us: run_fwd(): pl.pallas_call(partial(fwd_kernel, parts), grid=(micro, tokens // span),...]
    unnamed x73 -> x76, local copies, waits for them, and re-layouts: 3.88 us -> 7.18 us
  transfers between devices with their start and end apart: 53 -> 36, of which waited for: 21 -> 12; matrix products, arithmetic and copies ran while one was open for 5% -> 4% of each run, Pallas kernels for 19% -> 26%
where the time goes in v1:
time: 189 us; the launch traced here: 188 us
  Pallas kernels  69.6 us (37%)
  waiting for transfers between devices  53.4 us (28%)
  starting transfers between devices  50.7 us (27%)
  local copies, waits for them, and re-layouts  8.88 us (5%)
  other arithmetic  4.32 us (2%)
    ppermute x36, waiting for transfers between devices, swap(): return lax.ppermute(value, axis, [(i, i ^ mask) for i in range(count)])  53.4 us
    ppermute x36, starting transfers between devices, swap(): return lax.ppermute(value, axis, [(i, i ^ mask) for i in range(count)])  50.7 us
    pallas_call x1, Pallas kernels, run_bwd(): pl.pallas_call(partial(bwd_kernel, parts), grid=(micro, blocks), in_specs...  21.4 us
    pallas_call x1, Pallas kernels, run_fwd(): pl.pallas_call(partial(fwd_kernel, parts), grid=(micro, tokens // span),...  16.2 us
    pallas_call x3, Pallas kernels, run_local(): pl.pallas_call(kernel, in_specs=([SMEM] if ids is not None else []) + [VM...  8.97 us
    pallas_call x1, Pallas kernels, run_post(): pl.pallas_call(partial(post_kernel, parts), grid=(micro,), in_specs=[SMEM...  8.05 us
    pallas_call x1, Pallas kernels, run_pre(): pl.pallas_call(partial(pre_kernel, len(xs), len(ws)), grid=(micro,), in_s...  7.57 us
    pallas_call x2, Pallas kernels, run_grad(): pl.pallas_call(partial(grad_kernel, chips), in_specs=[SMEM, pl.BlockSpec(...  7.4 us
  transfers between devices with their start and end apart: 36, of which 12 were waited for; matrix products, arithmetic and copies ran while one was open for 4% of the time, Pallas kernels for 26%

profile of v1, /device:TPU:0, one launch (start us, length us, event | category | flops | bytes accessed | tf_op | source)
XLA Modules:
  0.0 188.1 jit_solution(7122723784521658035)
XLA Ops:
  0.6 3.1 %collective-permute-start = (bf16[2,256,256]{2,1,0:T(8,128)(2,1)}, bf16[2,256,256]{2,1,0:T(8,128)(2,1)S(1)}, u32[]{:S(2)}, u32[]{:S(2)}) collective-permute-start(bf16[2,256,256]{2,1,0:T(8,128)(2,1)} %refs_4_.3), channel_id=1, source_target_pairs={{0,1},{1,0},{2,3},{3,2},{4,5},{5,4},{6,7},{7,6},{8,9},{9,8},{10,11... | collective-permute-start | bytes 786440 | tf_op jit(solution)/shard_map/ppermute | solution.py:34
  10.3 2.6 %collective-permute-start.5 = (bf16[128,1536]{1,0:T(8,128)(2,1)S(1)}, bf16[128,1536]{1,0:T(8,128)(2,1)S(1)}, u32[]{:S(2)}, u32[]{:S(2)}) collective-permute-start(bf16[128,1536]{1,0:T(8,128)(2,1)S(1)} %pad_maximum_fusion.refs_4_), channel_id=1, source_target_pairs={{0,24},{4,28},{8,16},{12,20},{16,8},{20,12},{24,0},{28,4},{1,25},{... | collective-permute-start | bytes 1179656 | tf_op jit(solution)/shard_map/ppermute | solution.py:34
  12.9 2.6 %collective-permute-start.1 = (bf16[2,256,256]{2,1,0:T(8,128)(2,1)}, bf16[2,256,256]{2,1,0:T(8,128)(2,1)S(1)}, u32[]{:S(2)}, u32[]{:S(2)}) collective-permute-start(bf16[2,256,256]{2,1,0:T(8,128)(2,1)} %refs_4_.3), channel_id=1, source_target_pairs={{0,2},{1,3},{2,0},{3,1},{4,6},{5,7},{6,4},{7,5},{8,10},{9,11},{10,... | collective-permute-start | bytes 786440 | tf_op jit(solution)/shard_map/ppermute | solution.py:34
  16.8 16.5 %collective-permute-done.1.refs_2_.refs_6_ = bf16[2,256,256]{2,1,0:T(8,128)(2,1)S(1)} collective-permute-done((bf16[2,256,256]{2,1,0:T(8,128)(2,1)}, bf16[2,256,256]{2,1,0:T(8,128)(2,1)S(1)}, u32[]{:S(2)}, u32[]{:S(2)}) %collective-permute-start.1) | collective-permute-done | bytes 262176 | tf_op jit(solution)/shard_map/ppermute | solution.py:34
  34.4 7.0 %collective-permute-start.17 = (bf16[2,256,256]{2,1,0:T(8,128)(2,1)}, bf16[2,256,256]{2,1,0:T(8,128)(2,1)S(1)}, u32[]{:S(2)}, u32[]{:S(2)}) collective-permute-start(bf16[2,256,256]{2,1,0:T(8,128)(2,1)} %refs_4_.2), channel_id=1, source_target_pairs={{0,2},{1,3},{2,0},{3,1},{4,6},{5,7},{6,4},{7,5},{8,10},{9,11},{10,... | collective-permute-start | bytes 786440 | tf_op jit(solution)/shard_map/ppermute | solution.py:34
  43.0 7.6 %pre.1 = (bf16[2,256,1024]{2,1,0:T(8,128)(2,1)}, bf16[1024,1536]{1,0:T(8,128)(2,1)}, f32[2,256,512]{2,1,0:T(8,128)}, f32[2,256,512]{2,1,0:T(8,128)}, f32[2,256,5...) custom-call(s32[2]{0:T(128)} %pad_add_fusion.ids, ...), custom_call_target="tpu_custom_call" | custom-call | tf_op jit(solution)/shard_map/pre/pallas_call | solution.py:481
  51.8 3.2 %collective-permute-start.12 = (bf16[2,96,256]{2,1,0:T(8,128)(2,1)}, bf16[2,96,256]{2,1,0:T(8,128)(2,1)S(1)}, u32[]{:S(2)}, u32[]{:S(2)}) collective-permute-start(bf16[2,96,256]{2,1,0:T(8,128)(2,1)} %get-tuple-element.86), channel_id=1, source_target_pairs={{0,3},{1,2},{2,1},{3,0},{4,7},{5,6},{6,5},{7,4},{8,11},{9,10},{10,... | collective-permute-start | bytes 294920 | tf_op jit(solution)/shard_map/ppermute | solution.py:34
  55.0 2.5 %collective-permute-done.10.refs_1_ = bf16[2,96,256]{2,1,0:T(8,128)(2,1)S(1)} collective-permute-done((bf16[2,96,256]{2,1,0:T(8,128)(2,1)}, bf16[2,96,256]{2,1,0:T(8,128)(2,1)S(1)}, u32[]{:S(2)}, u32[]{:S(2)}) %collective-permute-start.10) | collective-permute-done | bytes 98336 | tf_op jit(solution)/shard_map/ppermute | solution.py:34
  57.5 4.0 %collective-permute-done.11.refs_2_ = bf16[2,96,256]{2,1,0:T(8,128)(2,1)S(1)} collective-permute-done((bf16[2,96,256]{2,1,0:T(8,128)(2,1)}, bf16[2,96,256]{2,1,0:T(8,128)(2,1)S(1)}, u32[]{:S(2)}, u32[]{:S(2)}) %collective-permute-start.11) | collective-permute-done | bytes 98336 | tf_op jit(solution)/shard_map/ppermute | solution.py:34
  65.7 16.2 %scan_forward.1 = (f32[2,256,512]{2,1,0:T(8,128)}, f32[2,256,512]{2,1,0:T(8,128)}, bf16[2,256,512]{2,1,0:T(8,128)(2,1)}, f32[2,2,16,512]{3,2,1,0:T(8,128)}, bf16...) custom-call(s32[2]{0:T(128)} %pad_add_fusion.ids, ...), custom_call_target="tpu_custom_call" | custom-call | tf_op jit(solution)/shard_map/scan_forward/pallas_call | solution.py:525
  87.2 21.4 %scan_backward.1 = (bf16[2,256,1024]{2,1,0:T(8,128)(2,1)}, f32[2,96,256]{2,1,0:T(8,128)}, bf16[2,96,256]{2,1,0:T(8,128)(2,1)}, f32[2,256,512]{2,1,0:T(8,128)}, b...) custom-call(s32[2]{0:T(128)} %pad_add_fusion.ids, s32[2]{0:T(128)} %bitcast.36, f32[2,96,256]{2,1,0:T(8,128)} %get-tuple-element.85.refs_0_, ...), custom_call_target="tpu_custom_call" | custom-call | tf_op jit(solution)/shard_map/scan_backward/pallas_call | solution.py:573
  113.6 3.2 %grad_out.1 = (f32[4,128,512]{2,1,0:T(8,128)}, bf16[4,128,512]{2,1,0:T(8,128)(2,1)}) custom-call(s32[2]{0:T(128)} %pad_add_fusion.ids, bf16[512,1024]{1,0:T(8,128)(2,1)} %bitcast.23, bf16[512,512]{1,0:T(8,128)(2,1)} %bitcast.24), custom_call_target="tpu_custom_call" | custom-call | tf_op jit(solution)/shard_map/grad_out/pallas_call | solution.py:648
  118.8 8.1 %post.1 = (bf16[2,256,1024]{2,1,0:T(8,128)(2,1)}, f32[240,512]{1,0:T(8,128)}, f32[240,256]{1,0:T(8,128)}, f32[8,1024]{1,0:T(8,128)}, f32[2,256,256]{2,1,0:T(8,12...) custom-call(s32[2]{0:T(128)} %pad_add_fusion.ids, ...), custom_call_target="tpu_custom_call" | custom-call | tf_op jit(solution)/shard_map/post/pallas_call | solution.py:612
  128.5 2.5 %collective-permute-done.23 = f32[8,1024]{1,0:T(8,128)S(1)} collective-permute-done((f32[8,1024]{1,0:T(8,128)}, f32[8,1024]{1,0:T(8,128)S(1)}, u32[]{:S(2)}, u32[]{:S(2)}) %collective-permute-start.23) | collective-permute-done | bytes 32800 | tf_op jit(solution)/shard_map/ppermute | solution.py:34
  131.0 4.2 %grad_in.1 = (f32[4,128,1024]{2,1,0:T(8,128)}, bf16[4,128,1024]{2,1,0:T(8,128)(2,1)}) custom-call(s32[2]{0:T(128)} %pad_add_fusion.ids, bf16[512,1024]{1,0:T(8,128)(2,1)} %bitcast.20, bf16[512,1024]{1,0:T(8,128)(2,1)} %bitcast.21), custom_call_target="tpu_custom_call" | custom-call | tf_op jit(solution)/shard_map/grad_in/pallas_call | solution.py:648
  137.3 2.4 %collective-permute-start.25 = (f32[8,1024]{1,0:T(8,128)}, f32[8,1024]{1,0:T(8,128)S(1)}, u32[]{:S(2)}, u32[]{:S(2)}) collective-permute-start(f32[8,1024]{1,0:T(8,128)} %get-tuple-element.119), channel_id=1, source_target_pairs={{0,3},{1,2},{2,1},{3,0},{4,7},{5,6},{6,5},{7,4},{8,11},{9,10},{10,... | collective-permute-start | bytes 98312 | tf_op jit(solution)/shard_map/ppermute | solution.py:34
  141.2 2.4 %collective-permute-done.25 = f32[8,1024]{1,0:T(8,128)S(1)} collective-permute-done((f32[8,1024]{1,0:T(8,128)}, f32[8,1024]{1,0:T(8,128)S(1)}, u32[]{:S(2)}, u32[]{:S(2)}) %collective-permute-start.25) | collective-permute-done | bytes 32800 | tf_op jit(solution)/shard_map/ppermute | solution.py:34
  144.4 3.7 %collective-permute-done.22 = bf16[2,256,256]{2,1,0:T(8,128)(2,1)S(1)} collective-permute-done((bf16[2,256,256]{2,1,0:T(8,128)(2,1)}, bf16[2,256,256]{2,1,0:T(8,128)(2,1)S(1)}, u32[]{:S(2)}, u32[]{:S(2)}) %collective-permute-start.22) | collective-permute-done | bytes 262176 | tf_op jit(solution)/shard_map/ppermute | solution.py:34
  149.4 4.1 %merge.1 = (f32[128,1536]{1,0:T(8,128)}, f32[240,256]{1,0:T(8,128)}, bf16[176,1536]{1,0:T(8,128)(2,1)}, bf16[176,1536]{1,0:T(8,128)(2,1)}, bf16[176,1536]{1,0:T(8,128)(2,1)}) custom-call(s32[2]{0:T(128)} %pad_add_fusion.ids, f32[4,128,1024]{2,1,0:T(8,128)} %get-tuple-element.126.mine_in, bf16[4,128,1024]{2,1,0:T(8,128)(2,1)} %copy-done.7, ...), custom_call_target="tpu_custom_call" | custom-call | tf_op jit(solution)/shard_map/merge/pallas_call | solution.py:662
  154.6 2.5 %collective-permute-start.34 = (bf16[176,1536]{1,0:T(8,128)(2,1)}, bf16[176,1536]{1,0:T(8,128)(2,1)S(1)}, u32[]{:S(2)}, u32[]{:S(2)}) collective-permute-start(bf16[176,1536]{1,0:T(8,128)(2,1)} %get-tuple-element.136), channel_id=1, source_target_pairs={{0,24},{4,28},{8,16},{12,20},{16,8},{20,12},{24,0},{28,4},{1,25},{... | collective-permute-start | bytes 1622024 | tf_op jit(solution)/shard_map/ppermute | solution.py:34
  161.8 14.0 %collective-permute-done.26 = bf16[2,256,256]{2,1,0:T(8,128)(2,1)} collective-permute-done((bf16[2,256,256]{2,1,0:T(8,128)(2,1)}, bf16[2,256,256]{2,1,0:T(8,128)(2,1)}, u32[]{:S(2)}, u32[]{:S(2)}) %collective-permute-start.26) | collective-permute-done | bytes 262176 | tf_op jit(solution)/shard_map/ppermute | solution.py:34
  175.8 3.1 %collective-permute-done.33.refs_1_ = bf16[176,1536]{1,0:T(8,128)(2,1)S(1)} collective-permute-done((bf16[176,1536]{1,0:T(8,128)(2,1)}, bf16[176,1536]{1,0:T(8,128)(2,1)S(1)}, u32[]{:S(2)}, u32[]{:S(2)}) %collective-permute-start.33) | collective-permute-done | bytes 540704 | tf_op jit(solution)/shard_map/ppermute | solution.py:34
  179.8 3.0 %final.1 = (f32[128,2,512]{2,1,0:T(2,128)}, f32[512,128]{1,0:T(8,128)}, f32[240,256]{1,0:T(8,128)}) custom-call(f32[128,1536]{1,0:T(8,128)} %get-tuple-element.132.own, f32[240,256]{1,0:T(8,128)} %get-tuple-element.133.part, bf16[176,1536]{1,0:T(8,128)(2,1)} %copy-done.8, bf16[176,1536]{1,0:T(8,128)(2,1)} %copy-done.9, bf16[176,1536]{1,0:T(8,128)(2,1)} %copy-done.10), custom_call_target="tpu_custom_call" | custom-call | tf_op jit(solution)/shard_map/final/pallas_call | solution.py:662
  182.8 2.7 %fusion.2 = (f32[2,256,256]{2,1,0:T(8,128)}, bf16[2,256,256]{2,1,0:T(8,128)(2,1)}) fusion(bf16[2,256,256]{2,1,0:T(8,128)(2,1)S(1)} %copy-done, bf16[2,256,256]{2,1,0:T(8,128)(2,1)} %collective-permute-done.27, bf16[2,256,256]{2,1,0:T(8,128)(2,1)} %collective-permute-done.26, f32[2,256,256]{2,1,0:T(8,128)} %get-tuple-element.115, ...), kind=kLoop, calls=%fused_computation.4 | loop fusion | flops 2752512 | bytes 3937280 | tf_op jit(solution)/shard_map/add | solution.py:867
  (141 shorter events, 44.4 us)
Async XLA Ops:
  0.6 9.6 %collective-permute-start = (bf16[2,256,256]{2,1,0:T(8,128)(2,1)}, bf16[2,256,256]{2,1,0:T(8,128)(2,1)S(1)}, u32[]{:S(2)}, u32[]{:S(2)}) collective-permute-start(bf16[2,256,256]{2,1,0:T(8,128)(2,1)} %refs_4_.3), channel_id=1, source_target_pairs={{0,1},{1,0},{2,3},{3,2},{4,5},{5,4},{6,7},{7,6},{8,9},{9,8},{10,11... | collective-permute-start | bytes 786440 | tf_op jit(solution)/shard_map/ppermute | solution.py:34
  5.8 27.5 %collective-permute-start.3 = (bf16[128,1536]{1,0:T(8,128)(2,1)S(1)}, bf16[128,1536]{1,0:T(8,128)(2,1)S(1)}, u32[]{:S(2)}, u32[]{:S(2)}) collective-permute-start(bf16[128,1536]{1,0:T(8,128)(2,1)S(1)} %pad_maximum_fusion.refs_4_), channel_id=1, source_target_pairs={{0,8},{4,12},{8,0},{12,4},{16,24},{20,28},{24,16},{28,20},{1,9},{5... | collective-permute-start | bytes 1179656 | tf_op jit(solution)/shard_map/ppermute | solution.py:34
  7.3 26.0 %collective-permute-start.4 = (bf16[128,1536]{1,0:T(8,128)(2,1)S(1)}, bf16[128,1536]{1,0:T(8,128)(2,1)S(1)}, u32[]{:S(2)}, u32[]{:S(2)}) collective-permute-start(bf16[128,1536]{1,0:T(8,128)(2,1)S(1)} %pad_maximum_fusion.refs_4_), channel_id=1, source_target_pairs={{0,16},{4,20},{8,24},{12,28},{16,0},{20,4},{24,8},{28,12},{1,17},{... | collective-permute-start | bytes 1179656 | tf_op jit(solution)/shard_map/ppermute | solution.py:34
  10.3 23.1 %collective-permute-start.5 = (bf16[128,1536]{1,0:T(8,128)(2,1)S(1)}, bf16[128,1536]{1,0:T(8,128)(2,1)S(1)}, u32[]{:S(2)}, u32[]{:S(2)}) collective-permute-start(bf16[128,1536]{1,0:T(8,128)(2,1)S(1)} %pad_maximum_fusion.refs_4_), channel_id=1, source_target_pairs={{0,24},{4,28},{8,16},{12,20},{16,8},{20,12},{24,0},{28,4},{1,25},{... | collective-permute-start | bytes 1179656 | tf_op jit(solution)/shard_map/ppermute | solution.py:34
  12.9 20.4 %collective-permute-start.1 = (bf16[2,256,256]{2,1,0:T(8,128)(2,1)}, bf16[2,256,256]{2,1,0:T(8,128)(2,1)S(1)}, u32[]{:S(2)}, u32[]{:S(2)}) collective-permute-start(bf16[2,256,256]{2,1,0:T(8,128)(2,1)} %refs_4_.3), channel_id=1, source_target_pairs={{0,2},{1,3},{2,0},{3,1},{4,6},{5,7},{6,4},{7,5},{8,10},{9,11},{10,... | collective-permute-start | bytes 786440 | tf_op jit(solution)/shard_map/ppermute | solution.py:34
  15.5 17.8 %collective-permute-start.2 = (bf16[2,256,256]{2,1,0:T(8,128)(2,1)}, bf16[2,256,256]{2,1,0:T(8,128)(2,1)S(1)}, u32[]{:S(2)}, u32[]{:S(2)}) collective-permute-start(bf16[2,256,256]{2,1,0:T(8,128)(2,1)} %refs_4_.3), channel_id=1, source_target_pairs={{0,3},{1,2},{2,1},{3,0},{4,7},{5,6},{6,5},{7,4},{8,11},{9,10},{10,... | collective-permute-start | bytes 786440 | tf_op jit(solution)/shard_map/ppermute | solution.py:34
  33.3 8.7 %collective-permute-start.6 = (bf16[128,1536]{1,0:T(8,128)(2,1)S(1)}, bf16[128,1536]{1,0:T(8,128)(2,1)S(1)}, u32[]{:S(2)}, u32[]{:S(2)}) collective-permute-start(bf16[128,1536]{1,0:T(8,128)(2,1)S(1)} %pad_maximum_fusion.refs_4_), channel_id=1, source_target_pairs={{0,4},{4,0},{8,12},{12,8},{16,20},{20,16},{24,28},{28,24},{1,5},{5... | collective-permute-start | bytes 1179656 | tf_op jit(solution)/shard_map/ppermute | solution.py:34
  33.4 8.7 %collective-permute-start.7 = (bf16[128,1536]{1,0:T(8,128)(2,1)S(1)}, bf16[128,1536]{1,0:T(8,128)(2,1)S(1)}, u32[]{:S(2)}, u32[]{:S(2)}) collective-permute-start(bf16[128,1536]{1,0:T(8,128)(2,1)S(1)} %collective-permute-done.3.refs_5_), channel_id=1, source_target_pairs={{0,4},{4,0},{8,12},{12,8},{16,20},{20,16},{24,28},{28,24},{1,5},{5... | collective-permute-start | bytes 1179656 | tf_op jit(solution)/shard_map/ppermute | solution.py:34
  34.4 49.6 %collective-permute-start.17 = (bf16[2,256,256]{2,1,0:T(8,128)(2,1)}, bf16[2,256,256]{2,1,0:T(8,128)(2,1)S(1)}, u32[]{:S(2)}, u32[]{:S(2)}) collective-permute-start(bf16[2,256,256]{2,1,0:T(8,128)(2,1)} %refs_4_.2), channel_id=1, source_target_pairs={{0,2},{1,3},{2,0},{3,1},{4,6},{5,7},{6,4},{7,5},{8,10},{9,11},{10,... | collective-permute-start | bytes 786440 | tf_op jit(solution)/shard_map/ppermute | solution.py:34
  50.6 10.9 %collective-permute-start.11 = (bf16[2,96,256]{2,1,0:T(8,128)(2,1)}, bf16[2,96,256]{2,1,0:T(8,128)(2,1)S(1)}, u32[]{:S(2)}, u32[]{:S(2)}) collective-permute-start(bf16[2,96,256]{2,1,0:T(8,128)(2,1)} %get-tuple-element.86), channel_id=1, source_target_pairs={{0,2},{1,3},{2,0},{3,1},{4,6},{5,7},{6,4},{7,5},{8,10},{9,11},{10,... | collective-permute-start | bytes 294920 | tf_op jit(solution)/shard_map/ppermute | solution.py:34
  51.8 9.8 %collective-permute-start.12 = (bf16[2,96,256]{2,1,0:T(8,128)(2,1)}, bf16[2,96,256]{2,1,0:T(8,128)(2,1)S(1)}, u32[]{:S(2)}, u32[]{:S(2)}) collective-permute-start(bf16[2,96,256]{2,1,0:T(8,128)(2,1)} %get-tuple-element.86), channel_id=1, source_target_pairs={{0,3},{1,2},{2,1},{3,0},{4,7},{5,6},{6,5},{7,4},{8,11},{9,10},{10,... | collective-permute-start | bytes 294920 | tf_op jit(solution)/shard_map/ppermute | solution.py:34
  61.6 24.8 %collective-permute-start.16 = (bf16[2,256,256]{2,1,0:T(8,128)(2,1)}, bf16[2,256,256]{2,1,0:T(8,128)(2,1)S(1)}, u32[]{:S(2)}, u32[]{:S(2)}) collective-permute-start(bf16[2,256,256]{2,1,0:T(8,128)(2,1)} %refs_4_.2), channel_id=1, source_target_pairs={{0,1},{1,0},{2,3},{3,2},{4,5},{5,4},{6,7},{7,6},{8,9},{9,8},{10,11... | collective-permute-start | bytes 786440 | tf_op jit(solution)/shard_map/ppermute | solution.py:34
  63.3 23.1 %collective-permute-start.18 = (bf16[2,256,256]{2,1,0:T(8,128)(2,1)}, bf16[2,256,256]{2,1,0:T(8,128)(2,1)S(1)}, u32[]{:S(2)}, u32[]{:S(2)}) collective-permute-start(bf16[2,256,256]{2,1,0:T(8,128)(2,1)} %refs_4_.2), channel_id=1, source_target_pairs={{0,3},{1,2},{2,1},{3,0},{4,7},{5,6},{6,5},{7,4},{8,11},{9,10},{10,... | collective-permute-start | bytes 786440 | tf_op jit(solution)/shard_map/ppermute | solution.py:34
  81.9 26.7 %collective-permute-start.13 = (bf16[2,256,256]{2,1,0:T(8,128)(2,1)}, bf16[2,256,256]{2,1,0:T(8,128)(2,1)S(1)}, u32[]{:S(2)}, u32[]{:S(2)}) collective-permute-start(bf16[2,256,256]{2,1,0:T(8,128)(2,1)} %get-tuple-element.91), channel_id=1, source_target_pairs={{0,1},{1,0},{2,3},{3,2},{4,5},{5,4},{6,7},{7,6},{8,9},{9,8},{10,11... | collective-permute-start | bytes 786440 | tf_op jit(solution)/shard_map/ppermute | solution.py:34
  82.0 26.7 %collective-permute-start.14 = (bf16[2,256,256]{2,1,0:T(8,128)(2,1)}, bf16[2,256,256]{2,1,0:T(8,128)(2,1)S(1)}, u32[]{:S(2)}, u32[]{:S(2)}) collective-permute-start(bf16[2,256,256]{2,1,0:T(8,128)(2,1)} %get-tuple-element.92), channel_id=1, source_target_pairs={{0,2},{1,3},{2,0},{3,1},{4,6},{5,7},{6,4},{7,5},{8,10},{9,11},{10,... | collective-permute-start | bytes 786440 | tf_op jit(solution)/shard_map/ppermute | solution.py:34
  84.0 24.7 %collective-permute-start.15 = (bf16[2,256,256]{2,1,0:T(8,128)(2,1)}, bf16[2,256,256]{2,1,0:T(8,128)(2,1)S(1)}, u32[]{:S(2)}, u32[]{:S(2)}) collective-permute-start(bf16[2,256,256]{2,1,0:T(8,128)(2,1)} %get-tuple-element.93), channel_id=1, source_target_pairs={{0,3},{1,2},{2,1},{3,0},{4,7},{5,6},{6,5},{7,4},{8,11},{9,10},{10,... | collective-permute-start | bytes 786440 | tf_op jit(solution)/shard_map/ppermute | solution.py:34
  108.8 9.3 %collective-permute-start.20 = (bf16[2,96,256]{2,1,0:T(8,128)(2,1)}, bf16[2,96,256]{2,1,0:T(8,128)(2,1)S(1)}, u32[]{:S(2)}, u32[]{:S(2)}) collective-permute-start(bf16[2,96,256]{2,1,0:T(8,128)(2,1)} %get-tuple-element.104), channel_id=1, source_target_pairs={{0,2},{1,3},{2,0},{3,1},{4,6},{5,7},{6,4},{7,5},{8,10},{9,11},{10,... | collective-permute-start | bytes 294920 | tf_op jit(solution)/shard_map/ppermute | solution.py:34
  135.2 13.0 %collective-permute-start.28 = (bf16[4,128,1024]{2,1,0:T(8,128)(2,1)}, bf16[4,128,1024]{2,1,0:T(8,128)(2,1)S(1)}, u32[]{:S(2)}, u32[]{:S(2)}) collective-permute-start(bf16[4,128,1024]{2,1,0:T(8,128)(2,1)} %get-tuple-element.127), channel_id=1, source_target_pairs={{0,4},{4,0},{8,12},{12,8},{16,20},{20,16},{24,28},{28,24},{1,5},{5... | collective-permute-start | bytes 3145736 | tf_op jit(solution)/shard_map/ppermute | solution.py:34
  135.3 12.9 %collective-permute-start.29 = (bf16[4,128,512]{2,1,0:T(8,128)(2,1)S(1)}, bf16[4,128,512]{2,1,0:T(8,128)(2,1)S(1)}, u32[]{:S(2)}, u32[]{:S(2)}) collective-permute-start(bf16[4,128,512]{2,1,0:T(8,128)(2,1)S(1)} %copy-done.36), channel_id=1, source_target_pairs={{0,4},{4,0},{8,12},{12,8},{16,20},{20,16},{24,28},{28,24},{1,5},{5... | collective-permute-start | bytes 1572872 | tf_op jit(solution)/shard_map/ppermute | solution.py:34
  153.6 22.2 %collective-permute-start.32 = (bf16[176,1536]{1,0:T(8,128)(2,1)}, bf16[176,1536]{1,0:T(8,128)(2,1)S(1)}, u32[]{:S(2)}, u32[]{:S(2)}) collective-permute-start(bf16[176,1536]{1,0:T(8,128)(2,1)} %get-tuple-element.134), channel_id=1, source_target_pairs={{0,8},{4,12},{8,0},{12,4},{16,24},{20,28},{24,16},{28,20},{1,9},{5... | collective-permute-start | bytes 1622024 | tf_op jit(solution)/shard_map/ppermute | solution.py:34
  154.1 24.8 %collective-permute-start.33 = (bf16[176,1536]{1,0:T(8,128)(2,1)}, bf16[176,1536]{1,0:T(8,128)(2,1)S(1)}, u32[]{:S(2)}, u32[]{:S(2)}) collective-permute-start(bf16[176,1536]{1,0:T(8,128)(2,1)} %get-tuple-element.135), channel_id=1, source_target_pairs={{0,16},{4,20},{8,24},{12,28},{16,0},{20,4},{24,8},{28,12},{1,17},{... | collective-permute-start | bytes 1622024 | tf_op jit(solution)/shard_map/ppermute | solution.py:34
  154.6 24.3 %collective-permute-start.34 = (bf16[176,1536]{1,0:T(8,128)(2,1)}, bf16[176,1536]{1,0:T(8,128)(2,1)S(1)}, u32[]{:S(2)}, u32[]{:S(2)}) collective-permute-start(bf16[176,1536]{1,0:T(8,128)(2,1)} %get-tuple-element.136), channel_id=1, source_target_pairs={{0,24},{4,28},{8,16},{12,20},{16,8},{20,12},{24,0},{28,4},{1,25},{... | collective-permute-start | bytes 1622024 | tf_op jit(solution)/shard_map/ppermute | solution.py:34
  157.0 18.7 %collective-permute-start.26 = (bf16[2,256,256]{2,1,0:T(8,128)(2,1)}, bf16[2,256,256]{2,1,0:T(8,128)(2,1)}, u32[]{:S(2)}, u32[]{:S(2)}) collective-permute-start(bf16[2,256,256]{2,1,0:T(8,128)(2,1)} %get-tuple-element.120), channel_id=1, source_target_pairs={{0,2},{1,3},{2,0},{3,1},{4,6},{5,7},{6,4},{7,5},{8,10},{9,11},{10,... | collective-permute-start | bytes 786440 | tf_op jit(solution)/shard_map/ppermute | solution.py:34
  157.6 18.2 %collective-permute-start.27 = (bf16[2,256,256]{2,1,0:T(8,128)(2,1)}, bf16[2,256,256]{2,1,0:T(8,128)(2,1)}, u32[]{:S(2)}, u32[]{:S(2)}) collective-permute-start(bf16[2,256,256]{2,1,0:T(8,128)(2,1)} %get-tuple-element.121), channel_id=1, source_target_pairs={{0,3},{1,2},{2,1},{3,0},{4,7},{5,6},{6,5},{7,4},{8,11},{9,10},{10,... | collective-permute-start | bytes 786440 | tf_op jit(solution)/shard_map/ppermute | solution.py:34
  (49 other events, 596.0 us)

commit v2 on v1

--- a/solution.py
+++ b/solution.py
@@ -12,7 +12,8 @@
 BF16 = jnp.bfloat16
 GROUP = 8
 LANES = 128
-STEP = 48
+SCAN_STEP = 32
+POST_STEP = 64
 
 
 def contract(left, right, left_dim, right_dim):
@@ -211,8 +212,8 @@
     cots, refs = refs[:parts], refs[parts:]
     w_full, u_act, gate, dt, y_rows, edge, low_state, vectors, dt_w, a_log, skip = refs[:11]
     refs = refs[11:]
-    cot_full, d_proj, d_proj_low, d_scan, d_gate, small = refs[:6]
-    dtu, d_y, d_dtu, d_dta, pend_q, pend_r, carry, g_rate, low_grad = refs[6:]
+    cot_full, d_proj, d_proj_low, d_scan, d_gate, small, small_theirs = refs[:7]
+    dtu, d_y, d_dtu, d_dta, pend_q, pend_r, carry, g_rate, low_grad = refs[7:]
     span, chans = dtu.shape
     nstate = a_log.shape[0]
     rank = dt_w.shape[0]
@@ -315,28 +316,27 @@
     @pl.when(last)
     def _():
         small[rank : rank + nstate, :] = g_rate[...] * rate
+        small_theirs[...] = small[:, core_half(ids, chans, 1)]
 
 
 def post_kernel(parts, ids, *refs):
     projs, refs = refs[:parts], refs[parts:]
     xs, refs = refs[:parts], refs[parts:]
-    d_scan, d_gate, u_act, summed, inner, inv, w_full, gain, xw_t, conv_w, scan_small = refs[:11]
-    refs = refs[11:]
-    d_both, small, small_theirs, tiny, own = refs[:5]
+    d_scan, d_gate, u_act, summed, inner, inv, w_full, gain, xw_t, conv_w = refs[:10]
+    refs = refs[10:]
+    d_inner_low, small, small_theirs, tiny, own = refs[:5]
     sends, refs = refs[5 : 4 + parts], refs[4 + parts :]
-    padded, front = refs
+    padded, front, d_both = refs
     tokens, chans = d_scan.shape[1:]
     quarter = own.shape[2]
     taps = conv_w.shape[0]
     m = pl.program_id(0)
-    base = scan_small.shape[0]
 
     @pl.when(m == 0)
     def _():
         padded[tokens:, :] = jnp.zeros((GROUP, chans), F32)
         front[:GROUP, :] = jnp.zeros((GROUP, chans), F32)
         small[...] = jnp.zeros(small.shape, F32)
-        small[:base, :] = scan_small[...]
         tiny[...] = jnp.zeros(tiny.shape, F32)
 
     proj = projs[0][0]
@@ -345,7 +345,7 @@
     d_proj = proj.astype(BF16)
     count = d_proj.shape[0]
     d_u = d_scan[0] + contract(d_proj, xw_t[...], 0, 0)
-    small[base : base + count, :] += jnp.dot(d_proj, u_act[0].astype(BF16), preferred_element_type=F32)
+    small[:count, :] += jnp.dot(d_proj, u_act[0].astype(BF16), preferred_element_type=F32)
     conv = summed[0]
     sig = sigmoid(conv)
     d_conv = d_u * (sig * (1.0 + conv * (1.0 - sig)))
@@ -354,22 +354,23 @@
     d_inner = 0.0
     for j in range(taps):
         d_inner = d_inner + conv_w[j : j + 1, :] * padded[pl.ds(taps - 1 - j, tokens), :]
-        small[base + count + j : base + count + j + 1, :] += jnp.sum(
+        small[count + j : count + j + 1, :] += jnp.sum(
             d_conv * front[pl.ds(GROUP - taps + 1 + j, tokens), :], axis=0, keepdims=True
         )
-    small[base + count + taps : base + count + taps + 1, :] += jnp.sum(d_conv, axis=0, keepdims=True)
+    small[count + taps : count + taps + 1, :] += jnp.sum(d_conv, axis=0, keepdims=True)
 
     @pl.when(m == pl.num_programs(0) - 1)
     def _():
         small_theirs[...] = small[:, core_half(ids, chans, 1)]
 
-    d_both[0, :, :chans] = d_inner.astype(BF16)
-    d_both[0, :, chans:] = d_gate[0]
+    d_inner_low[0] = d_inner.astype(BF16)
+    d_both[:, :chans] = d_inner.astype(BF16)
+    d_both[:, chans:] = d_gate[0]
     scale = inv[0][:, :1]
     dots = 0.0
     for k in range(parts):
         cols = pl.ds(pl.multiple_of((ids[0] ^ k) * quarter, LANES), quarter)
-        d_norm = contract(d_both[0], w_full[cols, :], 1, 1)
+        d_norm = contract(d_both[...], w_full[cols, :], 1, 1)
         if k == 0:
             own[0] = d_norm
         else:
@@ -383,76 +384,91 @@
     tiny[1:2, pl.ds(pl.multiple_of(m * tokens, LANES), tokens)] = dots
 
 
-def grad_kernel(chips, ids, rows_of, columns_of, mine, theirs):
-    if chips == 0:
-        mine[...] = contract(rows_of[...], columns_of[...], 0, 0)
-        return
+def grad_kernel(chips, pairs, ids, *refs):
+    lefts, rights, (mine, theirs) = refs[:pairs], refs[pairs : 2 * pairs], refs[2 * pairs :]
+    wide = rights[0].shape[1]
+    for p, (left, right) in enumerate(zip(lefts, rights)):
+        at = slice(p * wide, (p + 1) * wide)
+        if chips == 0:
+            mine[:, at] = contract(left[...], right[...], 0, 0)
+            continue
+        rows = mine.shape[1]
+        for side, out in enumerate((theirs, mine)):
+            for j in range(chips):
+                index = (ids[1] ^ (2 * j)) ^ (1 - side)
+                cols = pl.ds(pl.multiple_of(index * rows, LANES), rows)
+                out[j, :, at] = contract(left[:, cols], right[...], 0, 0).astype(out.dtype)
+
+
+def merge_kernel(step, row, ids, mine, got, small, small_got, *refs):
+    tinies, (own, part, *sends) = (refs[:2], refs[2:]) if row else ((), refs)
     rows = mine.shape[1]
-    for side, out in enumerate((theirs, mine)):
-        for j in range(chips):
-            index = (ids[1] ^ (2 * j)) ^ (1 - side)
-            cols = pl.ds(pl.multiple_of(index * rows, LANES), rows)
-            out[j] = contract(rows_of[:, cols], columns_of[...], 0, 0).astype(out.dtype)
-
-
-def merge_kernel(
-    row, ids, mine_in, got_in, mine_out, got_out, small, small_got, tiny, tiny_got, own, part, *sends
-):
-    rows, wide = mine_in.shape[1:]
     chans = small.shape[1]
     half = chans // 2
-    width = tiny.shape[1]
     part[...] = small[:, core_half(ids, chans)] + small_got[...]
-    for i in range(width // chans):
-        cols = pl.ds(pl.multiple_of((ids[1] & 1) * half, LANES) + i * chans, half)
-        part[row + i : row + i + 1, :] = tiny[0:1, cols] + tiny_got[0:1, cols]
-    own[:, :wide] = mine_in[0] + got_in[0].astype(F32)
-    own[:, wide:] = mine_out[0] + got_out[0].astype(F32)
-    pieces = part.shape[0] // STEP
+    if row:
+        for i in range(tinies[0].shape[1] // chans):
+            cols = pl.ds(pl.multiple_of((ids[1] & 1) * half, LANES) + i * chans, half)
+            part[row + i : row + i + 1, :] = tinies[0][0:1, cols] + tinies[1][0:1, cols]
+    own[...] = mine[0] + got[0].astype(F32)
+    pieces = part.shape[0] // step
     for j, send in enumerate(sends):
-        send[:rows, :wide] = (mine_in[j + 1] + got_in[j + 1].astype(F32)).astype(BF16)
-        send[:rows, wide:] = (mine_out[j + 1] + got_out[j + 1].astype(F32)).astype(BF16)
+        send[:rows, :] = (mine[j + 1] + got[j + 1].astype(F32)).astype(BF16)
         for c in range(pieces):
-            send[rows:, c * half : (c + 1) * half] = part[c * STEP : (c + 1) * STEP, :].astype(BF16)
-        send[rows:, pieces * half :] = jnp.zeros((STEP, send.shape[1] - pieces * half), BF16)
-
-
-def final_kernel(own, part, *refs):
-    gots, (grad_in, grad_out, half) = refs[:-3], refs[-3:]
-    rows, kinds, chans = grad_in.shape
-    wide = kinds * chans
+            send[rows:, c * half : (c + 1) * half] = part[c * step : (c + 1) * step, :].astype(BF16)
+        if pieces * half < send.shape[1]:
+            send[rows:, pieces * half :] = jnp.zeros((step, send.shape[1] - pieces * half), BF16)
+
+
+def add_received(step, own, part, gots, half):
+    rows = own.shape[0]
     total = own[...]
     for got in gots:
         total = total + got[:rows, :].astype(F32)
-    for k in range(kinds):
-        grad_in[:, k, :] = total[:, k * chans : (k + 1) * chans]
+    lanes = part.shape[1]
+    for c in range(part.shape[0] // step):
+        piece = part[c * step : (c + 1) * step, :]
+        for got in gots:
+            piece = piece + got[rows:, c * lanes : (c + 1) * lanes].astype(F32)
+        half[c * step : (c + 1) * step, :] = piece
+    return total
+
+
+def final_early_kernel(step, own, part, *refs):
+    gots, (grad_gate, grad_out, half) = refs[:-3], refs[-3:]
+    total = add_received(step, own, part, gots, half)
+    wide = grad_gate.shape[1]
+    grad_gate[...] = total[:, :wide]
     grad_out[...] = jnp.transpose(total[:, wide:])
-    lanes = part.shape[1]
-    for c in range(part.shape[0] // STEP):
-        total = part[c * STEP : (c + 1) * STEP, :]
-        for got in gots:
-            total = total + got[rows:, c * lanes : (c + 1) * lanes].astype(F32)
-        half[c * STEP : (c + 1) * STEP, :] = total
-
-
-def outputs_kernel(base, ids, half, half_got, gain, x_w, dt_w, dt_b, conv_w, conv_b, a_log, skip, full):
-    chans = full.shape[1]
-    full[:, core_half(ids, chans)] = half[...]
-    full[:, core_half(ids, chans, 1)] = half_got[...]
+
+
+def final_late_kernel(step, own, part, grad_gate, *refs):
+    gots, (grad_in, half) = refs[:-2], refs[-2:]
+    grad_in[:, 0, :] = add_received(step, own, part, gots, half)
+    grad_in[:, 1, :] = grad_gate[...]
+
+
+def outputs_kernel(
+    ids, scan_half, scan_got, post_half, post_got, gain, x_w, dt_w, dt_b, conv_w, conv_b, a_log, skip, scan, post
+):
+    chans = scan.shape[1]
+    for full, half, got in ((scan, scan_half, scan_got), (post, post_half, post_got)):
+        full[:, core_half(ids, chans)] = half[...]
+        full[:, core_half(ids, chans, 1)] = got[...]
     rank = dt_w.shape[0]
     nstate = a_log.shape[0]
     count = x_w.shape[0]
     taps = conv_w.shape[0]
-    dt_w[...] = full[:rank, :]
-    a_log[...] = full[rank : rank + nstate, :]
-    dt_b[...] = full[rank + nstate : rank + nstate + 1, :]
-    skip[...] = full[rank + nstate + 1 : rank + nstate + 2, :]
-    x_w[...] = full[base : base + count, :]
-    conv_w[...] = full[base + count : base + count + taps, :]
-    conv_b[...] = full[base + count + taps : base + count + taps + 1, :]
+    dt_w[...] = scan[:rank, :]
+    a_log[...] = scan[rank : rank + nstate, :]
+    dt_b[...] = scan[rank + nstate : rank + nstate + 1, :]
+    skip[...] = scan[rank + nstate + 1 : rank + nstate + 2, :]
+    x_w[...] = post[:count, :]
+    conv_w[...] = post[count : count + taps, :]
+    conv_b[...] = post[count + taps : count + taps + 1, :]
     for i in range(gain.shape[1] // chans):
-        row = base + count + taps + 1 + i
-        gain[:, i * chans : (i + 1) * chans] = full[row : row + 1, :]
+        row = count + taps + 1 + i
+        gain[:, i * chans : (i + 1) * chans] = post[row : row + 1, :]
 
 
 def whole(shape):
@@ -466,6 +482,10 @@
     return pltpu.CompilerParams(
         dimension_semantics=("arbitrary",) * grid, vmem_limit_bytes=mib * 1024 * 1024
     )
+
+
+def cost(micros):
+    return pl.CostEstimate(flops=int(micros * 1.15e9), bytes_accessed=0, transcendentals=0)
 
 
 def struct(shape, dtype):
@@ -509,6 +529,7 @@
         ],
         scratch_shapes=[pltpu.VMEM((tokens + GROUP, chans), F32)],
         compiler_params=params(1),
+        cost_estimate=cost(7),
         name="pre",
     )(ids, *xs, *ws, gain, conv_w, conv_b, xw_t)
 
@@ -551,6 +572,7 @@
         scratch_shapes=[pltpu.VMEM((span, chans), F32)] * 2
         + [pltpu.VMEM((chans // LANES, 2 * GROUP * GROUP, LANES), F32), pltpu.VMEM((nstate, chans), F32)],
         compiler_params=params(2),
+        cost_estimate=cost(16),
         name="scan_forward",
     )(ids, lens, *projs, w_full, u_act, gate, dt_w, dt_b, a_log, skip)
 
@@ -565,7 +587,7 @@
     rank = dt_w.shape[0]
     span = min(LANES, tokens)
     blocks = tokens // span
-    small = STEP * -(-(rank + nstate + 2) // STEP)
+    small = SCAN_STEP * -(-(rank + nstate + 2) // SCAN_STEP)
     rows = lambda *tail: pl.BlockSpec(
         (1, span) + tail, lambda m, b: (m, blocks - 1 - b) + (0,) * len(tail)
     )
@@ -581,7 +603,7 @@
         + [pl.BlockSpec((1, span * nstate, chans), lambda m, b: (m, blocks - 1 - b, 0))]
         + [pl.BlockSpec((1, span * nstate, 2 * LANES), lambda m, b: (m, blocks - 1 - b, 0))]
         + [whole(v.shape) for v in (dt_w, a_log, skip)],
-        out_specs=[rows(width), proj, proj, rows(chans), rows(chans), whole((small, chans))],
+        out_specs=[rows(width), proj, proj, rows(chans), rows(chans), whole((small, chans)), whole((small, chans // 2))],
         out_shape=[
             struct((micro, tokens, width), BF16),
             struct((micro, count, tokens), F32),
@@ -589,24 +611,26 @@
             struct((micro, tokens, chans), F32),
             struct((micro, tokens, chans), BF16),
             struct((small, chans), F32),
+            struct((small, chans // 2), F32),
         ],
         scratch_shapes=[pltpu.VMEM((span, chans), F32)] * 4
         + [pltpu.VMEM((chans // LANES, 2 * GROUP * GROUP, LANES), F32)] * 2
         + [pltpu.VMEM((nstate, chans), F32)] * 2
         + [pltpu.VMEM((span * nstate, chans), BF16)],
         compiler_params=params(2),
+        cost_estimate=cost(21),
         name="scan_backward",
     )(ids, lens, *projs, *cots, w_full, u_act, gate, dt, y_rows, edge, low_state, vectors, dt_w, a_log, skip)
 
 
-def run_post(ids, projs, xs, d_scan, d_gate, u_act, summed, inner, inv, w_full, gain, xw_t, conv_w, scan_small):
+def run_post(ids, projs, xs, d_scan, d_gate, u_act, summed, inner, inv, w_full, gain, xw_t, conv_w):
     micro, tokens, chans = u_act.shape
     parts = len(projs)
     width = w_full.shape[0]
     quarter = width // parts
     count = projs[0].shape[1]
     taps = conv_w.shape[0]
-    small = scan_small.shape[0] + STEP * -(-(count + taps + 1 + width // chans) // STEP)
+    small = POST_STEP * -(-(count + taps + 1 + width // chans) // POST_STEP)
     lanes = max(width, LANES * -(-micro * tokens // LANES))
     per = lambda *tail: pl.BlockSpec((1,) + tail, lambda m: (m,) + (0,) * len(tail))
     return pl.pallas_call(
@@ -618,41 +642,39 @@
         + [per(tokens, chans)] * 5
         + [per(tokens, LANES)]
         + [whole((width, 2 * chans))]
-        + [whole(v.shape) for v in (gain, xw_t, conv_w, scan_small)],
+        + [whole(v.shape) for v in (gain, xw_t, conv_w)],
         out_specs=[
-            per(tokens, 2 * chans),
+            per(tokens, chans),
             whole((small, chans)),
             whole((small, chans // 2)),
             whole((GROUP, lanes)),
         ]
         + [per(tokens, quarter)] * parts,
         out_shape=[
-            struct((micro, tokens, 2 * chans), BF16),
+            struct((micro, tokens, chans), BF16),
             struct((small, chans), F32),
             struct((small, chans // 2), F32),
             struct((GROUP, lanes), F32),
             struct((micro, tokens, quarter), F32),
         ]
         + [struct((micro, tokens, quarter), BF16)] * (parts - 1),
-        scratch_shapes=[pltpu.VMEM((tokens + GROUP, chans), F32)] * 2,
+        scratch_shapes=[pltpu.VMEM((tokens + GROUP, chans), F32)] * 2
+        + [pltpu.VMEM((tokens, 2 * chans), BF16)],
         compiler_params=params(1),
+        cost_estimate=cost(8),
         name="post",
-    )(ids, *projs, *xs, d_scan, d_gate, u_act, summed, inner, inv, w_full, gain, xw_t, conv_w, scan_small)
-
-
-def run_grad(name, ids, left, right, shape, chips):
+    )(ids, *projs, *xs, d_scan, d_gate, u_act, summed, inner, inv, w_full, gain, xw_t, conv_w)
+
+
+def run_grad(name, ids, lefts, rights, shape, chips):
     if chips == 0:
         outs = [struct(shape, F32), struct((GROUP, LANES), BF16)]
     else:
         outs = [struct((chips,) + shape, F32), struct((chips,) + shape, BF16)]
-    return pl.pallas_call(
-        partial(grad_kernel, chips),
-        in_specs=[SMEM, pl.BlockSpec(memory_space=pltpu.VMEM), pl.BlockSpec(memory_space=pltpu.VMEM)],
-        out_specs=[pl.BlockSpec(memory_space=pltpu.VMEM)] * 2,
-        out_shape=outs,
-        compiler_params=pltpu.CompilerParams(vmem_limit_bytes=56 * 1024 * 1024),
-        name=name,
-    )(ids, left, right)
+    flat = lambda v: v.reshape(-1, v.shape[-1])
+    return run_local(
+        partial(grad_kernel, chips, len(lefts)), name, outs, ids, *map(flat, lefts), *map(flat, rights)
+    )
 
 
 VMEM = pl.BlockSpec(memory_space=pltpu.VMEM)
@@ -666,6 +688,7 @@
         out_shape=outs,
         scratch_shapes=list(scratch),
         compiler_params=pltpu.CompilerParams(vmem_limit_bytes=56 * 1024 * 1024),
+        cost_estimate=cost(3),
         name=name,
     )(*(() if ids is None else (ids,)), *operands)
 
@@ -677,6 +700,18 @@
 def others(value, axis, step=1):
     count = lax.axis_size(axis)
     return [swap(value, axis, mask) for mask in range(step, count, step)]
+
+
+def gather_line(value, axis, early=()):
+    count = lax.axis_size(axis)
+    got = {0: value}
+    mask = count // 2
+    while mask:
+        for known in sorted(got):
+            fresh = swap(got[known], axis, mask) if known or mask not in early else early[mask]
+            got[known | mask] = fresh
+        mask //= 2
+    return [got[k] for k in range(count)]
 
 
 def with_sibling(blocks):
@@ -731,10 +766,10 @@
     parts = lax.axis_size("tensor")
     weight = jnp.concatenate([in_rows, out_weight.T], axis=1)
 
-    xs = [tokens] + others(tokens, "tensor")
+    xs = gather_line(tokens, "tensor")
     if by_block:
         mine = [weight] + [
-            swap(after(weight, xs[1]) if mask > 4 else weight, "dp", mask) for mask in range(2, dps, 2)
+            swap(weight, "dp", mask) for mask in range(2, dps, 2)
         ]
         blocks = with_sibling(after(mine, *xs))
     else:
@@ -742,15 +777,17 @@
     normed, w_full, inner, summed, u_act, gate, inv, proj, proj_low = run_pre(
         ids, xs, blocks, gain, conv_weight, conv_bias[None], xw_t
     )
-    early = swap(after(cotangent, *xs), "tensor", 2)
+    cot_early = after(cotangent, *xs)
+    early = {mask: swap(cot_early, "tensor", mask) for mask in (parts // 2, 1)}
     projs = [proj] + others(proj_low, "tensor")
-    late = after(cotangent, *projs)
-    cots = [cotangent] + [early if mask == 2 else swap(late, "tensor", mask) for mask in range(1, parts)]
+    far = after(early[parts // 2], *projs)
+    early[parts // 2] = far
+    cots = gather_line(cotangent, "tensor", early)
     dt, y_rows, gated, edge, low_state, vectors, own_out, *out_terms = run_fwd(
         ids, lens, projs, w_full, u_act, gate, dt_weight, dt_bias[None], a_log, skip[None]
     )
     out_got = [swap(term, "tensor", k + 1) for k, term in enumerate(out_terms)]
-    cot_full, d_proj, d_proj_low, d_scan, d_gate, small = run_bwd(
+    cot_full, d_proj, d_proj_low, d_scan, d_gate, scan_small, scan_theirs = run_bwd(
         ids, lens, projs, cots, w_full, u_act, gate, dt, y_rows, edge, low_state, vectors, dt_weight, a_log, skip[None]
     )
     d_projs = [d_proj] + others(after(d_proj_low, *out_got), "tensor")
@@ -758,74 +795,87 @@
     for term in out_got:
         branch = branch + term.astype(F32)
     mixed = (tokens.astype(F32) + branch).astype(BF16)
-    out_mine, out_theirs = run_grad(
-        "grad_out",
+    rows = weight.shape[0] if chips else width
+    early_mine, early_theirs = run_grad(
+        "grad_early",
         ids,
-        after(cot_full, d_projs[1]).reshape(micro * seq, width),
-        gated.reshape(micro * seq, chans),
-        (weight.shape[0] if chips else width, chans),
+        [after(normed, d_projs), cot_full],
+        [d_gate, gated],
+        (rows, 2 * chans),
         chips,
     )
-    d_both, small, small_theirs, tiny, own_norm, *norm_terms = run_post(
-        ids,
-        d_projs,
-        xs,
-        after(d_scan, out_mine),
-        d_gate,
-        u_act,
-        summed,
-        inner,
-        inv,
-        w_full,
-        gain,
-        xw_t,
-        conv_weight,
-        small,
+
+    def merged(name, step, row, mine, theirs, small, small_theirs, tinies, wide):
+        part = struct((small.shape[0], chans // 2), F32)
+        own, part, *sends = run_local(
+            partial(merge_kernel, step, row),
+            name,
+            [struct((rows, wide), F32), part] + [struct((rows + step, wide), BF16)] * (chips - 1),
+            ids,
+            mine,
+            swap(theirs, "dp", 1),
+            small,
+            swap(small_theirs, "dp", 1),
+            *tinies,
+        )
+        return own, part, sends
+
+    if chips:
+        early_own, early_part, sends = merged(
+            "merge_early", SCAN_STEP, 0, early_mine, early_theirs, scan_small, scan_theirs, (), 2 * chans
+        )
+        early_gots = [swap(send, "dp", 2 * (j + 1)) for j, send in enumerate(sends)]
+    d_inner, small, small_theirs, tiny, own_norm, *norm_terms = run_post(
+        ids, d_projs, xs, d_scan, d_gate, u_act, summed, inner, inv, w_full, gain, xw_t, conv_weight
     )
     tiny_got = others(tiny, "tensor")
-    norm_got = [swap(term, "tensor", k + 1) for k, term in enumerate(norm_terms[:1] + list(after(norm_terms[1:], *tiny_got)))]
-    in_mine, in_theirs = run_grad(
-        "grad_in",
-        ids,
-        after(normed, tiny_got[0]).reshape(micro * seq, width),
-        d_both.reshape(micro * seq, 2 * chans),
-        (weight.shape[0] if chips else width, 2 * chans),
-        chips,
-    )
+    near = parts // 2
+    halves = [own_norm] + norm_terms
+    passed = [swap(halves[k], "tensor", k) for k in range(1, near)]
+    relayed = [swap(halves[near + k], "tensor", k) for k in range(1, near)]
+    far = halves[near].astype(F32)
+    for got in relayed:
+        far = far + got.astype(F32)
+    far = far.astype(BF16)
+    norm_got = passed + [swap(far, "tensor", near)]
+    late_mine, late_theirs = run_grad("grad_late", ids, [normed], [d_inner], (rows, chans), chips)
     for got in tiny_got:
         tiny = tiny + got
-    base = STEP * -(-(rank + nstate + 2) // STEP)
-    row = base + count + taps + 1
+    row = count + taps + 1
     if chips:
-        part_shape = struct((small.shape[0], chans // 2), F32)
-        own_grad, part, *sends = run_local(
-            partial(merge_kernel, row),
-            "merge",
-            [struct(weight.shape, F32), part_shape]
-            + [struct((weight.shape[0] + STEP, weight.shape[1]), BF16)] * (chips - 1),
-            ids,
-            after(in_mine, norm_got[0]),
-            swap(in_theirs, "dp", 1),
-            out_mine,
-            swap(out_theirs, "dp", 1),
+        late_own, late_part, sends = merged(
+            "merge_late",
+            POST_STEP,
+            row,
+            after(late_mine, far),
+            late_theirs,
             small,
-            swap(small_theirs, "dp", 1),
-            tiny,
-            swap(tiny, "dp", 1),
+            small_theirs,
+            (tiny, swap(tiny, "dp", 1)),
+            chans,
         )
-        gots = [swap(send, "dp", 2 * (j + 1)) for j, send in enumerate(sends)]
-        own_grad = after(own_grad, *norm_got)
-        grad_in, grad_out, half = run_local(
-            final_kernel,
-            "final",
-            [struct(in_weight.shape, F32), struct(out_weight.shape, F32), part_shape],
+        late_gots = [swap(send, "dp", 2 * (j + 1)) for j, send in enumerate(sends)]
+        grad_gate, grad_out, scan_half = run_local(
+            partial(final_early_kernel, SCAN_STEP),
+            "final_early",
+            [struct((rows, chans), F32), struct(out_weight.shape, F32), struct(early_part.shape, F32)],
             None,
-            own_grad,
-            part,
-            *gots,
+            early_own,
+            early_part,
+            *early_gots,
+        )
+        grad_in, post_half = run_local(
+            partial(final_late_kernel, POST_STEP),
+            "final_late",
+            [struct(in_weight.shape, F32), struct(late_part.shape, F32)],
+            None,
+            late_own,
+            late_part,
+            grad_gate,
+            *late_gots,
         )
         g_gain, g_x, g_dt, g_dtb, g_conv, g_convb, g_alog, g_skip = run_local(
-            partial(outputs_kernel, base),
+            outputs_kernel,
             "outputs",
             [
                 struct((1, width), F32),
@@ -838,24 +888,29 @@
                 struct((1, chans), F32),
             ],
             ids,
-            half,
-            swap(half, "dp", 1),
-            scratch=[pltpu.VMEM((small.shape[0], chans), F32)],
+            scan_half,
+            swap(scan_half, "dp", 1),
+            post_half,
+            swap(post_half, "dp", 1),
+            scratch=[pltpu.VMEM((scan_small.shape[0], chans), F32), pltpu.VMEM((small.shape[0], chans), F32)],
         )
         smalls = (g_gain[0], g_x.T, g_dt, g_dtb[0], g_conv, g_convb[0], g_alog, g_skip[0])
     else:
-        grad_in = lax.psum_scatter(in_mine, "dp", scatter_dimension=0, tiled=True)
-        grad_out = lax.psum_scatter(out_mine, "dp", scatter_dimension=0, tiled=True).T
+        grad_inner = lax.psum_scatter(late_mine, "dp", scatter_dimension=0, tiled=True)
+        early = lax.psum_scatter(early_mine, "dp", scatter_dimension=0, tiled=True)
+        grad_in = jnp.stack([grad_inner, early[:, :chans]], axis=1)
+        grad_out = early[:, chans:].T
+        scan_small = sum_all(scan_small)
         small = sum_all(lax.dynamic_update_slice_in_dim(small, tiny[0, :width].reshape(-1, chans), row, 0))
         smalls = (
             small[row : row + width // chans].reshape(width),
-            small[base : base + count].T,
-            small[:rank],
-            small[rank + nstate],
-            small[base + count : base + count + taps],
-            small[base + count + taps],
-            small[rank : rank + nstate],
-            small[rank + nstate + 1],
+            small[:count].T,
+            scan_small[:rank],
+            scan_small[rank + nstate],
+            small[count : count + taps],
+            small[count + taps],
+            scan_small[rank : rank + nstate],
+            scan_small[rank + nstate + 1],
         )
     d_norm = own_norm
     for term in norm_got:

time: 189 us -> 168 us (0.89)
  waiting for transfers between devices: 53.4 us -> 38.1 us
  starting transfers between devices: 50.7 us -> 45.6 us
  Pallas kernels: 69.6 us -> 72.9 us
  other arithmetic: 4.32 us -> 2.18 us
    ppermute x36 -> x41, waiting for transfers between devices: 53.4 us -> 38.1 us  [swap(): return lax.ppermute(value, axis, [(i, i ^ mask) for i in range(count)])]
    pallas_call x3 -> x7, Pallas kernels: 8.97 us -> 19.8 us  [run_local(): pl.pallas_call(kernel, in_specs=([SMEM] if ids is not None else []) + [VM...]
    pallas_call x2 -> x0, Pallas kernels: 7.4 us -> none  [run_grad(): pl.pallas_call(partial(grad_kernel, chips), in_specs=[SMEM, pl.BlockSpec(...]
    ppermute x36 -> x41, starting transfers between devices: 50.7 us -> 45.6 us  [swap(): return lax.ppermute(value, axis, [(i, i ^ mask) for i in range(count)])]
    unnamed x76 -> x88, local copies, waits for them, and re-layouts: 7.18 us -> 7.01 us
  transfers between devices with their start and end apart: 36 -> 41, of which waited for: 12 -> 13; matrix products, arithmetic and copies ran while one was open for 4% -> 3% of each run, Pallas kernels for 26% -> 42%
where the time goes in v2:
time: 168 us
  Pallas kernels  72.9 us (43%)
  starting transfers between devices  45.6 us (27%)
  waiting for transfers between devices  38.1 us (23%)
  local copies, waits for them, and re-layouts  7.99 us (5%)
  other arithmetic  2.18 us (1%)
    ppermute x41, starting transfers between devices, swap(): return lax.ppermute(value, axis, [(i, i ^ mask) for i in range(count)])  45.6 us
    ppermute x41, waiting for transfers between devices, swap(): return lax.ppermute(value, axis, [(i, i ^ mask) for i in range(count)])  38.1 us
    pallas_call x1, Pallas kernels, run_bwd(): pl.pallas_call(partial(bwd_kernel, parts), grid=(micro, blocks), in_specs...  21.5 us
    pallas_call x7, Pallas kernels, run_local(): pl.pallas_call(kernel, in_specs=([SMEM] if ids is not None else []) + [VM...  19.8 us
    pallas_call x1, Pallas kernels, run_fwd(): pl.pallas_call(partial(fwd_kernel, parts), grid=(micro, tokens // span),...  16.2 us
    pallas_call x1, Pallas kernels, run_post(): pl.pallas_call(partial(post_kernel, parts), grid=(micro,), in_specs=[SMEM...  7.78 us
    pallas_call x1, Pallas kernels, run_pre(): pl.pallas_call(partial(pre_kernel, len(xs), len(ws)), grid=(micro,), in_s...  7.6 us
    unnamed x88, local copies, waits for them, and re-layouts  7.01 us
  transfers between devices with their start and end apart: 41, of which 13 were waited for; matrix products, arithmetic and copies ran while one was open for 3% of the time, Pallas kernels for 42%

profile of v2, /device:TPU:0, one launch (start us, length us, event | category | flops | bytes accessed | tf_op | source)
XLA Modules:
  0.0 168.0 jit_solution(9237993130398971355)
XLA Ops:
  0.6 4.1 %collective-permute-start.1 = (bf16[2,256,256]{2,1,0:T(8,128)(2,1)}, bf16[2,256,256]{2,1,0:T(8,128)(2,1)S(1)}, u32[]{:S(2)}, u32[]{:S(2)}) collective-permute-start(bf16[2,256,256]{2,1,0:T(8,128)(2,1)} %refs_4_.3), channel_id=1, source_target_pairs={{0,2},{1,3},{2,0},{3,1},{4,6},{5,7},{6,4},{7,5},{8,10},{9,11},{10,... | collective-permute-start | bytes 786440 | tf_op jit(solution)/shard_map/ppermute | solution.py:35
  11.9 5.1 %collective-permute-done.1.refs_2_.refs_6_ = bf16[2,256,256]{2,1,0:T(8,128)(2,1)S(1)} collective-permute-done((bf16[2,256,256]{2,1,0:T(8,128)(2,1)}, bf16[2,256,256]{2,1,0:T(8,128)(2,1)S(1)}, u32[]{:S(2)}, u32[]{:S(2)}) %collective-permute-start.1) | collective-permute-done | bytes 262176 | tf_op jit(solution)/shard_map/ppermute | solution.py:35
  17.8 4.9 %collective-permute-done.refs_1_.refs_5_ = bf16[2,256,256]{2,1,0:T(8,128)(2,1)S(1)} collective-permute-done((bf16[2,256,256]{2,1,0:T(8,128)(2,1)}, bf16[2,256,256]{2,1,0:T(8,128)(2,1)S(1)}, u32[]{:S(2)}, u32[]{:S(2)}) %collective-permute-start) | collective-permute-done | bytes 262176 | tf_op jit(solution)/shard_map/ppermute | solution.py:35
  22.7 4.4 %collective-permute-done.4.refs_6_ = bf16[128,1536]{1,0:T(8,128)(2,1)S(1)} collective-permute-done((bf16[128,1536]{1,0:T(8,128)(2,1)S(1)}, bf16[128,1536]{1,0:T(8,128)(2,1)S(1)}, u32[]{:S(2)}, u32[]{:S(2)}) %collective-permute-start.4) | collective-permute-done | bytes 393248 | tf_op jit(solution)/shard_map/ppermute | solution.py:35
  31.7 7.6 %pre.1 = (bf16[2,256,1024]{2,1,0:T(8,128)(2,1)}, bf16[1024,1536]{1,0:T(8,128)(2,1)}, f32[2,256,512]{2,1,0:T(8,128)}, f32[2,256,512]{2,1,0:T(8,128)}, f32[2,256,5...) custom-call(s32[2]{0:T(128)} %pad_add_fusion.ids, ...), custom_call_target="tpu_custom_call" | custom-call | flops 8049999872 | tf_op jit(solution)/shard_map/pre/pallas_call | solution.py:501
  44.6 3.6 %collective-permute-done.10.refs_1_ = bf16[2,96,256]{2,1,0:T(8,128)(2,1)S(1)} collective-permute-done((bf16[2,96,256]{2,1,0:T(8,128)(2,1)}, bf16[2,96,256]{2,1,0:T(8,128)(2,1)S(1)}, u32[]{:S(2)}, u32[]{:S(2)}) %collective-permute-start.10) | collective-permute-done | bytes 98336 | tf_op jit(solution)/shard_map/ppermute | solution.py:35
  48.2 3.3 %collective-permute-done.11.refs_2_ = bf16[2,96,256]{2,1,0:T(8,128)(2,1)S(1)} collective-permute-done((bf16[2,96,256]{2,1,0:T(8,128)(2,1)}, bf16[2,96,256]{2,1,0:T(8,128)(2,1)S(1)}, u32[]{:S(2)}, u32[]{:S(2)}) %collective-permute-start.11) | collective-permute-done | bytes 98336 | tf_op jit(solution)/shard_map/ppermute | solution.py:35
  53.4 16.2 %scan_forward.1 = (f32[2,256,512]{2,1,0:T(8,128)}, f32[2,256,512]{2,1,0:T(8,128)}, bf16[2,256,512]{2,1,0:T(8,128)(2,1)}, f32[2,2,16,512]{3,2,1,0:T(8,128)}, bf16...) custom-call(s32[2]{0:T(128)} %pad_add_fusion.ids, ...), custom_call_target="tpu_custom_call" | custom-call | flops 18400000000 | tf_op jit(solution)/shard_map/scan_forward/pallas_call | solution.py:546
  71.8 2.4 %collective-permute-start.15 = (bf16[2,256,256]{2,1,0:T(8,128)(2,1)}, bf16[2,256,256]{2,1,0:T(8,128)(2,1)S(1)}, u32[]{:S(2)}, u32[]{:S(2)}) collective-permute-start(bf16[2,256,256]{2,1,0:T(8,128)(2,1)} %get-tuple-element.94), channel_id=1, source_target_pairs={{0,3},{1,2},{2,1},{3,0},{4,7},{5,6},{6,5},{7,4},{8,11},{9,10},{10,... | collective-permute-start | bytes 786440 | tf_op jit(solution)/shard_map/ppermute | solution.py:35
  74.9 21.5 %scan_backward.1 = (bf16[2,256,1024]{2,1,0:T(8,128)(2,1)}, f32[2,96,256]{2,1,0:T(8,128)}, bf16[2,96,256]{2,1,0:T(8,128)(2,1)}, f32[2,256,512]{2,1,0:T(8,128)}, b...) custom-call(s32[2]{0:T(128)} %pad_add_fusion.ids, s32[2]{0:T(128)} %bitcast.34, ...), custom_call_target="tpu_custom_call" | custom-call | flops 24149999616 | tf_op jit(solution)/shard_map/scan_backward/pallas_call | solution.py:595
  96.5 2.0 %collective-permute-start.20 = (bf16[2,96,256]{2,1,0:T(8,128)(2,1)}, bf16[2,96,256]{2,1,0:T(8,128)(2,1)S(1)}, u32[]{:S(2)}, u32[]{:S(2)}) collective-permute-start(bf16[2,96,256]{2,1,0:T(8,128)(2,1)} %get-tuple-element.105), channel_id=1, source_target_pairs={{0,2},{1,3},{2,0},{3,1},{4,6},{5,7},{6,4},{7,5},{8,10},{9,11},{10,... | collective-permute-start | bytes 294920 | tf_op jit(solution)/shard_map/ppermute | solution.py:35
  98.5 2.4 %collective-permute-start.21 = (bf16[2,96,256]{2,1,0:T(8,128)(2,1)}, bf16[2,96,256]{2,1,0:T(8,128)(2,1)S(1)}, u32[]{:S(2)}, u32[]{:S(2)}) collective-permute-start(bf16[2,96,256]{2,1,0:T(8,128)(2,1)} %get-tuple-element.105), channel_id=1, source_target_pairs={{0,3},{1,2},{2,1},{3,0},{4,7},{5,6},{6,5},{7,4},{8,11},{9,10},{10,... | collective-permute-start | bytes 294920 | tf_op jit(solution)/shard_map/ppermute | solution.py:35
  101.7 4.3 %collective-permute-done.20.refs_2_ = bf16[2,96,256]{2,1,0:T(8,128)(2,1)S(1)} collective-permute-done((bf16[2,96,256]{2,1,0:T(8,128)(2,1)}, bf16[2,96,256]{2,1,0:T(8,128)(2,1)S(1)}, u32[]{:S(2)}, u32[]{:S(2)}) %collective-permute-start.20) | collective-permute-done | bytes 98336 | tf_op jit(solution)/shard_map/ppermute | solution.py:35
  106.0 4.6 %grad_early.1 = (f32[4,128,1024]{2,1,0:T(8,128)}, bf16[4,128,1024]{2,1,0:T(8,128)(2,1)}) custom-call(s32[2]{0:T(128)} %pad_add_fusion.ids, bf16[512,1024]{1,0:T(8,128)(2,1)} %bitcast.35, bf16[512,1024]{1,0:T(8,128)(2,1)} %bitcast.37, bf16[512,512]{1,0:T(8,128)(2,1)} %bitcast.39, bf16[512,512]{1,0:T(8,128)(2,1)} %bitcast.38), custom_call_target="tpu_custom_call" | custom-call | flops 3449999872 | tf_op jit(solution)/shard_map/grad_early/pallas_call | solution.py:684
  110.6 7.8 %post.1 = (bf16[2,256,512]{2,1,0:T(8,128)(2,1)}, f32[128,512]{1,0:T(8,128)}, f32[128,256]{1,0:T(8,128)}, f32[8,1024]{1,0:T(8,128)}, f32[2,256,256]{2,1,0:T(8,128...) custom-call(s32[2]{0:T(128)} %pad_add_fusion.ids, ...), custom_call_target="tpu_custom_call" | custom-call | flops 9200000000 | tf_op jit(solution)/shard_map/post/pallas_call | solution.py:636
  120.7 2.2 %collective-permute-start.27 = (f32[8,1024]{1,0:T(8,128)}, f32[8,1024]{1,0:T(8,128)S(1)}, u32[]{:S(2)}, u32[]{:S(2)}) collective-permute-start(f32[8,1024]{1,0:T(8,128)} %get-tuple-element.114), channel_id=1, source_target_pairs={{0,3},{1,2},{2,1},{3,0},{4,7},{5,6},{6,5},{7,4},{8,11},{9,10},{10,... | collective-permute-start | bytes 98312 | tf_op jit(solution)/shard_map/ppermute | solution.py:35
  122.9 3.1 %grad_late.1 = (f32[4,128,512]{2,1,0:T(8,128)}, bf16[4,128,512]{2,1,0:T(8,128)(2,1)}) custom-call(s32[2]{0:T(128)} %pad_add_fusion.ids, bf16[512,1024]{1,0:T(8,128)(2,1)} %bitcast.36, bf16[512,512]{1,0:T(8,128)(2,1)} %bitcast.40), custom_call_target="tpu_custom_call" | custom-call | flops 3449999872 | tf_op jit(solution)/shard_map/grad_late/pallas_call | solution.py:684
  128.9 3.1 %merge_early.1 = (f32[128,1024]{1,0:T(8,128)}, f32[96,256]{1,0:T(8,128)}, bf16[160,1024]{1,0:T(8,128)(2,1)}, bf16[160,1024]{1,0:T(8,128)(2,1)}, bf16[160,1024]{1,0:T(8,128)(2,1)}) custom-call(s32[2]{0:T(128)} %pad_add_fusion.ids, f32[4,128,1024]{2,1,0:T(8,128)} %get-tuple-element.119.mine, bf16[4,128,1024]{2,1,0:T(8,128)(2,1)} %copy-done.10, ...), custom_call_target="tpu_custom_call" | custom-call | flops 3449999872 | tf_op jit(solution)/shard_map/merge_early/pallas_call | solution.py:684
  135.1 2.4 %collective-permute-start.32 = (bf16[160,1024]{1,0:T(8,128)(2,1)}, bf16[160,1024]{1,0:T(8,128)(2,1)S(1)}, u32[]{:S(2)}, u32[]{:S(2)}) collective-permute-start(bf16[160,1024]{1,0:T(8,128)(2,1)} %get-tuple-element.127), channel_id=1, source_target_pairs={{0,24},{4,28},{8,16},{12,20},{16,8},{20,12},{24,0},{28,4},{1,25},{... | collective-permute-start | bytes 983048 | tf_op jit(solution)/shard_map/ppermute | solution.py:35
  139.8 2.4 %merge_late.1 = (f32[128,512]{1,0:T(8,128)}, f32[128,256]{1,0:T(8,128)}, bf16[192,512]{1,0:T(8,128)(2,1)}, bf16[192,512]{1,0:T(8,128)(2,1)}, bf16[192,512]{1,0:T(8,128)(2,1)}) custom-call(s32[2]{0:T(128)} %pad_add_fusion.ids, f32[4,128,512]{2,1,0:T(8,128)} %get-tuple-element.131.mine, bf16[4,128,512]{2,1,0:T(8,128)(2,1)} %copy-done.11, ...), custom_call_target="tpu_custom_call" | custom-call | flops 3449999872 | tf_op jit(solution)/shard_map/merge_late/pallas_call | solution.py:684
  144.4 5.4 %collective-permute-done.31.refs_1_ = bf16[160,1024]{1,0:T(8,128)(2,1)S(1)} collective-permute-done((bf16[160,1024]{1,0:T(8,128)(2,1)}, bf16[160,1024]{1,0:T(8,128)(2,1)S(1)}, u32[]{:S(2)}, u32[]{:S(2)}) %collective-permute-start.31) | collective-permute-done | bytes 327712 | tf_op jit(solution)/shard_map/ppermute | solution.py:35
  152.6 2.3 %final_early.1 = (f32[128,512]{1,0:T(8,128)}, f32[512,128]{1,0:T(8,128)}, f32[96,256]{1,0:T(8,128)}) custom-call(f32[128,1024]{1,0:T(8,128)} %get-tuple-element.123.own, f32[96,256]{1,0:T(8,128)} %get-tuple-element.124.part, bf16[160,1024]{1,0:T(8,128)(2,1)} %copy-done.19, bf16[160,1024]{1,0:T(8,128)(2,1)} %copy-done.20, bf16[160,1024]{1,0:T(8,128)(2,1)} %copy-done.21), custom_call_target="tpu_custom_call" | custom-call | flops 3449999872 | tf_op jit(solution)/shard_map/final_early/pallas_call | solution.py:684
  155.0 4.9 %collective-permute-done.38.refs_1_ = bf16[192,512]{1,0:T(8,128)(2,1)S(1)} collective-permute-done((bf16[192,512]{1,0:T(8,128)(2,1)}, bf16[192,512]{1,0:T(8,128)(2,1)S(1)}, u32[]{:S(2)}, u32[]{:S(2)}) %collective-permute-start.38) | collective-permute-done | bytes 196640 | tf_op jit(solution)/shard_map/ppermute | solution.py:35
  160.7 2.3 %final_late.1 = (f32[128,2,512]{2,1,0:T(2,128)}, f32[128,256]{1,0:T(8,128)}) custom-call(f32[128,512]{1,0:T(8,128)} %get-tuple-element.135.own, f32[128,256]{1,0:T(8,128)} %get-tuple-element.136.part, f32[128,512]{1,0:T(8,128)} %get-tuple-element.137.grad_gate, bf16[192,512]{1,0:T(8,128)(2,1)} %copy-done.29, bf16[192,512]{1,0:T(8,128)(2,1)} %copy-done.30, ...), custom_call_target="tpu_custom_call" | custom-call | flops 3449999872 | tf_op jit(solution)/shard_map/final_late/pallas_call | solution.py:684
  (166 shorter events, 44.4 us)
Async XLA Ops:
  0.6 16.3 %collective-permute-start.1 = (bf16[2,256,256]{2,1,0:T(8,128)(2,1)}, bf16[2,256,256]{2,1,0:T(8,128)(2,1)S(1)}, u32[]{:S(2)}, u32[]{:S(2)}) collective-permute-start(bf16[2,256,256]{2,1,0:T(8,128)(2,1)} %refs_4_.3), channel_id=1, source_target_pairs={{0,2},{1,3},{2,0},{3,1},{4,6},{5,7},{6,4},{7,5},{8,10},{9,11},{10,... | collective-permute-start | bytes 786440 | tf_op jit(solution)/shard_map/ppermute | solution.py:35
  6.8 15.9 %collective-permute-start.3 = (bf16[128,1536]{1,0:T(8,128)(2,1)S(1)}, bf16[128,1536]{1,0:T(8,128)(2,1)S(1)}, u32[]{:S(2)}, u32[]{:S(2)}) collective-permute-start(bf16[128,1536]{1,0:T(8,128)(2,1)S(1)} %pad_maximum_fusion.refs_4_), channel_id=1, source_target_pairs={{0,8},{4,12},{8,0},{12,4},{16,24},{20,28},{24,16},{28,20},{1,9},{5... | collective-permute-start | bytes 1179656 | tf_op jit(solution)/shard_map/ppermute | solution.py:35
  8.3 18.7 %collective-permute-start.4 = (bf16[128,1536]{1,0:T(8,128)(2,1)S(1)}, bf16[128,1536]{1,0:T(8,128)(2,1)S(1)}, u32[]{:S(2)}, u32[]{:S(2)}) collective-permute-start(bf16[128,1536]{1,0:T(8,128)(2,1)S(1)} %pad_maximum_fusion.refs_4_), channel_id=1, source_target_pairs={{0,16},{4,20},{8,24},{12,28},{16,0},{20,4},{24,8},{28,12},{1,17},{... | collective-permute-start | bytes 1179656 | tf_op jit(solution)/shard_map/ppermute | solution.py:35
  9.9 17.2 %collective-permute-start.5 = (bf16[128,1536]{1,0:T(8,128)(2,1)S(1)}, bf16[128,1536]{1,0:T(8,128)(2,1)S(1)}, u32[]{:S(2)}, u32[]{:S(2)}) collective-permute-start(bf16[128,1536]{1,0:T(8,128)(2,1)S(1)} %pad_maximum_fusion.refs_4_), channel_id=1, source_target_pairs={{0,24},{4,28},{8,16},{12,20},{16,8},{20,12},{24,0},{28,4},{1,25},{... | collective-permute-start | bytes 1179656 | tf_op jit(solution)/shard_map/ppermute | solution.py:35
  10.3 12.3 %collective-permute-start = (bf16[2,256,256]{2,1,0:T(8,128)(2,1)}, bf16[2,256,256]{2,1,0:T(8,128)(2,1)S(1)}, u32[]{:S(2)}, u32[]{:S(2)}) collective-permute-start(bf16[2,256,256]{2,1,0:T(8,128)(2,1)} %refs_4_.3), channel_id=1, source_target_pairs={{0,1},{1,0},{2,3},{3,2},{4,5},{5,4},{6,7},{7,6},{8,9},{9,8},{10,11... | collective-permute-start | bytes 786440 | tf_op jit(solution)/shard_map/ppermute | solution.py:35
  17.0 10.5 %collective-permute-start.2 = (bf16[2,256,256]{2,1,0:T(8,128)(2,1)S(1)}, bf16[2,256,256]{2,1,0:T(8,128)(2,1)S(1)}, u32[]{:S(2)}, u32[]{:S(2)}) collective-permute-start(bf16[2,256,256]{2,1,0:T(8,128)(2,1)S(1)} %collective-permute-done.1.refs_2_.refs_6_), channel_id=1, source_target_pairs={{0,1},{1,0},{2,3},{3,2},{4,5},{5,4},{6,7},{7,6},{8,9},{9,8},{10,11... | collective-permute-start | bytes 786440 | tf_op jit(solution)/shard_map/ppermute | solution.py:35
  29.2 15.4 %collective-permute-start.17 = (bf16[2,256,256]{2,1,0:T(8,128)(2,1)}, bf16[2,256,256]{2,1,0:T(8,128)(2,1)S(1)}, u32[]{:S(2)}, u32[]{:S(2)}) collective-permute-start(bf16[2,256,256]{2,1,0:T(8,128)(2,1)} %refs_4_.2), channel_id=1, source_target_pairs={{0,2},{1,3},{2,0},{3,1},{4,6},{5,7},{6,4},{7,5},{8,10},{9,11},{10,... | collective-permute-start | bytes 786440 | tf_op jit(solution)/shard_map/ppermute | solution.py:35
  41.1 10.4 %collective-permute-start.11 = (bf16[2,96,256]{2,1,0:T(8,128)(2,1)}, bf16[2,96,256]{2,1,0:T(8,128)(2,1)S(1)}, u32[]{:S(2)}, u32[]{:S(2)}) collective-permute-start(bf16[2,96,256]{2,1,0:T(8,128)(2,1)} %get-tuple-element.87), channel_id=1, source_target_pairs={{0,2},{1,3},{2,0},{3,1},{4,6},{5,7},{6,4},{7,5},{8,10},{9,11},{10,... | collective-permute-start | bytes 294920 | tf_op jit(solution)/shard_map/ppermute | solution.py:35
  43.7 30.4 %collective-permute-start.16 = (bf16[2,256,256]{2,1,0:T(8,128)(2,1)S(1)}, bf16[2,256,256]{2,1,0:T(8,128)(2,1)S(1)}, u32[]{:S(2)}, u32[]{:S(2)}) collective-permute-start(bf16[2,256,256]{2,1,0:T(8,128)(2,1)S(1)} %copy-done.4), channel_id=1, source_target_pairs={{0,1},{1,0},{2,3},{3,2},{4,5},{5,4},{6,7},{7,6},{8,9},{9,8},{10,11... | collective-permute-start | bytes 786440 | tf_op jit(solution)/shard_map/ppermute | solution.py:35
  51.5 22.6 %collective-permute-start.18 = (bf16[2,256,256]{2,1,0:T(8,128)(2,1)S(1)}, bf16[2,256,256]{2,1,0:T(8,128)(2,1)S(1)}, u32[]{:S(2)}, u32[]{:S(2)}) collective-permute-start(bf16[2,256,256]{2,1,0:T(8,128)(2,1)S(1)} %collective-permute-done.17.refs_6_), channel_id=1, source_target_pairs={{0,1},{1,0},{2,3},{3,2},{4,5},{5,4},{6,7},{7,6},{8,9},{9,8},{10,11... | collective-permute-start | bytes 786440 | tf_op jit(solution)/shard_map/ppermute | solution.py:35
  69.7 26.7 %collective-permute-start.13 = (bf16[2,256,256]{2,1,0:T(8,128)(2,1)}, bf16[2,256,256]{2,1,0:T(8,128)(2,1)S(1)}, u32[]{:S(2)}, u32[]{:S(2)}) collective-permute-start(bf16[2,256,256]{2,1,0:T(8,128)(2,1)} %get-tuple-element.92), channel_id=1, source_target_pairs={{0,1},{1,0},{2,3},{3,2},{4,5},{5,4},{6,7},{7,6},{8,9},{9,8},{10,11... | collective-permute-start | bytes 786440 | tf_op jit(solution)/shard_map/ppermute | solution.py:35
  70.4 26.1 %collective-permute-start.14 = (bf16[2,256,256]{2,1,0:T(8,128)(2,1)}, bf16[2,256,256]{2,1,0:T(8,128)(2,1)S(1)}, u32[]{:S(2)}, u32[]{:S(2)}) collective-permute-start(bf16[2,256,256]{2,1,0:T(8,128)(2,1)} %get-tuple-element.93), channel_id=1, source_target_pairs={{0,2},{1,3},{2,0},{3,1},{4,6},{5,7},{6,4},{7,5},{8,10},{9,11},{10,... | collective-permute-start | bytes 786440 | tf_op jit(solution)/shard_map/ppermute | solution.py:35
  71.8 24.7 %collective-permute-start.15 = (bf16[2,256,256]{2,1,0:T(8,128)(2,1)}, bf16[2,256,256]{2,1,0:T(8,128)(2,1)S(1)}, u32[]{:S(2)}, u32[]{:S(2)}) collective-permute-start(bf16[2,256,256]{2,1,0:T(8,128)(2,1)} %get-tuple-element.94), channel_id=1, source_target_pairs={{0,3},{1,2},{2,1},{3,0},{4,7},{5,6},{6,5},{7,4},{8,11},{9,10},{10,... | collective-permute-start | bytes 786440 | tf_op jit(solution)/shard_map/ppermute | solution.py:35
  101.7 25.9 %collective-permute-start.29 = (f32[96,256]{1,0:T(8,128)}, f32[96,256]{1,0:T(8,128)S(1)}, u32[]{:S(2)}, u32[]{:S(2)}) collective-permute-start(f32[96,256]{1,0:T(8,128)} %get-tuple-element.122), channel_id=1, source_target_pairs={{0,4},{4,0},{8,12},{12,8},{16,20},{20,16},{24,28},{28,24},{1,5},{5... | collective-permute-start | bytes 294920 | tf_op jit(solution)/shard_map/ppermute | solution.py:35
  110.6 17.4 %collective-permute-start.28 = (bf16[4,128,1024]{2,1,0:T(8,128)(2,1)}, bf16[4,128,1024]{2,1,0:T(8,128)(2,1)S(1)}, u32[]{:S(2)}, u32[]{:S(2)}) collective-permute-start(bf16[4,128,1024]{2,1,0:T(8,128)(2,1)} %get-tuple-element.120), channel_id=1, source_target_pairs={{0,4},{4,0},{8,12},{12,8},{16,20},{20,16},{24,28},{28,24},{1,5},{5... | collective-permute-start | bytes 3145736 | tf_op jit(solution)/shard_map/ppermute | solution.py:35
  126.0 12.3 %collective-permute-start.34 = (bf16[4,128,512]{2,1,0:T(8,128)(2,1)}, bf16[4,128,512]{2,1,0:T(8,128)(2,1)S(1)}, u32[]{:S(2)}, u32[]{:S(2)}) collective-permute-start(bf16[4,128,512]{2,1,0:T(8,128)(2,1)} %get-tuple-element.132), channel_id=1, source_target_pairs={{0,4},{4,0},{8,12},{12,8},{16,20},{20,16},{24,28},{28,24},{1,5},{5... | collective-permute-start | bytes 1572872 | tf_op jit(solution)/shard_map/ppermute | solution.py:35
  126.9 10.7 %collective-permute-start.35 = (f32[128,256]{1,0:T(8,128)}, f32[128,256]{1,0:T(8,128)}, u32[]{:S(2)}, u32[]{:S(2)}) collective-permute-start(f32[128,256]{1,0:T(8,128)} %get-tuple-element.134), channel_id=1, source_target_pairs={{0,4},{4,0},{8,12},{12,8},{16,20},{20,16},{24,28},{28,24},{1,5},{5... | collective-permute-start | bytes 393224 | tf_op jit(solution)/shard_map/ppermute | solution.py:35
  132.1 10.8 %collective-permute-start.30 = (bf16[160,1024]{1,0:T(8,128)(2,1)}, bf16[160,1024]{1,0:T(8,128)(2,1)S(1)}, u32[]{:S(2)}, u32[]{:S(2)}) collective-permute-start(bf16[160,1024]{1,0:T(8,128)(2,1)} %get-tuple-element.125), channel_id=1, source_target_pairs={{0,8},{4,12},{8,0},{12,4},{16,24},{20,28},{24,16},{28,20},{1,9},{5... | collective-permute-start | bytes 983048 | tf_op jit(solution)/shard_map/ppermute | solution.py:35
  133.6 16.2 %collective-permute-start.31 = (bf16[160,1024]{1,0:T(8,128)(2,1)}, bf16[160,1024]{1,0:T(8,128)(2,1)S(1)}, u32[]{:S(2)}, u32[]{:S(2)}) collective-permute-start(bf16[160,1024]{1,0:T(8,128)(2,1)} %get-tuple-element.126), channel_id=1, source_target_pairs={{0,16},{4,20},{8,24},{12,28},{16,0},{20,4},{24,8},{28,12},{1,17},{... | collective-permute-start | bytes 983048 | tf_op jit(solution)/shard_map/ppermute | solution.py:35
  135.1 16.7 %collective-permute-start.32 = (bf16[160,1024]{1,0:T(8,128)(2,1)}, bf16[160,1024]{1,0:T(8,128)(2,1)S(1)}, u32[]{:S(2)}, u32[]{:S(2)}) collective-permute-start(bf16[160,1024]{1,0:T(8,128)(2,1)} %get-tuple-element.127), channel_id=1, source_target_pairs={{0,24},{4,28},{8,16},{12,20},{16,8},{20,12},{24,0},{28,4},{1,25},{... | collective-permute-start | bytes 983048 | tf_op jit(solution)/shard_map/ppermute | solution.py:35
  137.6 25.9 %collective-permute-start.22 = (bf16[2,256,256]{2,1,0:T(8,128)(2,1)S(1)}, bf16[2,256,256]{2,1,0:T(8,128)(2,1)S(1)}, u32[]{:S(2)}, u32[]{:S(2)}) collective-permute-start(bf16[2,256,256]{2,1,0:T(8,128)(2,1)S(1)} %copy-done.25), channel_id=1, source_target_pairs={{0,1},{1,0},{2,3},{3,2},{4,5},{5,4},{6,7},{7,6},{8,9},{9,8},{10,11... | collective-permute-start | bytes 786440 | tf_op jit(solution)/shard_map/ppermute | solution.py:35
  138.3 25.1 %collective-permute-start.24 = (bf16[2,256,256]{2,1,0:T(8,128)(2,1)S(1)}, bf16[2,256,256]{2,1,0:T(8,128)(2,1)S(1)}, u32[]{:S(2)}, u32[]{:S(2)}) collective-permute-start(bf16[2,256,256]{2,1,0:T(8,128)(2,1)S(1)} %add_convert_fusion), channel_id=1, source_target_pairs={{0,2},{1,3},{2,0},{3,1},{4,6},{5,7},{6,4},{7,5},{8,10},{9,11},{10,... | collective-permute-start | bytes 786440 | tf_op jit(solution)/shard_map/ppermute | solution.py:35
  142.8 12.1 %collective-permute-start.37 = (bf16[192,512]{1,0:T(8,128)(2,1)}, bf16[192,512]{1,0:T(8,128)(2,1)S(1)}, u32[]{:S(2)}, u32[]{:S(2)}) collective-permute-start(bf16[192,512]{1,0:T(8,128)(2,1)} %get-tuple-element.138), channel_id=1, source_target_pairs={{0,8},{4,12},{8,0},{12,4},{16,24},{20,28},{24,16},{28,20},{1,9},{5... | collective-permute-start | bytes 589832 | tf_op jit(solution)/shard_map/ppermute | solution.py:35
  149.8 10.1 %collective-permute-start.38 = (bf16[192,512]{1,0:T(8,128)(2,1)}, bf16[192,512]{1,0:T(8,128)(2,1)S(1)}, u32[]{:S(2)}, u32[]{:S(2)}) collective-permute-start(bf16[192,512]{1,0:T(8,128)(2,1)} %get-tuple-element.139), channel_id=1, source_target_pairs={{0,16},{4,20},{8,24},{12,28},{16,0},{20,4},{24,8},{28,12},{1,17},{... | collective-permute-start | bytes 589832 | tf_op jit(solution)/shard_map/ppermute | solution.py:35
  (60 other events, 350.4 us)

commit v3 on v2

--- a/solution.py
+++ b/solution.py
@@ -410,10 +410,10 @@
         for i in range(tinies[0].shape[1] // chans):
             cols = pl.ds(pl.multiple_of((ids[1] & 1) * half, LANES) + i * chans, half)
             part[row + i : row + i + 1, :] = tinies[0][0:1, cols] + tinies[1][0:1, cols]
-    own[...] = mine[0] + got[0].astype(F32)
+    own[...] = mine[0].astype(F32) + got[0].astype(F32)
     pieces = part.shape[0] // step
     for j, send in enumerate(sends):
-        send[:rows, :] = (mine[j + 1] + got[j + 1].astype(F32)).astype(BF16)
+        send[:rows, :] = (mine[j + 1].astype(F32) + got[j + 1].astype(F32)).astype(BF16)
         for c in range(pieces):
             send[rows:, c * half : (c + 1) * half] = part[c * step : (c + 1) * step, :].astype(BF16)
         if pieces * half < send.shape[1]:
@@ -661,7 +661,7 @@
         scratch_shapes=[pltpu.VMEM((tokens + GROUP, chans), F32)] * 2
         + [pltpu.VMEM((tokens, 2 * chans), BF16)],
         compiler_params=params(1),
-        cost_estimate=cost(8),
+        cost_estimate=cost(20),
         name="post",
     )(ids, *projs, *xs, d_scan, d_gate, u_act, summed, inner, inv, w_full, gain, xw_t, conv_w)
 
@@ -670,7 +670,7 @@
     if chips == 0:
         outs = [struct(shape, F32), struct((GROUP, LANES), BF16)]
     else:
-        outs = [struct((chips,) + shape, F32), struct((chips,) + shape, BF16)]
+        outs = [struct((chips,) + shape, BF16)] * 2
     flat = lambda v: v.reshape(-1, v.shape[-1])
     return run_local(
         partial(grad_kernel, chips, len(lefts)), name, outs, ids, *map(flat, lefts), *map(flat, rights)
@@ -683,12 +683,13 @@
 def run_local(kernel, name, outs, ids, *operands, scratch=()):
     return pl.pallas_call(
         kernel,
-        in_specs=([SMEM] if ids is not None else []) + [VMEM] * len(operands),
-        out_specs=[VMEM] * len(outs),
+        grid=(1,),
+        in_specs=([SMEM] if ids is not None else []) + [whole(v.shape) for v in operands],
+        out_specs=[whole(v.shape) for v in outs],
         out_shape=outs,
         scratch_shapes=list(scratch),
         compiler_params=pltpu.CompilerParams(vmem_limit_bytes=56 * 1024 * 1024),
-        cost_estimate=cost(3),
+        cost_estimate=cost(0.3),
         name=name,
     )(*(() if ids is None else (ids,)), *operands)
 
@@ -799,7 +800,7 @@
     early_mine, early_theirs = run_grad(
         "grad_early",
         ids,
-        [after(normed, d_projs), cot_full],
+        [after(normed, d_projs[1]), cot_full],
         [d_gate, gated],
         (rows, 2 * chans),
         chips,

time: 168 us -> 166 us (0.988)
  waiting for transfers between devices: 38.1 us -> 33.4 us
  other arithmetic: 2.18 us -> 6.74 us
  starting transfers between devices: 45.6 us -> 43.2 us
    ppermute x41, waiting for transfers between devices: 38.1 us -> 33.4 us  [swap(): return lax.ppermute(value, axis, [(i, i ^ mask) for i in range(count)])]
    ppermute x41, starting transfers between devices: 45.6 us -> 43.2 us  [swap(): return lax.ppermute(value, axis, [(i, i ^ mask) for i in range(count)])]
    convert_element_type x1, other arithmetic: 0.06 us -> 1.8 us  [body(): far = far.astype(BF16)]
    unnamed x88 -> x82, local copies, waits for them, and re-layouts: 7.01 us -> 6.75 us
  transfers between devices with their start and end apart: 41 -> 41, of which waited for: 13 -> 12; matrix products, arithmetic and copies ran while one was open for 3% -> 6% of each run, Pallas kernels for 42% -> 42%
where the time goes in v3:
time: 166 us; the launch traced here: 165 us
  Pallas kernels  71.9 us (43%)
  starting transfers between devices  43.2 us (26%)
  waiting for transfers between devices  33.4 us (20%)
  local copies, waits for them, and re-layouts  8.45 us (5%)
  other arithmetic  6.74 us (4%)
    ppermute x41, starting transfers between devices, swap(): return lax.ppermute(value, axis, [(i, i ^ mask) for i in range(count)])  43.2 us
    ppermute x41, waiting for transfers between devices, swap(): return lax.ppermute(value, axis, [(i, i ^ mask) for i in range(count)])  33.4 us
    pallas_call x1, Pallas kernels, run_bwd(): pl.pallas_call(partial(bwd_kernel, parts), grid=(micro, blocks), in_specs...  21.5 us
    pallas_call x7, Pallas kernels, run_local(): pl.pallas_call(kernel, grid=(1,), in_specs=([SMEM] if ids is not None els...  18.8 us
    pallas_call x1, Pallas kernels, run_fwd(): pl.pallas_call(partial(fwd_kernel, parts), grid=(micro, tokens // span),...  16.2 us
    pallas_call x1, Pallas kernels, run_post(): pl.pallas_call(partial(post_kernel, parts), grid=(micro,), in_specs=[SMEM...  7.77 us
    pallas_call x1, Pallas kernels, run_pre(): pl.pallas_call(partial(pre_kernel, len(xs), len(ws)), grid=(micro,), in_s...  7.59 us
    unnamed x82, local copies, waits for them, and re-layouts  6.75 us
  transfers between devices with their start and end apart: 41, of which 12 were waited for; matrix products, arithmetic and copies ran while one was open for 6% of the time, Pallas kernels for 42%

profile of v3, /device:TPU:0, one launch (start us, length us, event | category | flops | bytes accessed | tf_op | source)
XLA Modules:
  0.0 165.0 jit_solution(1715929194328168949)
XLA Ops:
  0.6 4.1 %collective-permute-start.1 = (bf16[2,256,256]{2,1,0:T(8,128)(2,1)}, bf16[2,256,256]{2,1,0:T(8,128)(2,1)S(1)}, u32[]{:S(2)}, u32[]{:S(2)}) collective-permute-start(bf16[2,256,256]{2,1,0:T(8,128)(2,1)} %refs_4_.3), channel_id=1, source_target_pairs={{0,2},{1,3},{2,0},{3,1},{4,6},{5,7},{6,4},{7,5},{8,10},{9,11},{10,... | collective-permute-start | bytes 786440 | tf_op jit(solution)/shard_map/ppermute | solution.py:35
  11.9 5.1 %collective-permute-done.1.refs_2_.refs_6_ = bf16[2,256,256]{2,1,0:T(8,128)(2,1)S(1)} collective-permute-done((bf16[2,256,256]{2,1,0:T(8,128)(2,1)}, bf16[2,256,256]{2,1,0:T(8,128)(2,1)S(1)}, u32[]{:S(2)}, u32[]{:S(2)}) %collective-permute-start.1) | collective-permute-done | bytes 262176 | tf_op jit(solution)/shard_map/ppermute | solution.py:35
  17.8 4.9 %collective-permute-done.refs_1_.refs_5_ = bf16[2,256,256]{2,1,0:T(8,128)(2,1)S(1)} collective-permute-done((bf16[2,256,256]{2,1,0:T(8,128)(2,1)}, bf16[2,256,256]{2,1,0:T(8,128)(2,1)S(1)}, u32[]{:S(2)}, u32[]{:S(2)}) %collective-permute-start) | collective-permute-done | bytes 262176 | tf_op jit(solution)/shard_map/ppermute | solution.py:35
  22.7 4.4 %collective-permute-done.4.refs_6_ = bf16[128,1536]{1,0:T(8,128)(2,1)S(1)} collective-permute-done((bf16[128,1536]{1,0:T(8,128)(2,1)S(1)}, bf16[128,1536]{1,0:T(8,128)(2,1)S(1)}, u32[]{:S(2)}, u32[]{:S(2)}) %collective-permute-start.4) | collective-permute-done | bytes 393248 | tf_op jit(solution)/shard_map/ppermute | solution.py:35
  31.7 7.6 %pre.1 = (bf16[2,256,1024]{2,1,0:T(8,128)(2,1)}, bf16[1024,1536]{1,0:T(8,128)(2,1)}, f32[2,256,512]{2,1,0:T(8,128)}, f32[2,256,512]{2,1,0:T(8,128)}, f32[2,256,5...) custom-call(s32[2]{0:T(128)} %pad_add_fusion.ids, ...), custom_call_target="tpu_custom_call" | custom-call | flops 8049999872 | tf_op jit(solution)/shard_map/pre/pallas_call | solution.py:501
  39.3 1.9 %collective-permute-start.10 = (bf16[2,96,256]{2,1,0:T(8,128)(2,1)}, bf16[2,96,256]{2,1,0:T(8,128)(2,1)S(1)}, u32[]{:S(2)}, u32[]{:S(2)}) collective-permute-start(bf16[2,96,256]{2,1,0:T(8,128)(2,1)} %get-tuple-element.87), channel_id=1, source_target_pairs={{0,1},{1,0},{2,3},{3,2},{4,5},{5,4},{6,7},{7,6},{8,9},{9,8},{10,11... | collective-permute-start | bytes 294920 | tf_op jit(solution)/shard_map/ppermute | solution.py:35
  44.7 3.9 %collective-permute-done.10.refs_1_ = bf16[2,96,256]{2,1,0:T(8,128)(2,1)S(1)} collective-permute-done((bf16[2,96,256]{2,1,0:T(8,128)(2,1)}, bf16[2,96,256]{2,1,0:T(8,128)(2,1)S(1)}, u32[]{:S(2)}, u32[]{:S(2)}) %collective-permute-start.10) | collective-permute-done | bytes 98336 | tf_op jit(solution)/shard_map/ppermute | solution.py:35
  48.6 2.9 %collective-permute-done.11.refs_2_ = bf16[2,96,256]{2,1,0:T(8,128)(2,1)S(1)} collective-permute-done((bf16[2,96,256]{2,1,0:T(8,128)(2,1)}, bf16[2,96,256]{2,1,0:T(8,128)(2,1)S(1)}, u32[]{:S(2)}, u32[]{:S(2)}) %collective-permute-start.11) | collective-permute-done | bytes 98336 | tf_op jit(solution)/shard_map/ppermute | solution.py:35
  53.3 16.2 %scan_forward.1 = (f32[2,256,512]{2,1,0:T(8,128)}, f32[2,256,512]{2,1,0:T(8,128)}, bf16[2,256,512]{2,1,0:T(8,128)(2,1)}, f32[2,2,16,512]{3,2,1,0:T(8,128)}, bf16...) custom-call(s32[2]{0:T(128)} %pad_add_fusion.ids, ...), custom_call_target="tpu_custom_call" | custom-call | flops 18400000000 | tf_op jit(solution)/shard_map/scan_forward/pallas_call | solution.py:546
  71.7 2.3 %collective-permute-start.15 = (bf16[2,256,256]{2,1,0:T(8,128)(2,1)}, bf16[2,256,256]{2,1,0:T(8,128)(2,1)S(1)}, u32[]{:S(2)}, u32[]{:S(2)}) collective-permute-start(bf16[2,256,256]{2,1,0:T(8,128)(2,1)} %get-tuple-element.94), channel_id=1, source_target_pairs={{0,3},{1,2},{2,1},{3,0},{4,7},{5,6},{6,5},{7,4},{8,11},{9,10},{10,... | collective-permute-start | bytes 786440 | tf_op jit(solution)/shard_map/ppermute | solution.py:35
  74.8 21.5 %scan_backward.1 = (bf16[2,256,1024]{2,1,0:T(8,128)(2,1)}, f32[2,96,256]{2,1,0:T(8,128)}, bf16[2,96,256]{2,1,0:T(8,128)(2,1)}, f32[2,256,512]{2,1,0:T(8,128)}, b...) custom-call(s32[2]{0:T(128)} %pad_add_fusion.ids, s32[2]{0:T(128)} %bitcast.40, ...), custom_call_target="tpu_custom_call" | custom-call | flops 24149999616 | tf_op jit(solution)/shard_map/scan_backward/pallas_call | solution.py:595
  96.5 2.1 %collective-permute-start.20 = (bf16[2,96,256]{2,1,0:T(8,128)(2,1)}, bf16[2,96,256]{2,1,0:T(8,128)(2,1)S(1)}, u32[]{:S(2)}, u32[]{:S(2)}) collective-permute-start(bf16[2,96,256]{2,1,0:T(8,128)(2,1)} %get-tuple-element.105), channel_id=1, source_target_pairs={{0,2},{1,3},{2,0},{3,1},{4,6},{5,7},{6,4},{7,5},{8,10},{9,11},{10,... | collective-permute-start | bytes 294920 | tf_op jit(solution)/shard_map/ppermute | solution.py:35
  98.6 2.3 %collective-permute-start.21 = (bf16[2,96,256]{2,1,0:T(8,128)(2,1)}, bf16[2,96,256]{2,1,0:T(8,128)(2,1)S(1)}, u32[]{:S(2)}, u32[]{:S(2)}) collective-permute-start(bf16[2,96,256]{2,1,0:T(8,128)(2,1)} %get-tuple-element.105), channel_id=1, source_target_pairs={{0,3},{1,2},{2,1},{3,0},{4,7},{5,6},{6,5},{7,4},{8,11},{9,10},{10,... | collective-permute-start | bytes 294920 | tf_op jit(solution)/shard_map/ppermute | solution.py:35
  101.3 4.3 %grad_early.1 = (bf16[4,128,1024]{2,1,0:T(8,128)(2,1)}, bf16[4,128,1024]{2,1,0:T(8,128)(2,1)}) custom-call(s32[2]{0:T(128)} %pad_add_fusion.ids, bf16[512,1024]{1,0:T(8,128)(2,1)} %bitcast.22, bf16[512,1024]{1,0:T(8,128)(2,1)} %bitcast.25, bf16[512,512]{1,0:T(8,128)(2,1)} %bitcast.28, bf16[512,512]{1,0:T(8,128)(2,1)} %bitcast.29), custom_call_target="tpu_custom_call" | custom-call | flops 345000000 | tf_op jit(solution)/shard_map/grad_early/pallas_call | solution.py:684
  106.5 7.8 %post.1 = (bf16[2,256,512]{2,1,0:T(8,128)(2,1)}, f32[128,512]{1,0:T(8,128)}, f32[128,256]{1,0:T(8,128)}, f32[8,1024]{1,0:T(8,128)}, f32[2,256,256]{2,1,0:T(8,128...) custom-call(s32[2]{0:T(128)} %pad_add_fusion.ids, ...), custom_call_target="tpu_custom_call" | custom-call | flops 23000000512 | tf_op jit(solution)/shard_map/post/pallas_call | solution.py:636
  116.7 2.1 %collective-permute-start.27 = (f32[8,1024]{1,0:T(8,128)}, f32[8,1024]{1,0:T(8,128)S(1)}, u32[]{:S(2)}, u32[]{:S(2)}) collective-permute-start(f32[8,1024]{1,0:T(8,128)} %get-tuple-element.114), channel_id=1, source_target_pairs={{0,3},{1,2},{2,1},{3,0},{4,7},{5,6},{6,5},{7,4},{8,11},{9,10},{10,... | collective-permute-start | bytes 98312 | tf_op jit(solution)/shard_map/ppermute | solution.py:35
  118.8 2.9 %grad_late.1 = (bf16[4,128,512]{2,1,0:T(8,128)(2,1)}, bf16[4,128,512]{2,1,0:T(8,128)(2,1)}) custom-call(s32[2]{0:T(128)} %pad_add_fusion.ids, bf16[512,1024]{1,0:T(8,128)(2,1)} %bitcast.23, bf16[512,512]{1,0:T(8,128)(2,1)} %bitcast.26), custom_call_target="tpu_custom_call" | custom-call | flops 345000000 | tf_op jit(solution)/shard_map/grad_late/pallas_call | solution.py:684
  124.5 2.8 %merge_early.1 = (f32[128,1024]{1,0:T(8,128)}, f32[96,256]{1,0:T(8,128)}, bf16[160,1024]{1,0:T(8,128)(2,1)}, bf16[160,1024]{1,0:T(8,128)(2,1)}, bf16[160,1024]{1,0:T(8,128)(2,1)}) custom-call(s32[2]{0:T(128)} %pad_add_fusion.ids, bf16[4,128,1024]{2,1,0:T(8,128)(2,1)} %get-tuple-element.119.mine, bf16[4,128,1024]{2,1,0:T(8,128)(2,1)} %copy-done, ...), custom_call_target="tpu_custom_call" | custom-call | flops 345000000 | tf_op jit(solution)/shard_map/merge_early/pallas_call | solution.py:684
  136.0 2.3 %merge_late.1 = (f32[128,512]{1,0:T(8,128)}, f32[128,256]{1,0:T(8,128)}, bf16[192,512]{1,0:T(8,128)(2,1)}, bf16[192,512]{1,0:T(8,128)(2,1)}, bf16[192,512]{1,0:T(8,128)(2,1)}) custom-call(s32[2]{0:T(128)} %pad_add_fusion.ids, bf16[4,128,512]{2,1,0:T(8,128)(2,1)} %get-tuple-element.131.mine, bf16[4,128,512]{2,1,0:T(8,128)(2,1)} %copy-done.3, ...), custom_call_target="tpu_custom_call" | custom-call | flops 345000000 | tf_op jit(solution)/shard_map/merge_late/pallas_call | solution.py:684
  140.0 5.8 %collective-permute-done.31.refs_1_ = bf16[160,1024]{1,0:T(8,128)(2,1)S(1)} collective-permute-done((bf16[160,1024]{1,0:T(8,128)(2,1)}, bf16[160,1024]{1,0:T(8,128)(2,1)S(1)}, u32[]{:S(2)}, u32[]{:S(2)}) %collective-permute-start.31) | collective-permute-done | bytes 327712 | tf_op jit(solution)/shard_map/ppermute | solution.py:35
  149.7 2.3 %final_early.1 = (f32[128,512]{1,0:T(8,128)}, f32[512,128]{1,0:T(8,128)}, f32[96,256]{1,0:T(8,128)}) custom-call(f32[128,1024]{1,0:T(8,128)} %get-tuple-element.123.own, f32[96,256]{1,0:T(8,128)} %get-tuple-element.124.part, bf16[160,1024]{1,0:T(8,128)(2,1)} %copy-done.5, bf16[160,1024]{1,0:T(8,128)(2,1)} %copy-done.6, bf16[160,1024]{1,0:T(8,128)(2,1)} %copy-done.7), custom_call_target="tpu_custom_call" | custom-call | flops 345000000 | tf_op jit(solution)/shard_map/final_early/pallas_call | solution.py:684
  152.1 4.4 %collective-permute-done.38.refs_1_ = bf16[192,512]{1,0:T(8,128)(2,1)} collective-permute-done((bf16[192,512]{1,0:T(8,128)(2,1)}, bf16[192,512]{1,0:T(8,128)(2,1)}, u32[]{:S(2)}, u32[]{:S(2)}) %collective-permute-start.38) | collective-permute-done | bytes 196640 | tf_op jit(solution)/shard_map/ppermute | solution.py:35
  156.5 2.3 %final_late.1 = (f32[128,2,512]{2,1,0:T(2,128)}, f32[128,256]{1,0:T(8,128)}) custom-call(f32[128,512]{1,0:T(8,128)} %get-tuple-element.135.own, f32[128,256]{1,0:T(8,128)} %get-tuple-element.136.part, f32[128,512]{1,0:T(8,128)} %get-tuple-element.137.grad_gate, bf16[192,512]{1,0:T(8,128)(2,1)} %copy-done.30, ...), custom_call_target="tpu_custom_call" | custom-call | flops 345000000 | tf_op jit(solution)/shard_map/final_late/pallas_call | solution.py:684
  159.3 2.4 %fusion.2 = (f32[2,256,256]{2,1,0:T(8,128)}, bf16[2,256,256]{2,1,0:T(8,128)(2,1)}) fusion(bf16[2,256,256]{2,1,0:T(8,128)(2,1)S(1)} %copy-done.8, bf16[2,256,256]{2,1,0:T(8,128)(2,1)} %collective-permute-done.24, f32[2,256,256]{2,1,0:T(8,128)S(1)} %copy-done.2, bf16[2,256,256]{2,1,0:T(8,128)(2,1)} %collective-permute-done.22, ...), kind=kLoop, calls=%fused_computation.4 | loop fusion | flops 2490368 | bytes 3675136 | tf_op jit(solution)/shard_map/add | solution.py:923
  (160 shorter events, 45.2 us)
Async XLA Ops:
  0.6 16.3 %collective-permute-start.1 = (bf16[2,256,256]{2,1,0:T(8,128)(2,1)}, bf16[2,256,256]{2,1,0:T(8,128)(2,1)S(1)}, u32[]{:S(2)}, u32[]{:S(2)}) collective-permute-start(bf16[2,256,256]{2,1,0:T(8,128)(2,1)} %refs_4_.3), channel_id=1, source_target_pairs={{0,2},{1,3},{2,0},{3,1},{4,6},{5,7},{6,4},{7,5},{8,10},{9,11},{10,... | collective-permute-start | bytes 786440 | tf_op jit(solution)/shard_map/ppermute | solution.py:35
  6.8 15.9 %collective-permute-start.3 = (bf16[128,1536]{1,0:T(8,128)(2,1)S(1)}, bf16[128,1536]{1,0:T(8,128)(2,1)S(1)}, u32[]{:S(2)}, u32[]{:S(2)}) collective-permute-start(bf16[128,1536]{1,0:T(8,128)(2,1)S(1)} %pad_maximum_fusion.refs_4_), channel_id=1, source_target_pairs={{0,8},{4,12},{8,0},{12,4},{16,24},{20,28},{24,16},{28,20},{1,9},{5... | collective-permute-start | bytes 1179656 | tf_op jit(solution)/shard_map/ppermute | solution.py:35
  8.3 18.7 %collective-permute-start.4 = (bf16[128,1536]{1,0:T(8,128)(2,1)S(1)}, bf16[128,1536]{1,0:T(8,128)(2,1)S(1)}, u32[]{:S(2)}, u32[]{:S(2)}) collective-permute-start(bf16[128,1536]{1,0:T(8,128)(2,1)S(1)} %pad_maximum_fusion.refs_4_), channel_id=1, source_target_pairs={{0,16},{4,20},{8,24},{12,28},{16,0},{20,4},{24,8},{28,12},{1,17},{... | collective-permute-start | bytes 1179656 | tf_op jit(solution)/shard_map/ppermute | solution.py:35
  9.9 17.2 %collective-permute-start.5 = (bf16[128,1536]{1,0:T(8,128)(2,1)S(1)}, bf16[128,1536]{1,0:T(8,128)(2,1)S(1)}, u32[]{:S(2)}, u32[]{:S(2)}) collective-permute-start(bf16[128,1536]{1,0:T(8,128)(2,1)S(1)} %pad_maximum_fusion.refs_4_), channel_id=1, source_target_pairs={{0,24},{4,28},{8,16},{12,20},{16,8},{20,12},{24,0},{28,4},{1,25},{... | collective-permute-start | bytes 1179656 | tf_op jit(solution)/shard_map/ppermute | solution.py:35
  10.3 12.3 %collective-permute-start = (bf16[2,256,256]{2,1,0:T(8,128)(2,1)}, bf16[2,256,256]{2,1,0:T(8,128)(2,1)S(1)}, u32[]{:S(2)}, u32[]{:S(2)}) collective-permute-start(bf16[2,256,256]{2,1,0:T(8,128)(2,1)} %refs_4_.3), channel_id=1, source_target_pairs={{0,1},{1,0},{2,3},{3,2},{4,5},{5,4},{6,7},{7,6},{8,9},{9,8},{10,11... | collective-permute-start | bytes 786440 | tf_op jit(solution)/shard_map/ppermute | solution.py:35
  17.0 10.5 %collective-permute-start.2 = (bf16[2,256,256]{2,1,0:T(8,128)(2,1)S(1)}, bf16[2,256,256]{2,1,0:T(8,128)(2,1)S(1)}, u32[]{:S(2)}, u32[]{:S(2)}) collective-permute-start(bf16[2,256,256]{2,1,0:T(8,128)(2,1)S(1)} %collective-permute-done.1.refs_2_.refs_6_), channel_id=1, source_target_pairs={{0,1},{1,0},{2,3},{3,2},{4,5},{5,4},{6,7},{7,6},{8,9},{9,8},{10,11... | collective-permute-start | bytes 786440 | tf_op jit(solution)/shard_map/ppermute | solution.py:35
  29.3 15.3 %collective-permute-start.17 = (bf16[2,256,256]{2,1,0:T(8,128)(2,1)}, bf16[2,256,256]{2,1,0:T(8,128)(2,1)S(1)}, u32[]{:S(2)}, u32[]{:S(2)}) collective-permute-start(bf16[2,256,256]{2,1,0:T(8,128)(2,1)} %refs_4_.2), channel_id=1, source_target_pairs={{0,2},{1,3},{2,0},{3,1},{4,6},{5,7},{6,4},{7,5},{8,10},{9,11},{10,... | collective-permute-start | bytes 786440 | tf_op jit(solution)/shard_map/ppermute | solution.py:35
  41.2 10.3 %collective-permute-start.11 = (bf16[2,96,256]{2,1,0:T(8,128)(2,1)}, bf16[2,96,256]{2,1,0:T(8,128)(2,1)S(1)}, u32[]{:S(2)}, u32[]{:S(2)}) collective-permute-start(bf16[2,96,256]{2,1,0:T(8,128)(2,1)} %get-tuple-element.87), channel_id=1, source_target_pairs={{0,2},{1,3},{2,0},{3,1},{4,6},{5,7},{6,4},{7,5},{8,10},{9,11},{10,... | collective-permute-start | bytes 294920 | tf_op jit(solution)/shard_map/ppermute | solution.py:35
  43.7 30.3 %collective-permute-start.16 = (bf16[2,256,256]{2,1,0:T(8,128)(2,1)S(1)}, bf16[2,256,256]{2,1,0:T(8,128)(2,1)S(1)}, u32[]{:S(2)}, u32[]{:S(2)}) collective-permute-start(bf16[2,256,256]{2,1,0:T(8,128)(2,1)S(1)} %copy-done.9), channel_id=1, source_target_pairs={{0,1},{1,0},{2,3},{3,2},{4,5},{5,4},{6,7},{7,6},{8,9},{9,8},{10,11... | collective-permute-start | bytes 786440 | tf_op jit(solution)/shard_map/ppermute | solution.py:35
  51.5 22.5 %collective-permute-start.18 = (bf16[2,256,256]{2,1,0:T(8,128)(2,1)S(1)}, bf16[2,256,256]{2,1,0:T(8,128)(2,1)S(1)}, u32[]{:S(2)}, u32[]{:S(2)}) collective-permute-start(bf16[2,256,256]{2,1,0:T(8,128)(2,1)S(1)} %collective-permute-done.17.refs_6_), channel_id=1, source_target_pairs={{0,1},{1,0},{2,3},{3,2},{4,5},{5,4},{6,7},{7,6},{8,9},{9,8},{10,11... | collective-permute-start | bytes 786440 | tf_op jit(solution)/shard_map/ppermute | solution.py:35
  69.6 26.8 %collective-permute-start.13 = (bf16[2,256,256]{2,1,0:T(8,128)(2,1)}, bf16[2,256,256]{2,1,0:T(8,128)(2,1)S(1)}, u32[]{:S(2)}, u32[]{:S(2)}) collective-permute-start(bf16[2,256,256]{2,1,0:T(8,128)(2,1)} %get-tuple-element.92), channel_id=1, source_target_pairs={{0,1},{1,0},{2,3},{3,2},{4,5},{5,4},{6,7},{7,6},{8,9},{9,8},{10,11... | collective-permute-start | bytes 786440 | tf_op jit(solution)/shard_map/ppermute | solution.py:35
  70.2 26.1 %collective-permute-start.14 = (bf16[2,256,256]{2,1,0:T(8,128)(2,1)}, bf16[2,256,256]{2,1,0:T(8,128)(2,1)S(1)}, u32[]{:S(2)}, u32[]{:S(2)}) collective-permute-start(bf16[2,256,256]{2,1,0:T(8,128)(2,1)} %get-tuple-element.93), channel_id=1, source_target_pairs={{0,2},{1,3},{2,0},{3,1},{4,6},{5,7},{6,4},{7,5},{8,10},{9,11},{10,... | collective-permute-start | bytes 786440 | tf_op jit(solution)/shard_map/ppermute | solution.py:35
  71.7 24.6 %collective-permute-start.15 = (bf16[2,256,256]{2,1,0:T(8,128)(2,1)}, bf16[2,256,256]{2,1,0:T(8,128)(2,1)S(1)}, u32[]{:S(2)}, u32[]{:S(2)}) collective-permute-start(bf16[2,256,256]{2,1,0:T(8,128)(2,1)} %get-tuple-element.94), channel_id=1, source_target_pairs={{0,3},{1,2},{2,1},{3,0},{4,7},{5,6},{6,5},{7,4},{8,11},{9,10},{10,... | collective-permute-start | bytes 786440 | tf_op jit(solution)/shard_map/ppermute | solution.py:35
  96.5 9.3 %collective-permute-start.20 = (bf16[2,96,256]{2,1,0:T(8,128)(2,1)}, bf16[2,96,256]{2,1,0:T(8,128)(2,1)S(1)}, u32[]{:S(2)}, u32[]{:S(2)}) collective-permute-start(bf16[2,96,256]{2,1,0:T(8,128)(2,1)} %get-tuple-element.105), channel_id=1, source_target_pairs={{0,2},{1,3},{2,0},{3,1},{4,6},{5,7},{6,4},{7,5},{8,10},{9,11},{10,... | collective-permute-start | bytes 294920 | tf_op jit(solution)/shard_map/ppermute | solution.py:35
  105.6 17.9 %collective-permute-start.28 = (bf16[4,128,1024]{2,1,0:T(8,128)(2,1)}, bf16[4,128,1024]{2,1,0:T(8,128)(2,1)S(1)}, u32[]{:S(2)}, u32[]{:S(2)}) collective-permute-start(bf16[4,128,1024]{2,1,0:T(8,128)(2,1)} %get-tuple-element.120), channel_id=1, source_target_pairs={{0,4},{4,0},{8,12},{12,8},{16,20},{20,16},{24,28},{28,24},{1,5},{5... | collective-permute-start | bytes 3145736 | tf_op jit(solution)/shard_map/ppermute | solution.py:35
  121.7 13.0 %collective-permute-start.34 = (bf16[4,128,512]{2,1,0:T(8,128)(2,1)}, bf16[4,128,512]{2,1,0:T(8,128)(2,1)S(1)}, u32[]{:S(2)}, u32[]{:S(2)}) collective-permute-start(bf16[4,128,512]{2,1,0:T(8,128)(2,1)} %get-tuple-element.132), channel_id=1, source_target_pairs={{0,4},{4,0},{8,12},{12,8},{16,20},{20,16},{24,28},{28,24},{1,5},{5... | collective-permute-start | bytes 1572872 | tf_op jit(solution)/shard_map/ppermute | solution.py:35
  121.9 9.7 %collective-permute-start.23 = (bf16[2,256,256]{2,1,0:T(8,128)(2,1)}, bf16[2,256,256]{2,1,0:T(8,128)(2,1)}, u32[]{:S(2)}, u32[]{:S(2)}) collective-permute-start(bf16[2,256,256]{2,1,0:T(8,128)(2,1)} %get-tuple-element.113), channel_id=1, source_target_pairs={{0,1},{1,0},{2,3},{3,2},{4,5},{5,4},{6,7},{7,6},{8,9},{9,8},{10,11... | collective-permute-start | bytes 786440 | tf_op jit(solution)/shard_map/ppermute | solution.py:35
  127.3 11.0 %collective-permute-start.30 = (bf16[160,1024]{1,0:T(8,128)(2,1)}, bf16[160,1024]{1,0:T(8,128)(2,1)S(1)}, u32[]{:S(2)}, u32[]{:S(2)}) collective-permute-start(bf16[160,1024]{1,0:T(8,128)(2,1)} %get-tuple-element.125), channel_id=1, source_target_pairs={{0,8},{4,12},{8,0},{12,4},{16,24},{20,28},{24,16},{28,20},{1,9},{5... | collective-permute-start | bytes 983048 | tf_op jit(solution)/shard_map/ppermute | solution.py:35
  128.9 16.9 %collective-permute-start.31 = (bf16[160,1024]{1,0:T(8,128)(2,1)}, bf16[160,1024]{1,0:T(8,128)(2,1)S(1)}, u32[]{:S(2)}, u32[]{:S(2)}) collective-permute-start(bf16[160,1024]{1,0:T(8,128)(2,1)} %get-tuple-element.126), channel_id=1, source_target_pairs={{0,16},{4,20},{8,24},{12,28},{16,0},{20,4},{24,8},{28,12},{1,17},{... | collective-permute-start | bytes 983048 | tf_op jit(solution)/shard_map/ppermute | solution.py:35
  130.3 17.1 %collective-permute-start.32 = (bf16[160,1024]{1,0:T(8,128)(2,1)}, bf16[160,1024]{1,0:T(8,128)(2,1)S(1)}, u32[]{:S(2)}, u32[]{:S(2)}) collective-permute-start(bf16[160,1024]{1,0:T(8,128)(2,1)} %get-tuple-element.127), channel_id=1, source_target_pairs={{0,24},{4,28},{8,16},{12,20},{16,8},{20,12},{24,0},{28,4},{1,25},{... | collective-permute-start | bytes 983048 | tf_op jit(solution)/shard_map/ppermute | solution.py:35
  133.4 25.9 %collective-permute-start.22 = (bf16[2,256,256]{2,1,0:T(8,128)(2,1)}, bf16[2,256,256]{2,1,0:T(8,128)(2,1)}, u32[]{:S(2)}, u32[]{:S(2)}) collective-permute-start(bf16[2,256,256]{2,1,0:T(8,128)(2,1)} %get-tuple-element.111), channel_id=1, source_target_pairs={{0,1},{1,0},{2,3},{3,2},{4,5},{5,4},{6,7},{7,6},{8,9},{9,8},{10,11... | collective-permute-start | bytes 786440 | tf_op jit(solution)/shard_map/ppermute | solution.py:35
  134.7 24.5 %collective-permute-start.24 = (bf16[2,256,256]{2,1,0:T(8,128)(2,1)}, bf16[2,256,256]{2,1,0:T(8,128)(2,1)}, u32[]{:S(2)}, u32[]{:S(2)}) collective-permute-start(bf16[2,256,256]{2,1,0:T(8,128)(2,1)} %add_convert_fusion), channel_id=1, source_target_pairs={{0,2},{1,3},{2,0},{3,1},{4,6},{5,7},{6,4},{7,5},{8,10},{9,11},{10,... | collective-permute-start | bytes 786440 | tf_op jit(solution)/shard_map/ppermute | solution.py:35
  138.3 13.7 %collective-permute-start.37 = (bf16[192,512]{1,0:T(8,128)(2,1)}, bf16[192,512]{1,0:T(8,128)(2,1)S(1)}, u32[]{:S(2)}, u32[]{:S(2)}) collective-permute-start(bf16[192,512]{1,0:T(8,128)(2,1)} %get-tuple-element.138), channel_id=1, source_target_pairs={{0,8},{4,12},{8,0},{12,4},{16,24},{20,28},{24,16},{28,20},{1,9},{5... | collective-permute-start | bytes 589832 | tf_op jit(solution)/shard_map/ppermute | solution.py:35
  145.8 10.7 %collective-permute-start.38 = (bf16[192,512]{1,0:T(8,128)(2,1)}, bf16[192,512]{1,0:T(8,128)(2,1)}, u32[]{:S(2)}, u32[]{:S(2)}) collective-permute-start(bf16[192,512]{1,0:T(8,128)(2,1)} %get-tuple-element.139), channel_id=1, source_target_pairs={{0,16},{4,20},{8,24},{12,28},{16,0},{20,4},{24,8},{28,12},{1,17},{... | collective-permute-start | bytes 589832 | tf_op jit(solution)/shard_map/ppermute | solution.py:35
  (57 other events, 461.5 us)

commit v4 on v3

--- a/solution.py
+++ b/solution.py
@@ -478,7 +478,7 @@
 SMEM = pl.BlockSpec(memory_space=pltpu.SMEM)
 
 
-def params(grid, mib=56):
+def params(grid, mib=64):
     return pltpu.CompilerParams(
         dimension_semantics=("arbitrary",) * grid, vmem_limit_bytes=mib * 1024 * 1024
     )
@@ -688,7 +688,7 @@
         out_specs=[whole(v.shape) for v in outs],
         out_shape=outs,
         scratch_shapes=list(scratch),
-        compiler_params=pltpu.CompilerParams(vmem_limit_bytes=56 * 1024 * 1024),
+        compiler_params=pltpu.CompilerParams(vmem_limit_bytes=64 * 1024 * 1024),
         cost_estimate=cost(0.3),
         name=name,
     )(*(() if ids is None else (ids,)), *operands)

time: 166 us -> 164 us (0.988)
  local copies, waits for them, and re-layouts: 8.45 us -> 5.15 us
  other arithmetic: 6.74 us -> 8.59 us
    unnamed x82 -> x24, local copies, waits for them, and re-layouts: 6.75 us -> 2.89 us
  transfers between devices with their start and end apart: 41 -> 41, of which waited for: 12 -> 13; matrix products, arithmetic and copies ran while one was open for 6% -> 8% of each run, Pallas kernels for 42% -> 43%
where the time goes in v4:
time: 164 us; the launch traced here: 163 us
  Pallas kernels  71.8 us (44%)
  starting transfers between devices  43.2 us (26%)
  waiting for transfers between devices  33.2 us (20%)
  other arithmetic  8.59 us (5%)
  local copies, waits for them, and re-layouts  5.15 us (3%)
    ppermute x41, starting transfers between devices, swap(): return lax.ppermute(value, axis, [(i, i ^ mask) for i in range(count)])  43.2 us
    ppermute x41, waiting for transfers between devices, swap(): return lax.ppermute(value, axis, [(i, i ^ mask) for i in range(count)])  33.2 us
    pallas_call x1, Pallas kernels, run_bwd(): pl.pallas_call(partial(bwd_kernel, parts), grid=(micro, blocks), in_specs...  21.5 us
    pallas_call x7, Pallas kernels, run_local(): pl.pallas_call(kernel, grid=(1,), in_specs=([SMEM] if ids is not None els...  18.8 us
    pallas_call x1, Pallas kernels, run_fwd(): pl.pallas_call(partial(fwd_kernel, parts), grid=(micro, tokens // span),...  16.2 us
    pallas_call x1, Pallas kernels, run_post(): pl.pallas_call(partial(post_kernel, parts), grid=(micro,), in_specs=[SMEM...  7.76 us
    pallas_call x1, Pallas kernels, run_pre(): pl.pallas_call(partial(pre_kernel, len(xs), len(ws)), grid=(micro,), in_s...  7.56 us
  transfers between devices with their start and end apart: 41, of which 13 were waited for; matrix products, arithmetic and copies ran while one was open for 8% of the time, Pallas kernels for 43%

profile of v4, /device:TPU:0, one launch (start us, length us, event | category | flops | bytes accessed | tf_op | source)
XLA Modules:
  0.0 162.9 jit_solution(1122369534824132121)
XLA Ops:
  0.6 4.1 %collective-permute-start.1 = (bf16[2,256,256]{2,1,0:T(8,128)(2,1)}, bf16[2,256,256]{2,1,0:T(8,128)(2,1)S(1)}, u32[]{:S(2)}, u32[]{:S(2)}) collective-permute-start(bf16[2,256,256]{2,1,0:T(8,128)(2,1)} %refs_4_.3), channel_id=1, source_target_pairs={{0,2},{1,3},{2,0},{3,1},{4,6},{5,7},{6,4},{7,5},{8,10},{9,11},{10,... | collective-permute-start | bytes 786440 | tf_op jit(solution)/shard_map/ppermute | solution.py:35
  11.9 5.1 %collective-permute-done.1.refs_2_.refs_6_ = bf16[2,256,256]{2,1,0:T(8,128)(2,1)S(1)} collective-permute-done((bf16[2,256,256]{2,1,0:T(8,128)(2,1)}, bf16[2,256,256]{2,1,0:T(8,128)(2,1)S(1)}, u32[]{:S(2)}, u32[]{:S(2)}) %collective-permute-start.1) | collective-permute-done | bytes 262176 | tf_op jit(solution)/shard_map/ppermute | solution.py:35
  17.8 4.9 %collective-permute-done.refs_1_.refs_5_ = bf16[2,256,256]{2,1,0:T(8,128)(2,1)S(1)} collective-permute-done((bf16[2,256,256]{2,1,0:T(8,128)(2,1)}, bf16[2,256,256]{2,1,0:T(8,128)(2,1)S(1)}, u32[]{:S(2)}, u32[]{:S(2)}) %collective-permute-start) | collective-permute-done | bytes 262176 | tf_op jit(solution)/shard_map/ppermute | solution.py:35
  22.7 4.4 %collective-permute-done.4.refs_6_ = bf16[128,1536]{1,0:T(8,128)(2,1)S(1)} collective-permute-done((bf16[128,1536]{1,0:T(8,128)(2,1)S(1)}, bf16[128,1536]{1,0:T(8,128)(2,1)S(1)}, u32[]{:S(2)}, u32[]{:S(2)}) %collective-permute-start.4) | collective-permute-done | bytes 393248 | tf_op jit(solution)/shard_map/ppermute | solution.py:35
  31.7 7.6 %pre.1 = (bf16[2,256,1024]{2,1,0:T(8,128)(2,1)}, bf16[1024,1536]{1,0:T(8,128)(2,1)}, f32[2,256,512]{2,1,0:T(8,128)}, f32[2,256,512]{2,1,0:T(8,128)}, f32[2,256,5...) custom-call(s32[2]{0:T(128)} %pad_add_fusion.ids, ...), custom_call_target="tpu_custom_call" | custom-call | flops 8049999872 | tf_op jit(solution)/shard_map/pre/pallas_call | solution.py:501
  39.3 2.1 %collective-permute-start.10 = (bf16[2,96,256]{2,1,0:T(8,128)(2,1)}, bf16[2,96,256]{2,1,0:T(8,128)(2,1)}, u32[]{:S(2)}, u32[]{:S(2)}) collective-permute-start(bf16[2,96,256]{2,1,0:T(8,128)(2,1)} %get-tuple-element.87), channel_id=1, source_target_pairs={{0,1},{1,0},{2,3},{3,2},{4,5},{5,4},{6,7},{7,6},{8,9},{9,8},{10,11... | collective-permute-start | bytes 294920 | tf_op jit(solution)/shard_map/ppermute | solution.py:35
  44.9 3.5 %collective-permute-done.10.refs_1_ = bf16[2,96,256]{2,1,0:T(8,128)(2,1)} collective-permute-done((bf16[2,96,256]{2,1,0:T(8,128)(2,1)}, bf16[2,96,256]{2,1,0:T(8,128)(2,1)}, u32[]{:S(2)}, u32[]{:S(2)}) %collective-permute-start.10) | collective-permute-done | bytes 98336 | tf_op jit(solution)/shard_map/ppermute | solution.py:35
  48.4 3.4 %collective-permute-done.11.refs_2_ = bf16[2,96,256]{2,1,0:T(8,128)(2,1)} collective-permute-done((bf16[2,96,256]{2,1,0:T(8,128)(2,1)}, bf16[2,96,256]{2,1,0:T(8,128)(2,1)}, u32[]{:S(2)}, u32[]{:S(2)}) %collective-permute-start.11) | collective-permute-done | bytes 98336 | tf_op jit(solution)/shard_map/ppermute | solution.py:35
  53.7 16.2 %scan_forward.1 = (f32[2,256,512]{2,1,0:T(8,128)}, f32[2,256,512]{2,1,0:T(8,128)}, bf16[2,256,512]{2,1,0:T(8,128)(2,1)}, f32[2,2,16,512]{3,2,1,0:T(8,128)}, bf16...) custom-call(s32[2]{0:T(128)} %pad_add_fusion.ids, ...), custom_call_target="tpu_custom_call" | custom-call | flops 18400000000 | tf_op jit(solution)/shard_map/scan_forward/pallas_call | solution.py:546
  70.0 2.0 %collective-permute-start.14 = (bf16[2,256,256]{2,1,0:T(8,128)(2,1)}, bf16[2,256,256]{2,1,0:T(8,128)(2,1)}, u32[]{:S(2)}, u32[]{:S(2)}) collective-permute-start(bf16[2,256,256]{2,1,0:T(8,128)(2,1)} %get-tuple-element.93), channel_id=1, source_target_pairs={{0,2},{1,3},{2,0},{3,1},{4,6},{5,7},{6,4},{7,5},{8,10},{9,11},{10,... | collective-permute-start | bytes 786440 | tf_op jit(solution)/shard_map/ppermute | solution.py:35
  72.0 2.3 %collective-permute-start.15 = (bf16[2,256,256]{2,1,0:T(8,128)(2,1)}, bf16[2,256,256]{2,1,0:T(8,128)(2,1)}, u32[]{:S(2)}, u32[]{:S(2)}) collective-permute-start(bf16[2,256,256]{2,1,0:T(8,128)(2,1)} %get-tuple-element.94), channel_id=1, source_target_pairs={{0,3},{1,2},{2,1},{3,0},{4,7},{5,6},{6,5},{7,4},{8,11},{9,10},{10,... | collective-permute-start | bytes 786440 | tf_op jit(solution)/shard_map/ppermute | solution.py:35
  74.3 21.5 %scan_backward.1 = (bf16[2,256,1024]{2,1,0:T(8,128)(2,1)}, f32[2,96,256]{2,1,0:T(8,128)}, bf16[2,96,256]{2,1,0:T(8,128)(2,1)}, f32[2,256,512]{2,1,0:T(8,128)}, b...) custom-call(s32[2]{0:T(128)} %pad_add_fusion.ids, s32[2]{0:T(128)} %bitcast.40, ...), custom_call_target="tpu_custom_call" | custom-call | flops 24149999616 | tf_op jit(solution)/shard_map/scan_backward/pallas_call | solution.py:595
  98.0 2.3 %collective-permute-start.21 = (bf16[2,96,256]{2,1,0:T(8,128)(2,1)}, bf16[2,96,256]{2,1,0:T(8,128)(2,1)}, u32[]{:S(2)}, u32[]{:S(2)}) collective-permute-start(bf16[2,96,256]{2,1,0:T(8,128)(2,1)} %get-tuple-element.105), channel_id=1, source_target_pairs={{0,3},{1,2},{2,1},{3,0},{4,7},{5,6},{6,5},{7,4},{8,11},{9,10},{10,... | collective-permute-start | bytes 294920 | tf_op jit(solution)/shard_map/ppermute | solution.py:35
  100.8 4.2 %grad_early.1 = (bf16[4,128,1024]{2,1,0:T(8,128)(2,1)}, bf16[4,128,1024]{2,1,0:T(8,128)(2,1)}) custom-call(s32[2]{0:T(128)} %pad_add_fusion.ids, bf16[512,1024]{1,0:T(8,128)(2,1)} %bitcast.22, bf16[512,1024]{1,0:T(8,128)(2,1)} %bitcast.25, bf16[512,512]{1,0:T(8,128)(2,1)} %bitcast.28, bf16[512,512]{1,0:T(8,128)(2,1)} %bitcast.29), custom_call_target="tpu_custom_call" | custom-call | flops 345000000 | tf_op jit(solution)/shard_map/grad_early/pallas_call | solution.py:684
  105.5 7.8 %post.1 = (bf16[2,256,512]{2,1,0:T(8,128)(2,1)}, f32[128,512]{1,0:T(8,128)}, f32[128,256]{1,0:T(8,128)}, f32[8,1024]{1,0:T(8,128)}, f32[2,256,256]{2,1,0:T(8,128...) custom-call(s32[2]{0:T(128)} %pad_add_fusion.ids, ...), custom_call_target="tpu_custom_call" | custom-call | flops 23000000512 | tf_op jit(solution)/shard_map/post/pallas_call | solution.py:636
  115.5 2.2 %collective-permute-start.27 = (f32[8,1024]{1,0:T(8,128)}, f32[8,1024]{1,0:T(8,128)}, u32[]{:S(2)}, u32[]{:S(2)}) collective-permute-start(f32[8,1024]{1,0:T(8,128)} %get-tuple-element.114), channel_id=1, source_target_pairs={{0,3},{1,2},{2,1},{3,0},{4,7},{5,6},{6,5},{7,4},{8,11},{9,10},{10,... | collective-permute-start | bytes 98312 | tf_op jit(solution)/shard_map/ppermute | solution.py:35
  117.7 3.0 %grad_late.1 = (bf16[4,128,512]{2,1,0:T(8,128)(2,1)}, bf16[4,128,512]{2,1,0:T(8,128)(2,1)}) custom-call(s32[2]{0:T(128)} %pad_add_fusion.ids, bf16[512,1024]{1,0:T(8,128)(2,1)} %bitcast.23, bf16[512,512]{1,0:T(8,128)(2,1)} %bitcast.26), custom_call_target="tpu_custom_call" | custom-call | flops 345000000 | tf_op jit(solution)/shard_map/grad_late/pallas_call | solution.py:684
  123.0 2.9 %merge_early.1 = (f32[128,1024]{1,0:T(8,128)}, f32[96,256]{1,0:T(8,128)}, bf16[160,1024]{1,0:T(8,128)(2,1)}, bf16[160,1024]{1,0:T(8,128)(2,1)}, bf16[160,1024]{1,0:T(8,128)(2,1)}) custom-call(s32[2]{0:T(128)} %pad_add_fusion.ids, bf16[4,128,1024]{2,1,0:T(8,128)(2,1)} %get-tuple-element.119.mine, bf16[4,128,1024]{2,1,0:T(8,128)(2,1)} %collective-permute-done.28.got, ...), custom_call_target="tpu_custom_call" | custom-call | flops 345000000 | tf_op jit(solution)/shard_map/merge_early/pallas_call | solution.py:684
  135.2 2.3 %merge_late.1 = (f32[128,512]{1,0:T(8,128)}, f32[128,256]{1,0:T(8,128)}, bf16[192,512]{1,0:T(8,128)(2,1)}, bf16[192,512]{1,0:T(8,128)(2,1)}, bf16[192,512]{1,0:T(8,128)(2,1)}) custom-call(s32[2]{0:T(128)} %pad_add_fusion.ids, bf16[4,128,512]{2,1,0:T(8,128)(2,1)} %get-tuple-element.131.mine, bf16[4,128,512]{2,1,0:T(8,128)(2,1)} %collective-permute-done.34.got, ...), custom_call_target="tpu_custom_call" | custom-call | flops 345000000 | tf_op jit(solution)/shard_map/merge_late/pallas_call | solution.py:684
  139.0 5.4 %collective-permute-done.31.refs_1_ = bf16[160,1024]{1,0:T(8,128)(2,1)} collective-permute-done((bf16[160,1024]{1,0:T(8,128)(2,1)}, bf16[160,1024]{1,0:T(8,128)(2,1)}, u32[]{:S(2)}, u32[]{:S(2)}) %collective-permute-start.31) | collective-permute-done | bytes 327712 | tf_op jit(solution)/shard_map/ppermute | solution.py:35
  148.9 2.3 %final_early.1 = (f32[128,512]{1,0:T(8,128)}, f32[512,128]{1,0:T(8,128)}, f32[96,256]{1,0:T(8,128)}) custom-call(f32[128,1024]{1,0:T(8,128)} %get-tuple-element.123.own, f32[96,256]{1,0:T(8,128)} %get-tuple-element.124.part, bf16[160,1024]{1,0:T(8,128)(2,1)} %collective-permute-done.30.refs_0_, bf16[160,1024]{1,0:T(8,128)(2,1)} %collective-permute-done.31.refs_1_, ...), custom_call_target="tpu_custom_call" | custom-call | flops 345000000 | tf_op jit(solution)/shard_map/final_early/pallas_call | solution.py:684
  151.2 3.9 %collective-permute-done.38.refs_1_ = bf16[192,512]{1,0:T(8,128)(2,1)} collective-permute-done((bf16[192,512]{1,0:T(8,128)(2,1)}, bf16[192,512]{1,0:T(8,128)(2,1)}, u32[]{:S(2)}, u32[]{:S(2)}) %collective-permute-start.38) | collective-permute-done | bytes 196640 | tf_op jit(solution)/shard_map/ppermute | solution.py:35
  155.1 2.3 %final_late.1 = (f32[128,2,512]{2,1,0:T(2,128)}, f32[128,256]{1,0:T(8,128)}) custom-call(f32[128,512]{1,0:T(8,128)} %get-tuple-element.135.own, f32[128,256]{1,0:T(8,128)} %get-tuple-element.136.part, f32[128,512]{1,0:T(8,128)} %get-tuple-element.137.grad_gate, bf16[192,512]{1,0:T(8,128)(2,1)} %collective-permute-done.37.refs_0_, ...), custom_call_target="tpu_custom_call" | custom-call | flops 345000000 | tf_op jit(solution)/shard_map/final_late/pallas_call | solution.py:684
  157.9 3.0 %fusion.2 = (f32[2,256,256]{2,1,0:T(8,128)}, bf16[2,256,256]{2,1,0:T(8,128)(2,1)}) fusion(bf16[2,256,256]{2,1,0:T(8,128)(2,1)} %refs_4_.3, bf16[2,256,256]{2,1,0:T(8,128)(2,1)} %collective-permute-done.24, f32[2,256,256]{2,1,0:T(8,128)} %get-tuple-element.110, bf16[2,256,256]{2,1,0:T(8,128)(2,1)} %collective-permute-done.22, bf16[2,256,256]{2,1,0:T(8,128)(2,1)} %refs_4_.2, ...), kind=kLoop, calls=%fused_computation.4 | loop fusion | flops 2490368 | bytes 3675136 | tf_op jit(solution)/shard_map/add | solution.py:923
  (102 shorter events, 43.4 us)
Async XLA Ops:
  0.6 16.3 %collective-permute-start.1 = (bf16[2,256,256]{2,1,0:T(8,128)(2,1)}, bf16[2,256,256]{2,1,0:T(8,128)(2,1)S(1)}, u32[]{:S(2)}, u32[]{:S(2)}) collective-permute-start(bf16[2,256,256]{2,1,0:T(8,128)(2,1)} %refs_4_.3), channel_id=1, source_target_pairs={{0,2},{1,3},{2,0},{3,1},{4,6},{5,7},{6,4},{7,5},{8,10},{9,11},{10,... | collective-permute-start | bytes 786440 | tf_op jit(solution)/shard_map/ppermute | solution.py:35
  6.8 15.9 %collective-permute-start.3 = (bf16[128,1536]{1,0:T(8,128)(2,1)S(1)}, bf16[128,1536]{1,0:T(8,128)(2,1)S(1)}, u32[]{:S(2)}, u32[]{:S(2)}) collective-permute-start(bf16[128,1536]{1,0:T(8,128)(2,1)S(1)} %pad_maximum_fusion.refs_4_), channel_id=1, source_target_pairs={{0,8},{4,12},{8,0},{12,4},{16,24},{20,28},{24,16},{28,20},{1,9},{5... | collective-permute-start | bytes 1179656 | tf_op jit(solution)/shard_map/ppermute | solution.py:35
  8.3 18.7 %collective-permute-start.4 = (bf16[128,1536]{1,0:T(8,128)(2,1)S(1)}, bf16[128,1536]{1,0:T(8,128)(2,1)S(1)}, u32[]{:S(2)}, u32[]{:S(2)}) collective-permute-start(bf16[128,1536]{1,0:T(8,128)(2,1)S(1)} %pad_maximum_fusion.refs_4_), channel_id=1, source_target_pairs={{0,16},{4,20},{8,24},{12,28},{16,0},{20,4},{24,8},{28,12},{1,17},{... | collective-permute-start | bytes 1179656 | tf_op jit(solution)/shard_map/ppermute | solution.py:35
  9.9 17.2 %collective-permute-start.5 = (bf16[128,1536]{1,0:T(8,128)(2,1)S(1)}, bf16[128,1536]{1,0:T(8,128)(2,1)S(1)}, u32[]{:S(2)}, u32[]{:S(2)}) collective-permute-start(bf16[128,1536]{1,0:T(8,128)(2,1)S(1)} %pad_maximum_fusion.refs_4_), channel_id=1, source_target_pairs={{0,24},{4,28},{8,16},{12,20},{16,8},{20,12},{24,0},{28,4},{1,25},{... | collective-permute-start | bytes 1179656 | tf_op jit(solution)/shard_map/ppermute | solution.py:35
  10.3 12.3 %collective-permute-start = (bf16[2,256,256]{2,1,0:T(8,128)(2,1)}, bf16[2,256,256]{2,1,0:T(8,128)(2,1)S(1)}, u32[]{:S(2)}, u32[]{:S(2)}) collective-permute-start(bf16[2,256,256]{2,1,0:T(8,128)(2,1)} %refs_4_.3), channel_id=1, source_target_pairs={{0,1},{1,0},{2,3},{3,2},{4,5},{5,4},{6,7},{7,6},{8,9},{9,8},{10,11... | collective-permute-start | bytes 786440 | tf_op jit(solution)/shard_map/ppermute | solution.py:35
  17.0 10.5 %collective-permute-start.2 = (bf16[2,256,256]{2,1,0:T(8,128)(2,1)S(1)}, bf16[2,256,256]{2,1,0:T(8,128)(2,1)S(1)}, u32[]{:S(2)}, u32[]{:S(2)}) collective-permute-start(bf16[2,256,256]{2,1,0:T(8,128)(2,1)S(1)} %collective-permute-done.1.refs_2_.refs_6_), channel_id=1, source_target_pairs={{0,1},{1,0},{2,3},{3,2},{4,5},{5,4},{6,7},{7,6},{8,9},{9,8},{10,11... | collective-permute-start | bytes 786440 | tf_op jit(solution)/shard_map/ppermute | solution.py:35
  29.2 15.7 %collective-permute-start.17 = (bf16[2,256,256]{2,1,0:T(8,128)(2,1)}, bf16[2,256,256]{2,1,0:T(8,128)(2,1)}, u32[]{:S(2)}, u32[]{:S(2)}) collective-permute-start(bf16[2,256,256]{2,1,0:T(8,128)(2,1)} %refs_4_.2), channel_id=1, source_target_pairs={{0,2},{1,3},{2,0},{3,1},{4,6},{5,7},{6,4},{7,5},{8,10},{9,11},{10,... | collective-permute-start | bytes 786440 | tf_op jit(solution)/shard_map/ppermute | solution.py:35
  41.4 10.4 %collective-permute-start.11 = (bf16[2,96,256]{2,1,0:T(8,128)(2,1)}, bf16[2,96,256]{2,1,0:T(8,128)(2,1)}, u32[]{:S(2)}, u32[]{:S(2)}) collective-permute-start(bf16[2,96,256]{2,1,0:T(8,128)(2,1)} %get-tuple-element.87), channel_id=1, source_target_pairs={{0,2},{1,3},{2,0},{3,1},{4,6},{5,7},{6,4},{7,5},{8,10},{9,11},{10,... | collective-permute-start | bytes 294920 | tf_op jit(solution)/shard_map/ppermute | solution.py:35
  43.8 30.5 %collective-permute-start.16 = (bf16[2,256,256]{2,1,0:T(8,128)(2,1)}, bf16[2,256,256]{2,1,0:T(8,128)(2,1)}, u32[]{:S(2)}, u32[]{:S(2)}) collective-permute-start(bf16[2,256,256]{2,1,0:T(8,128)(2,1)} %refs_4_.2), channel_id=1, source_target_pairs={{0,1},{1,0},{2,3},{3,2},{4,5},{5,4},{6,7},{7,6},{8,9},{9,8},{10,11... | collective-permute-start | bytes 786440 | tf_op jit(solution)/shard_map/ppermute | solution.py:35
  51.7 22.6 %collective-permute-start.18 = (bf16[2,256,256]{2,1,0:T(8,128)(2,1)}, bf16[2,256,256]{2,1,0:T(8,128)(2,1)}, u32[]{:S(2)}, u32[]{:S(2)}) collective-permute-start(bf16[2,256,256]{2,1,0:T(8,128)(2,1)} %collective-permute-done.17.refs_6_), channel_id=1, source_target_pairs={{0,1},{1,0},{2,3},{3,2},{4,5},{5,4},{6,7},{7,6},{8,9},{9,8},{10,11... | collective-permute-start | bytes 786440 | tf_op jit(solution)/shard_map/ppermute | solution.py:35
  69.9 25.9 %collective-permute-start.13 = (bf16[2,256,256]{2,1,0:T(8,128)(2,1)}, bf16[2,256,256]{2,1,0:T(8,128)(2,1)}, u32[]{:S(2)}, u32[]{:S(2)}) collective-permute-start(bf16[2,256,256]{2,1,0:T(8,128)(2,1)} %get-tuple-element.92), channel_id=1, source_target_pairs={{0,1},{1,0},{2,3},{3,2},{4,5},{5,4},{6,7},{7,6},{8,9},{9,8},{10,11... | collective-permute-start | bytes 786440 | tf_op jit(solution)/shard_map/ppermute | solution.py:35
  70.0 25.8 %collective-permute-start.14 = (bf16[2,256,256]{2,1,0:T(8,128)(2,1)}, bf16[2,256,256]{2,1,0:T(8,128)(2,1)}, u32[]{:S(2)}, u32[]{:S(2)}) collective-permute-start(bf16[2,256,256]{2,1,0:T(8,128)(2,1)} %get-tuple-element.93), channel_id=1, source_target_pairs={{0,2},{1,3},{2,0},{3,1},{4,6},{5,7},{6,4},{7,5},{8,10},{9,11},{10,... | collective-permute-start | bytes 786440 | tf_op jit(solution)/shard_map/ppermute | solution.py:35
  72.0 23.8 %collective-permute-start.15 = (bf16[2,256,256]{2,1,0:T(8,128)(2,1)}, bf16[2,256,256]{2,1,0:T(8,128)(2,1)}, u32[]{:S(2)}, u32[]{:S(2)}) collective-permute-start(bf16[2,256,256]{2,1,0:T(8,128)(2,1)} %get-tuple-element.94), channel_id=1, source_target_pairs={{0,3},{1,2},{2,1},{3,0},{4,7},{5,6},{6,5},{7,4},{8,11},{9,10},{10,... | collective-permute-start | bytes 786440 | tf_op jit(solution)/shard_map/ppermute | solution.py:35
  96.1 9.4 %collective-permute-start.20 = (bf16[2,96,256]{2,1,0:T(8,128)(2,1)}, bf16[2,96,256]{2,1,0:T(8,128)(2,1)}, u32[]{:S(2)}, u32[]{:S(2)}) collective-permute-start(bf16[2,96,256]{2,1,0:T(8,128)(2,1)} %get-tuple-element.105), channel_id=1, source_target_pairs={{0,2},{1,3},{2,0},{3,1},{4,6},{5,7},{6,4},{7,5},{8,10},{9,11},{10,... | collective-permute-start | bytes 294920 | tf_op jit(solution)/shard_map/ppermute | solution.py:35
  105.1 17.9 %collective-permute-start.28 = (bf16[4,128,1024]{2,1,0:T(8,128)(2,1)}, bf16[4,128,1024]{2,1,0:T(8,128)(2,1)}, u32[]{:S(2)}, u32[]{:S(2)}) collective-permute-start(bf16[4,128,1024]{2,1,0:T(8,128)(2,1)} %get-tuple-element.120), channel_id=1, source_target_pairs={{0,4},{4,0},{8,12},{12,8},{16,20},{20,16},{24,28},{28,24},{1,5},{5... | collective-permute-start | bytes 3145736 | tf_op jit(solution)/shard_map/ppermute | solution.py:35
  120.7 13.2 %collective-permute-start.34 = (bf16[4,128,512]{2,1,0:T(8,128)(2,1)}, bf16[4,128,512]{2,1,0:T(8,128)(2,1)}, u32[]{:S(2)}, u32[]{:S(2)}) collective-permute-start(bf16[4,128,512]{2,1,0:T(8,128)(2,1)} %get-tuple-element.132), channel_id=1, source_target_pairs={{0,4},{4,0},{8,12},{12,8},{16,20},{20,16},{24,28},{28,24},{1,5},{5... | collective-permute-start | bytes 1572872 | tf_op jit(solution)/shard_map/ppermute | solution.py:35
  120.9 9.8 %collective-permute-start.23 = (bf16[2,256,256]{2,1,0:T(8,128)(2,1)}, bf16[2,256,256]{2,1,0:T(8,128)(2,1)}, u32[]{:S(2)}, u32[]{:S(2)}) collective-permute-start(bf16[2,256,256]{2,1,0:T(8,128)(2,1)} %get-tuple-element.113), channel_id=1, source_target_pairs={{0,1},{1,0},{2,3},{3,2},{4,5},{5,4},{6,7},{7,6},{8,9},{9,8},{10,11... | collective-permute-start | bytes 786440 | tf_op jit(solution)/shard_map/ppermute | solution.py:35
  125.9 11.6 %collective-permute-start.30 = (bf16[160,1024]{1,0:T(8,128)(2,1)}, bf16[160,1024]{1,0:T(8,128)(2,1)}, u32[]{:S(2)}, u32[]{:S(2)}) collective-permute-start(bf16[160,1024]{1,0:T(8,128)(2,1)} %get-tuple-element.125), channel_id=1, source_target_pairs={{0,8},{4,12},{8,0},{12,4},{16,24},{20,28},{24,16},{28,20},{1,9},{5... | collective-permute-start | bytes 983048 | tf_op jit(solution)/shard_map/ppermute | solution.py:35
  127.4 17.0 %collective-permute-start.31 = (bf16[160,1024]{1,0:T(8,128)(2,1)}, bf16[160,1024]{1,0:T(8,128)(2,1)}, u32[]{:S(2)}, u32[]{:S(2)}) collective-permute-start(bf16[160,1024]{1,0:T(8,128)(2,1)} %get-tuple-element.126), channel_id=1, source_target_pairs={{0,16},{4,20},{8,24},{12,28},{16,0},{20,4},{24,8},{28,12},{1,17},{... | collective-permute-start | bytes 983048 | tf_op jit(solution)/shard_map/ppermute | solution.py:35
  128.9 17.2 %collective-permute-start.32 = (bf16[160,1024]{1,0:T(8,128)(2,1)}, bf16[160,1024]{1,0:T(8,128)(2,1)}, u32[]{:S(2)}, u32[]{:S(2)}) collective-permute-start(bf16[160,1024]{1,0:T(8,128)(2,1)} %get-tuple-element.127), channel_id=1, source_target_pairs={{0,24},{4,28},{8,16},{12,20},{16,8},{20,12},{24,0},{28,4},{1,25},{... | collective-permute-start | bytes 983048 | tf_op jit(solution)/shard_map/ppermute | solution.py:35
  132.5 25.4 %collective-permute-start.22 = (bf16[2,256,256]{2,1,0:T(8,128)(2,1)}, bf16[2,256,256]{2,1,0:T(8,128)(2,1)}, u32[]{:S(2)}, u32[]{:S(2)}) collective-permute-start(bf16[2,256,256]{2,1,0:T(8,128)(2,1)} %get-tuple-element.111), channel_id=1, source_target_pairs={{0,1},{1,0},{2,3},{3,2},{4,5},{5,4},{6,7},{7,6},{8,9},{9,8},{10,11... | collective-permute-start | bytes 786440 | tf_op jit(solution)/shard_map/ppermute | solution.py:35
  133.8 24.1 %collective-permute-start.24 = (bf16[2,256,256]{2,1,0:T(8,128)(2,1)}, bf16[2,256,256]{2,1,0:T(8,128)(2,1)}, u32[]{:S(2)}, u32[]{:S(2)}) collective-permute-start(bf16[2,256,256]{2,1,0:T(8,128)(2,1)} %add_convert_fusion), channel_id=1, source_target_pairs={{0,2},{1,3},{2,0},{3,1},{4,6},{5,7},{6,4},{7,5},{8,10},{9,11},{10,... | collective-permute-start | bytes 786440 | tf_op jit(solution)/shard_map/ppermute | solution.py:35
  137.5 13.7 %collective-permute-start.37 = (bf16[192,512]{1,0:T(8,128)(2,1)}, bf16[192,512]{1,0:T(8,128)(2,1)}, u32[]{:S(2)}, u32[]{:S(2)}) collective-permute-start(bf16[192,512]{1,0:T(8,128)(2,1)} %get-tuple-element.138), channel_id=1, source_target_pairs={{0,8},{4,12},{8,0},{12,4},{16,24},{20,28},{24,16},{28,20},{1,9},{5... | collective-permute-start | bytes 589832 | tf_op jit(solution)/shard_map/ppermute | solution.py:35
  144.4 10.7 %collective-permute-start.38 = (bf16[192,512]{1,0:T(8,128)(2,1)}, bf16[192,512]{1,0:T(8,128)(2,1)}, u32[]{:S(2)}, u32[]{:S(2)}) collective-permute-start(bf16[192,512]{1,0:T(8,128)(2,1)} %get-tuple-element.139), channel_id=1, source_target_pairs={{0,16},{4,20},{8,24},{12,28},{16,0},{20,4},{24,8},{28,12},{1,17},{... | collective-permute-start | bytes 589832 | tf_op jit(solution)/shard_map/ppermute | solution.py:35
  (28 other events, 144.9 us)

commit v5 on v4

--- a/solution.py
+++ b/solution.py
@@ -829,7 +829,7 @@
     d_inner, small, small_theirs, tiny, own_norm, *norm_terms = run_post(
         ids, d_projs, xs, d_scan, d_gate, u_act, summed, inner, inv, w_full, gain, xw_t, conv_weight
     )
-    tiny_got = others(tiny, "tensor")
+    tiny_got = others(after(tiny, sends) if chips else tiny, "tensor")
     near = parts // 2
     halves = [own_norm] + norm_terms
     passed = [swap(halves[k], "tensor", k) for k in range(1, near)]

time: 164 us -> 163 us (level)
  waiting for transfers between devices: 33.2 us -> 29.3 us
  starting transfers between devices: 43.2 us -> 45.6 us
    ppermute x41, waiting for transfers between devices: 33.2 us -> 29.3 us  [swap(): return lax.ppermute(value, axis, [(i, i ^ mask) for i in range(count)])]
    ppermute x41, starting transfers between devices: 43.2 us -> 45.6 us  [swap(): return lax.ppermute(value, axis, [(i, i ^ mask) for i in range(count)])]
    unnamed x24 -> x28, local copies, waits for them, and re-layouts: 2.89 us -> 4.09 us
where the time goes in v5:
time: 163 us; the launch traced here: 162 us
  Pallas kernels  71.8 us (44%)
  starting transfers between devices  45.6 us (28%)
  waiting for transfers between devices  29.3 us (18%)
  other arithmetic  7.91 us (5%)
  local copies, waits for them, and re-layouts  6.36 us (4%)
    ppermute x41, starting transfers between devices, swap(): return lax.ppermute(value, axis, [(i, i ^ mask) for i in range(count)])  45.6 us
    ppermute x41, waiting for transfers between devices, swap(): return lax.ppermute(value, axis, [(i, i ^ mask) for i in range(count)])  29.3 us
    pallas_call x1, Pallas kernels, run_bwd(): pl.pallas_call(partial(bwd_kernel, parts), grid=(micro, blocks), in_specs...  21.5 us
    pallas_call x7, Pallas kernels, run_local(): pl.pallas_call(kernel, grid=(1,), in_specs=([SMEM] if ids is not None els...  18.9 us
    pallas_call x1, Pallas kernels, run_fwd(): pl.pallas_call(partial(fwd_kernel, parts), grid=(micro, tokens // span),...  16.2 us
    pallas_call x1, Pallas kernels, run_post(): pl.pallas_call(partial(post_kernel, parts), grid=(micro,), in_specs=[SMEM...  7.76 us
    pallas_call x1, Pallas kernels, run_pre(): pl.pallas_call(partial(pre_kernel, len(xs), len(ws)), grid=(micro,), in_s...  7.61 us
    unnamed x28, local copies, waits for them, and re-layouts  4.09 us
  transfers between devices with their start and end apart: 41, of which 13 were waited for; matrix products, arithmetic and copies ran while one was open for 8% of the time, Pallas kernels for 43%

profile of v5, /device:TPU:0, one launch (start us, length us, event | category | flops | bytes accessed | tf_op | source)
XLA Modules:
  0.0 162.0 jit_solution(482279194936987961)
XLA Ops:
  0.6 4.1 %collective-permute-start.1 = (bf16[2,256,256]{2,1,0:T(8,128)(2,1)}, bf16[2,256,256]{2,1,0:T(8,128)(2,1)S(1)}, u32[]{:S(2)}, u32[]{:S(2)}) collective-permute-start(bf16[2,256,256]{2,1,0:T(8,128)(2,1)} %refs_4_.3), channel_id=1, source_target_pairs={{0,2},{1,3},{2,0},{3,1},{4,6},{5,7},{6,4},{7,5},{8,10},{9,11},{10,... | collective-permute-start | bytes 786440 | tf_op jit(solution)/shard_map/ppermute | solution.py:35
  11.9 5.1 %collective-permute-done.1.refs_2_.refs_6_ = bf16[2,256,256]{2,1,0:T(8,128)(2,1)S(1)} collective-permute-done((bf16[2,256,256]{2,1,0:T(8,128)(2,1)}, bf16[2,256,256]{2,1,0:T(8,128)(2,1)S(1)}, u32[]{:S(2)}, u32[]{:S(2)}) %collective-permute-start.1) | collective-permute-done | bytes 262176 | tf_op jit(solution)/shard_map/ppermute | solution.py:35
  17.8 4.9 %collective-permute-done.refs_1_.refs_5_ = bf16[2,256,256]{2,1,0:T(8,128)(2,1)S(1)} collective-permute-done((bf16[2,256,256]{2,1,0:T(8,128)(2,1)}, bf16[2,256,256]{2,1,0:T(8,128)(2,1)S(1)}, u32[]{:S(2)}, u32[]{:S(2)}) %collective-permute-start) | collective-permute-done | bytes 262176 | tf_op jit(solution)/shard_map/ppermute | solution.py:35
  22.7 4.4 %collective-permute-done.4.refs_6_ = bf16[128,1536]{1,0:T(8,128)(2,1)S(1)} collective-permute-done((bf16[128,1536]{1,0:T(8,128)(2,1)S(1)}, bf16[128,1536]{1,0:T(8,128)(2,1)S(1)}, u32[]{:S(2)}, u32[]{:S(2)}) %collective-permute-start.4) | collective-permute-done | bytes 393248 | tf_op jit(solution)/shard_map/ppermute | solution.py:35
  31.7 7.6 %pre.1 = (bf16[2,256,1024]{2,1,0:T(8,128)(2,1)}, bf16[1024,1536]{1,0:T(8,128)(2,1)}, f32[2,256,512]{2,1,0:T(8,128)}, f32[2,256,512]{2,1,0:T(8,128)}, f32[2,256,5...) custom-call(s32[2]{0:T(128)} %pad_add_fusion.ids, ...), custom_call_target="tpu_custom_call" | custom-call | flops 8049999872 | tf_op jit(solution)/shard_map/pre/pallas_call | solution.py:501
  44.8 3.6 %collective-permute-done.10.refs_1_ = bf16[2,96,256]{2,1,0:T(8,128)(2,1)} collective-permute-done((bf16[2,96,256]{2,1,0:T(8,128)(2,1)}, bf16[2,96,256]{2,1,0:T(8,128)(2,1)}, u32[]{:S(2)}, u32[]{:S(2)}) %collective-permute-start.10) | collective-permute-done | bytes 98336 | tf_op jit(solution)/shard_map/ppermute | solution.py:35
  48.4 3.3 %collective-permute-done.11.refs_2_ = bf16[2,96,256]{2,1,0:T(8,128)(2,1)} collective-permute-done((bf16[2,96,256]{2,1,0:T(8,128)(2,1)}, bf16[2,96,256]{2,1,0:T(8,128)(2,1)}, u32[]{:S(2)}, u32[]{:S(2)}) %collective-permute-start.11) | collective-permute-done | bytes 98336 | tf_op jit(solution)/shard_map/ppermute | solution.py:35
  53.7 16.2 %scan_forward.1 = (f32[2,256,512]{2,1,0:T(8,128)}, f32[2,256,512]{2,1,0:T(8,128)}, bf16[2,256,512]{2,1,0:T(8,128)(2,1)}, f32[2,2,16,512]{3,2,1,0:T(8,128)}, bf16...) custom-call(s32[2]{0:T(128)} %pad_add_fusion.ids, ...), custom_call_target="tpu_custom_call" | custom-call | flops 18400000000 | tf_op jit(solution)/shard_map/scan_forward/pallas_call | solution.py:546
  71.9 2.3 %collective-permute-start.15 = (bf16[2,256,256]{2,1,0:T(8,128)(2,1)}, bf16[2,256,256]{2,1,0:T(8,128)(2,1)}, u32[]{:S(2)}, u32[]{:S(2)}) collective-permute-start(bf16[2,256,256]{2,1,0:T(8,128)(2,1)} %get-tuple-element.95), channel_id=1, source_target_pairs={{0,3},{1,2},{2,1},{3,0},{4,7},{5,6},{6,5},{7,4},{8,11},{9,10},{10,... | collective-permute-start | bytes 786440 | tf_op jit(solution)/shard_map/ppermute | solution.py:35
  74.3 21.5 %scan_backward.1 = (bf16[2,256,1024]{2,1,0:T(8,128)(2,1)}, f32[2,96,256]{2,1,0:T(8,128)}, bf16[2,96,256]{2,1,0:T(8,128)(2,1)}, f32[2,256,512]{2,1,0:T(8,128)}, b...) custom-call(s32[2]{0:T(128)} %pad_add_fusion.ids, s32[2]{0:T(128)} %bitcast.40, ...), custom_call_target="tpu_custom_call" | custom-call | flops 24149999616 | tf_op jit(solution)/shard_map/scan_backward/pallas_call | solution.py:595
  97.9 2.3 %collective-permute-start.21 = (bf16[2,96,256]{2,1,0:T(8,128)(2,1)}, bf16[2,96,256]{2,1,0:T(8,128)(2,1)}, u32[]{:S(2)}, u32[]{:S(2)}) collective-permute-start(bf16[2,96,256]{2,1,0:T(8,128)(2,1)} %get-tuple-element.106), channel_id=1, source_target_pairs={{0,3},{1,2},{2,1},{3,0},{4,7},{5,6},{6,5},{7,4},{8,11},{9,10},{10,... | collective-permute-start | bytes 294920 | tf_op jit(solution)/shard_map/ppermute | solution.py:35
  100.8 4.3 %grad_early.1 = (bf16[4,128,1024]{2,1,0:T(8,128)(2,1)}, bf16[4,128,1024]{2,1,0:T(8,128)(2,1)}) custom-call(s32[2]{0:T(128)} %pad_add_fusion.ids, bf16[512,1024]{1,0:T(8,128)(2,1)} %bitcast.22, bf16[512,1024]{1,0:T(8,128)(2,1)} %bitcast.25, bf16[512,512]{1,0:T(8,128)(2,1)} %bitcast.28, bf16[512,512]{1,0:T(8,128)(2,1)} %bitcast.29), custom_call_target="tpu_custom_call" | custom-call | flops 345000000 | tf_op jit(solution)/shard_map/grad_early/pallas_call | solution.py:684
  105.4 7.8 %post.1 = (bf16[2,256,512]{2,1,0:T(8,128)(2,1)}, f32[128,512]{1,0:T(8,128)}, f32[128,256]{1,0:T(8,128)}, f32[8,1024]{1,0:T(8,128)}, f32[2,256,256]{2,1,0:T(8,128...) custom-call(s32[2]{0:T(128)} %pad_add_fusion.ids, ...), custom_call_target="tpu_custom_call" | custom-call | flops 23000000512 | tf_op jit(solution)/shard_map/post/pallas_call | solution.py:636
  113.4 3.0 %grad_late.1 = (bf16[4,128,512]{2,1,0:T(8,128)(2,1)}, bf16[4,128,512]{2,1,0:T(8,128)(2,1)}) custom-call(s32[2]{0:T(128)} %pad_add_fusion.ids, bf16[512,1024]{1,0:T(8,128)(2,1)} %bitcast.23, bf16[512,512]{1,0:T(8,128)(2,1)} %bitcast.26), custom_call_target="tpu_custom_call" | custom-call | flops 345000000 | tf_op jit(solution)/shard_map/grad_late/pallas_call | solution.py:684
  118.3 2.9 %merge_early.1 = (f32[128,1024]{1,0:T(8,128)}, f32[96,256]{1,0:T(8,128)}, bf16[160,1024]{1,0:T(8,128)(2,1)}, bf16[160,1024]{1,0:T(8,128)(2,1)}, bf16[160,1024]{1,0:T(8,128)(2,1)}) custom-call(s32[2]{0:T(128)} %pad_add_fusion.ids, bf16[4,128,1024]{2,1,0:T(8,128)(2,1)} %get-tuple-element.120.mine, bf16[4,128,1024]{2,1,0:T(8,128)(2,1)} %collective-permute-done.25.got, ...), custom_call_target="tpu_custom_call" | custom-call | flops 345000000 | tf_op jit(solution)/shard_map/merge_early/pallas_call | solution.py:684
  123.1 2.4 %collective-permute-start.29 = (f32[8,1024]{1,0:T(8,128)}, f32[8,1024]{1,0:T(8,128)S(1)}, u32[]{:S(2)}, u32[]{:S(2)}) collective-permute-start(f32[8,1024]{1,0:T(8,128)} %get-tuple-element.127), channel_id=1, source_target_pairs={{0,3},{1,2},{2,1},{3,0},{4,7},{5,6},{6,5},{7,4},{8,11},{9,10},{10,... | collective-permute-start | bytes 98312 | tf_op jit(solution)/shard_map/ppermute | solution.py:35
  135.4 3.0 %collective-permute-start.24 = (bf16[2,256,256]{2,1,0:T(8,128)(2,1)}, bf16[2,256,256]{2,1,0:T(8,128)(2,1)}, u32[]{:S(2)}, u32[]{:S(2)}) collective-permute-start(bf16[2,256,256]{2,1,0:T(8,128)(2,1)} %add_convert_fusion), channel_id=1, source_target_pairs={{0,2},{1,3},{2,0},{3,1},{4,6},{5,7},{6,4},{7,5},{8,10},{9,11},{10,... | collective-permute-start | bytes 786440 | tf_op jit(solution)/shard_map/ppermute | solution.py:35
  138.4 2.3 %merge_late.1 = (f32[128,512]{1,0:T(8,128)}, f32[128,256]{1,0:T(8,128)}, bf16[192,512]{1,0:T(8,128)(2,1)}, bf16[192,512]{1,0:T(8,128)(2,1)}, bf16[192,512]{1,0:T(8,128)(2,1)}) custom-call(s32[2]{0:T(128)} %pad_add_fusion.ids, bf16[4,128,512]{2,1,0:T(8,128)(2,1)} %get-tuple-element.133.mine, bf16[4,128,512]{2,1,0:T(8,128)(2,1)} %collective-permute-done.34.got, ...), custom_call_target="tpu_custom_call" | custom-call | flops 345000000 | tf_op jit(solution)/shard_map/merge_late/pallas_call | solution.py:684
  141.2 2.9 %collective-permute-done.31.refs_1_ = bf16[160,1024]{1,0:T(8,128)(2,1)} collective-permute-done((bf16[160,1024]{1,0:T(8,128)(2,1)}, bf16[160,1024]{1,0:T(8,128)(2,1)}, u32[]{:S(2)}, u32[]{:S(2)}) %collective-permute-start.31) | collective-permute-done | bytes 327712 | tf_op jit(solution)/shard_map/ppermute | solution.py:35
  144.1 2.5 %collective-permute-start.38 = (bf16[192,512]{1,0:T(8,128)(2,1)}, bf16[192,512]{1,0:T(8,128)(2,1)}, u32[]{:S(2)}, u32[]{:S(2)}) collective-permute-start(bf16[192,512]{1,0:T(8,128)(2,1)} %get-tuple-element.141), channel_id=1, source_target_pairs={{0,16},{4,20},{8,24},{12,28},{16,0},{20,4},{24,8},{28,12},{1,17},{... | collective-permute-start | bytes 589832 | tf_op jit(solution)/shard_map/ppermute | solution.py:35
  149.3 2.4 %final_early.1 = (f32[128,512]{1,0:T(8,128)}, f32[512,128]{1,0:T(8,128)}, f32[96,256]{1,0:T(8,128)}) custom-call(f32[128,1024]{1,0:T(8,128)} %get-tuple-element.128.own, f32[96,256]{1,0:T(8,128)} %get-tuple-element.129.part, bf16[160,1024]{1,0:T(8,128)(2,1)} %collective-permute-done.30.refs_0_, bf16[160,1024]{1,0:T(8,128)(2,1)} %collective-permute-done.31.refs_1_, ...), custom_call_target="tpu_custom_call" | custom-call | flops 345000000 | tf_op jit(solution)/shard_map/final_early/pallas_call | solution.py:684
  151.7 2.5 %collective-permute-done.38.refs_1_ = bf16[192,512]{1,0:T(8,128)(2,1)} collective-permute-done((bf16[192,512]{1,0:T(8,128)(2,1)}, bf16[192,512]{1,0:T(8,128)(2,1)}, u32[]{:S(2)}, u32[]{:S(2)}) %collective-permute-start.38) | collective-permute-done | bytes 196640 | tf_op jit(solution)/shard_map/ppermute | solution.py:35
  154.2 2.3 %final_late.1 = (f32[128,2,512]{2,1,0:T(2,128)}, f32[128,256]{1,0:T(8,128)}) custom-call(f32[128,512]{1,0:T(8,128)} %get-tuple-element.137.own, f32[128,256]{1,0:T(8,128)} %get-tuple-element.138.part, f32[128,512]{1,0:T(8,128)} %get-tuple-element.139.grad_gate, bf16[192,512]{1,0:T(8,128)(2,1)} %collective-permute-done.37.refs_0_, ...), custom_call_target="tpu_custom_call" | custom-call | flops 345000000 | tf_op jit(solution)/shard_map/final_late/pallas_call | solution.py:684
  157.0 3.0 %fusion.2 = (f32[2,256,256]{2,1,0:T(8,128)}, bf16[2,256,256]{2,1,0:T(8,128)(2,1)}) fusion(bf16[2,256,256]{2,1,0:T(8,128)(2,1)} %refs_4_.3, bf16[2,256,256]{2,1,0:T(8,128)(2,1)} %collective-permute-done.24, f32[2,256,256]{2,1,0:T(8,128)} %get-tuple-element.111, bf16[2,256,256]{2,1,0:T(8,128)(2,1)} %collective-permute-done.22, bf16[2,256,256]{2,1,0:T(8,128)(2,1)} %refs_4_.2, ...), kind=kLoop, calls=%fused_computation.4 | loop fusion | flops 2490368 | bytes 3675136 | tf_op jit(solution)/shard_map/add | solution.py:923
  (106 shorter events, 44.7 us)
Async XLA Ops:
  0.6 16.3 %collective-permute-start.1 = (bf16[2,256,256]{2,1,0:T(8,128)(2,1)}, bf16[2,256,256]{2,1,0:T(8,128)(2,1)S(1)}, u32[]{:S(2)}, u32[]{:S(2)}) collective-permute-start(bf16[2,256,256]{2,1,0:T(8,128)(2,1)} %refs_4_.3), channel_id=1, source_target_pairs={{0,2},{1,3},{2,0},{3,1},{4,6},{5,7},{6,4},{7,5},{8,10},{9,11},{10,... | collective-permute-start | bytes 786440 | tf_op jit(solution)/shard_map/ppermute | solution.py:35
  6.8 15.9 %collective-permute-start.3 = (bf16[128,1536]{1,0:T(8,128)(2,1)S(1)}, bf16[128,1536]{1,0:T(8,128)(2,1)S(1)}, u32[]{:S(2)}, u32[]{:S(2)}) collective-permute-start(bf16[128,1536]{1,0:T(8,128)(2,1)S(1)} %pad_maximum_fusion.refs_4_), channel_id=1, source_target_pairs={{0,8},{4,12},{8,0},{12,4},{16,24},{20,28},{24,16},{28,20},{1,9},{5... | collective-permute-start | bytes 1179656 | tf_op jit(solution)/shard_map/ppermute | solution.py:35
  8.3 18.7 %collective-permute-start.4 = (bf16[128,1536]{1,0:T(8,128)(2,1)S(1)}, bf16[128,1536]{1,0:T(8,128)(2,1)S(1)}, u32[]{:S(2)}, u32[]{:S(2)}) collective-permute-start(bf16[128,1536]{1,0:T(8,128)(2,1)S(1)} %pad_maximum_fusion.refs_4_), channel_id=1, source_target_pairs={{0,16},{4,20},{8,24},{12,28},{16,0},{20,4},{24,8},{28,12},{1,17},{... | collective-permute-start | bytes 1179656 | tf_op jit(solution)/shard_map/ppermute | solution.py:35
  9.9 17.2 %collective-permute-start.5 = (bf16[128,1536]{1,0:T(8,128)(2,1)S(1)}, bf16[128,1536]{1,0:T(8,128)(2,1)S(1)}, u32[]{:S(2)}, u32[]{:S(2)}) collective-permute-start(bf16[128,1536]{1,0:T(8,128)(2,1)S(1)} %pad_maximum_fusion.refs_4_), channel_id=1, source_target_pairs={{0,24},{4,28},{8,16},{12,20},{16,8},{20,12},{24,0},{28,4},{1,25},{... | collective-permute-start | bytes 1179656 | tf_op jit(solution)/shard_map/ppermute | solution.py:35
  10.3 12.3 %collective-permute-start = (bf16[2,256,256]{2,1,0:T(8,128)(2,1)}, bf16[2,256,256]{2,1,0:T(8,128)(2,1)S(1)}, u32[]{:S(2)}, u32[]{:S(2)}) collective-permute-start(bf16[2,256,256]{2,1,0:T(8,128)(2,1)} %refs_4_.3), channel_id=1, source_target_pairs={{0,1},{1,0},{2,3},{3,2},{4,5},{5,4},{6,7},{7,6},{8,9},{9,8},{10,11... | collective-permute-start | bytes 786440 | tf_op jit(solution)/shard_map/ppermute | solution.py:35
  17.0 10.5 %collective-permute-start.2 = (bf16[2,256,256]{2,1,0:T(8,128)(2,1)S(1)}, bf16[2,256,256]{2,1,0:T(8,128)(2,1)S(1)}, u32[]{:S(2)}, u32[]{:S(2)}) collective-permute-start(bf16[2,256,256]{2,1,0:T(8,128)(2,1)S(1)} %collective-permute-done.1.refs_2_.refs_6_), channel_id=1, source_target_pairs={{0,1},{1,0},{2,3},{3,2},{4,5},{5,4},{6,7},{7,6},{8,9},{9,8},{10,11... | collective-permute-start | bytes 786440 | tf_op jit(solution)/shard_map/ppermute | solution.py:35
  29.1 15.7 %collective-permute-start.17 = (bf16[2,256,256]{2,1,0:T(8,128)(2,1)}, bf16[2,256,256]{2,1,0:T(8,128)(2,1)}, u32[]{:S(2)}, u32[]{:S(2)}) collective-permute-start(bf16[2,256,256]{2,1,0:T(8,128)(2,1)} %refs_4_.2), channel_id=1, source_target_pairs={{0,2},{1,3},{2,0},{3,1},{4,6},{5,7},{6,4},{7,5},{8,10},{9,11},{10,... | collective-permute-start | bytes 786440 | tf_op jit(solution)/shard_map/ppermute | solution.py:35
  41.3 10.4 %collective-permute-start.11 = (bf16[2,96,256]{2,1,0:T(8,128)(2,1)}, bf16[2,96,256]{2,1,0:T(8,128)(2,1)}, u32[]{:S(2)}, u32[]{:S(2)}) collective-permute-start(bf16[2,96,256]{2,1,0:T(8,128)(2,1)} %get-tuple-element.88), channel_id=1, source_target_pairs={{0,2},{1,3},{2,0},{3,1},{4,6},{5,7},{6,4},{7,5},{8,10},{9,11},{10,... | collective-permute-start | bytes 294920 | tf_op jit(solution)/shard_map/ppermute | solution.py:35
  43.8 30.5 %collective-permute-start.16 = (bf16[2,256,256]{2,1,0:T(8,128)(2,1)}, bf16[2,256,256]{2,1,0:T(8,128)(2,1)}, u32[]{:S(2)}, u32[]{:S(2)}) collective-permute-start(bf16[2,256,256]{2,1,0:T(8,128)(2,1)} %refs_4_.2), channel_id=1, source_target_pairs={{0,1},{1,0},{2,3},{3,2},{4,5},{5,4},{6,7},{7,6},{8,9},{9,8},{10,11... | collective-permute-start | bytes 786440 | tf_op jit(solution)/shard_map/ppermute | solution.py:35
  51.7 22.6 %collective-permute-start.18 = (bf16[2,256,256]{2,1,0:T(8,128)(2,1)}, bf16[2,256,256]{2,1,0:T(8,128)(2,1)}, u32[]{:S(2)}, u32[]{:S(2)}) collective-permute-start(bf16[2,256,256]{2,1,0:T(8,128)(2,1)} %collective-permute-done.17.refs_6_), channel_id=1, source_target_pairs={{0,1},{1,0},{2,3},{3,2},{4,5},{5,4},{6,7},{7,6},{8,9},{9,8},{10,11... | collective-permute-start | bytes 786440 | tf_op jit(solution)/shard_map/ppermute | solution.py:35
  69.8 25.9 %collective-permute-start.13 = (bf16[2,256,256]{2,1,0:T(8,128)(2,1)}, bf16[2,256,256]{2,1,0:T(8,128)(2,1)}, u32[]{:S(2)}, u32[]{:S(2)}) collective-permute-start(bf16[2,256,256]{2,1,0:T(8,128)(2,1)} %get-tuple-element.93), channel_id=1, source_target_pairs={{0,1},{1,0},{2,3},{3,2},{4,5},{5,4},{6,7},{7,6},{8,9},{9,8},{10,11... | collective-permute-start | bytes 786440 | tf_op jit(solution)/shard_map/ppermute | solution.py:35
  70.0 25.8 %collective-permute-start.14 = (bf16[2,256,256]{2,1,0:T(8,128)(2,1)}, bf16[2,256,256]{2,1,0:T(8,128)(2,1)}, u32[]{:S(2)}, u32[]{:S(2)}) collective-permute-start(bf16[2,256,256]{2,1,0:T(8,128)(2,1)} %get-tuple-element.94), channel_id=1, source_target_pairs={{0,2},{1,3},{2,0},{3,1},{4,6},{5,7},{6,4},{7,5},{8,10},{9,11},{10,... | collective-permute-start | bytes 786440 | tf_op jit(solution)/shard_map/ppermute | solution.py:35
  71.9 23.8 %collective-permute-start.15 = (bf16[2,256,256]{2,1,0:T(8,128)(2,1)}, bf16[2,256,256]{2,1,0:T(8,128)(2,1)}, u32[]{:S(2)}, u32[]{:S(2)}) collective-permute-start(bf16[2,256,256]{2,1,0:T(8,128)(2,1)} %get-tuple-element.95), channel_id=1, source_target_pairs={{0,3},{1,2},{2,1},{3,0},{4,7},{5,6},{6,5},{7,4},{8,11},{9,10},{10,... | collective-permute-start | bytes 786440 | tf_op jit(solution)/shard_map/ppermute | solution.py:35
  100.2 18.1 %collective-permute-start.26 = (f32[96,256]{1,0:T(8,128)}, f32[96,256]{1,0:T(8,128)}, u32[]{:S(2)}, u32[]{:S(2)}) collective-permute-start(f32[96,256]{1,0:T(8,128)} %get-tuple-element.123), channel_id=1, source_target_pairs={{0,4},{4,0},{8,12},{12,8},{16,20},{20,16},{24,28},{28,24},{1,5},{5... | collective-permute-start | bytes 294920 | tf_op jit(solution)/shard_map/ppermute | solution.py:35
  105.1 13.2 %collective-permute-start.25 = (bf16[4,128,1024]{2,1,0:T(8,128)(2,1)}, bf16[4,128,1024]{2,1,0:T(8,128)(2,1)}, u32[]{:S(2)}, u32[]{:S(2)}) collective-permute-start(bf16[4,128,1024]{2,1,0:T(8,128)(2,1)} %get-tuple-element.121), channel_id=1, source_target_pairs={{0,4},{4,0},{8,12},{12,8},{16,20},{20,16},{24,28},{28,24},{1,5},{5... | collective-permute-start | bytes 3145736 | tf_op jit(solution)/shard_map/ppermute | solution.py:35
  116.4 18.4 %collective-permute-start.34 = (bf16[4,128,512]{2,1,0:T(8,128)(2,1)}, bf16[4,128,512]{2,1,0:T(8,128)(2,1)}, u32[]{:S(2)}, u32[]{:S(2)}) collective-permute-start(bf16[4,128,512]{2,1,0:T(8,128)(2,1)} %get-tuple-element.134), channel_id=1, source_target_pairs={{0,4},{4,0},{8,12},{12,8},{16,20},{20,16},{24,28},{28,24},{1,5},{5... | collective-permute-start | bytes 1572872 | tf_op jit(solution)/shard_map/ppermute | solution.py:35
  116.7 15.6 %collective-permute-start.23 = (bf16[2,256,256]{2,1,0:T(8,128)(2,1)}, bf16[2,256,256]{2,1,0:T(8,128)(2,1)}, u32[]{:S(2)}, u32[]{:S(2)}) collective-permute-start(bf16[2,256,256]{2,1,0:T(8,128)(2,1)} %get-tuple-element.114), channel_id=1, source_target_pairs={{0,1},{1,0},{2,3},{3,2},{4,5},{5,4},{6,7},{7,6},{8,9},{9,8},{10,11... | collective-permute-start | bytes 786440 | tf_op jit(solution)/shard_map/ppermute | solution.py:35
  126.9 13.7 %collective-permute-start.30 = (bf16[160,1024]{1,0:T(8,128)(2,1)}, bf16[160,1024]{1,0:T(8,128)(2,1)}, u32[]{:S(2)}, u32[]{:S(2)}) collective-permute-start(bf16[160,1024]{1,0:T(8,128)(2,1)} %get-tuple-element.124), channel_id=1, source_target_pairs={{0,8},{4,12},{8,0},{12,4},{16,24},{20,28},{24,16},{28,20},{1,9},{5... | collective-permute-start | bytes 983048 | tf_op jit(solution)/shard_map/ppermute | solution.py:35
  128.4 15.7 %collective-permute-start.31 = (bf16[160,1024]{1,0:T(8,128)(2,1)}, bf16[160,1024]{1,0:T(8,128)(2,1)}, u32[]{:S(2)}, u32[]{:S(2)}) collective-permute-start(bf16[160,1024]{1,0:T(8,128)(2,1)} %get-tuple-element.125), channel_id=1, source_target_pairs={{0,16},{4,20},{8,24},{12,28},{16,0},{20,4},{24,8},{28,12},{1,17},{... | collective-permute-start | bytes 983048 | tf_op jit(solution)/shard_map/ppermute | solution.py:35
  130.0 16.6 %collective-permute-start.32 = (bf16[160,1024]{1,0:T(8,128)(2,1)}, bf16[160,1024]{1,0:T(8,128)(2,1)}, u32[]{:S(2)}, u32[]{:S(2)}) collective-permute-start(bf16[160,1024]{1,0:T(8,128)(2,1)} %get-tuple-element.126), channel_id=1, source_target_pairs={{0,24},{4,28},{8,16},{12,20},{16,8},{20,12},{24,0},{28,4},{1,25},{... | collective-permute-start | bytes 983048 | tf_op jit(solution)/shard_map/ppermute | solution.py:35
  134.7 22.2 %collective-permute-start.22 = (bf16[2,256,256]{2,1,0:T(8,128)(2,1)}, bf16[2,256,256]{2,1,0:T(8,128)(2,1)}, u32[]{:S(2)}, u32[]{:S(2)}) collective-permute-start(bf16[2,256,256]{2,1,0:T(8,128)(2,1)} %get-tuple-element.112), channel_id=1, source_target_pairs={{0,1},{1,0},{2,3},{3,2},{4,5},{5,4},{6,7},{7,6},{8,9},{9,8},{10,11... | collective-permute-start | bytes 786440 | tf_op jit(solution)/shard_map/ppermute | solution.py:35
  135.4 21.6 %collective-permute-start.24 = (bf16[2,256,256]{2,1,0:T(8,128)(2,1)}, bf16[2,256,256]{2,1,0:T(8,128)(2,1)}, u32[]{:S(2)}, u32[]{:S(2)}) collective-permute-start(bf16[2,256,256]{2,1,0:T(8,128)(2,1)} %add_convert_fusion), channel_id=1, source_target_pairs={{0,2},{1,3},{2,0},{3,1},{4,6},{5,7},{6,4},{7,5},{8,10},{9,11},{10,... | collective-permute-start | bytes 786440 | tf_op jit(solution)/shard_map/ppermute | solution.py:35
  140.6 11.0 %collective-permute-start.37 = (bf16[192,512]{1,0:T(8,128)(2,1)}, bf16[192,512]{1,0:T(8,128)(2,1)}, u32[]{:S(2)}, u32[]{:S(2)}) collective-permute-start(bf16[192,512]{1,0:T(8,128)(2,1)} %get-tuple-element.140), channel_id=1, source_target_pairs={{0,8},{4,12},{8,0},{12,4},{16,24},{20,28},{24,16},{28,20},{1,9},{5... | collective-permute-start | bytes 589832 | tf_op jit(solution)/shard_map/ppermute | solution.py:35
  144.1 10.1 %collective-permute-start.38 = (bf16[192,512]{1,0:T(8,128)(2,1)}, bf16[192,512]{1,0:T(8,128)(2,1)}, u32[]{:S(2)}, u32[]{:S(2)}) collective-permute-start(bf16[192,512]{1,0:T(8,128)(2,1)} %get-tuple-element.141), channel_id=1, source_target_pairs={{0,16},{4,20},{8,24},{12,28},{16,0},{20,4},{24,8},{28,12},{1,17},{... | collective-permute-start | bytes 589832 | tf_op jit(solution)/shard_map/ppermute | solution.py:35
  (30 other events, 150.6 us)
